TPU v7x, 32 devices: a whole 2x2x4 slice. The times are simulated.
32 devices in a mesh: dp: 8 (over z, x), mp: 4 (over y, core).
Axes of the slice: x: 2, y: 2, z: 4, core: 2. Of those that a mesh axis runs over, the one named last changes fastest.
Arguments:
- block_input: bfloat16 [32768, 768], P('dp'), may hold values from -6 to 6
- cotangent: bfloat16 [32768, 768], P(('dp', 'mp')), may hold values from -6 to 6
- lengths: int32 [64, 4], P('dp'), may hold values from 1 to 256, 512 in all within a row
- partner: int32 [256], P('dp'), may hold values from 0 to 255, as said below
- qkv_weight: float32 [3, 768, 768], P(None, 'dp', 'mp')
- out_weight: float32 [768, 768], P('mp', 'dp')
- up_weight: float32 [768, 3072], P('dp', 'mp')
- down_weight: float32 [3072, 768], P('mp', 'dp')
- qkv_first: float32 [3, 768, 768], P(None, 'dp', 'mp'), may hold values from -512 to 512
- out_first: float32 [768, 768], P('mp', 'dp'), may hold values from -112 to 112
- up_first: float32 [768, 3072], P('dp', 'mp'), may hold values from -224 to 224
- down_first: float32 [3072, 768], P('mp', 'dp'), may hold values from -384 to 384
- qkv_second: float32 [3, 768, 768], P(None, 'dp', 'mp'), as said below
- out_second: float32 [768, 768], P('mp', 'dp'), as said below
- up_second: float32 [768, 3072], P('dp', 'mp'), as said below
- down_second: float32 [3072, 768], P('mp', 'dp'), as said below
- vectors: float32 [9216], replicated, as said below
- vector_first: float32 [9216], replicated, may hold values from -1024 to 1024
- vector_second: float32 [9216], replicated, may hold values from 32768 to 131072
Outputs:
- block_output: bfloat16 [32768, 768], P(('dp', 'mp'))
- input_grad: float32 [32768, 768], P(('dp', 'mp'))
- qkv_grad: float32 [3, 768, 768], P(None, 'dp', 'mp')
- out_grad: float32 [768, 768], P('mp', 'dp')
- up_grad: float32 [768, 3072], P('dp', 'mp')
- down_grad: float32 [3072, 768], P('mp', 'dp')
- qkv_second_new: float32 [3, 768, 768], P(None, 'dp', 'mp')
- out_second_new: float32 [768, 768], P('mp', 'dp')
- up_second_new: float32 [768, 3072], P('dp', 'mp')
- down_second_new: float32 [3072, 768], P('mp', 'dp')
- qkv_new: float32 [3, 768, 768], P(None, 'dp', 'mp')
- out_new: float32 [768, 768], P('mp', 'dp')
- up_new: float32 [768, 3072], P('dp', 'mp')
- down_new: float32 [3072, 768], P('mp', 'dp')
- qkv_copy: bfloat16 [3, 768, 768], P(None, 'dp', 'mp')
- out_copy: bfloat16 [768, 768], P('mp', 'dp')
- up_copy: bfloat16 [768, 3072], P('dp', 'mp')
- down_copy: bfloat16 [3072, 768], P('mp', 'dp')
- vector_grad: float32 [9216], replicated
- vector_second_new: float32 [9216], replicated
- vector_new: float32 [9216], replicated
- norms: float32 [6, 2], replicated
Inputs may be any that keep to these rules, and one draw needn't show every extreme that they name: partner[partner[a]] = a and partner[a] != a for every passage a. `qkv_second`: entries are positive. `out_second`: entries are positive. `up_second`: entries are positive. `down_second`: entries are positive. `vectors`: gains g1 and g2 are positive.
All inputs are finite; a program needn't handle non-finite values.
Results may differ from a plain program's by a relative error of at most 0.025.
The roundings to bfloat16 on the way count: a program that leaves them out, or rounds other values in their place, can miss the bound.
Values may be sent and summed in bfloat16 or wider, within the bound.
No kernel may reach another device: no remote copies, remote signals or barrier semaphores. Data moves between devices by JAX's collectives and lax.ppermute only.
A program may use at most 192 MiB of HBM per device.

v0:
```python
from functools import partial
import math

import jax
import jax.numpy as jnp
from jax import lax
from jax.sharding import PartitionSpec as P

D = 768
HEADS = 12
HD = 64
FF = 3072
L = 512
PASS = 4
STEP = 10
ROWS_DEV = 8


masked_value = -1e30
grid_weight = 4.0
norm_eps = 1e-12
beta_decay = 0.5
adam_eps = 1e-06
norm_guard = 1e-06
weight_decay = 0.01
rate_matrix = 1.0
rate_vector = 0.2


def merged(part, axis, combine):
    gathered = jax.tree.map(lambda a: lax.all_gather(a, axis), part)

    def take(source):
        return jax.tree.map(lambda a: lax.dynamic_index_in_dim(a, source, 0, False), gathered)

    return lax.fori_loop(
        1, lax.axis_size(axis), lambda source, state: combine(state, take(source)), take(0)
    )


def layer_norm(value, gain, shift):
    center = jnp.mean(value, axis=-1, keepdims=True)
    offsets = value - center
    spread = jnp.mean(offsets * offsets, axis=-1, keepdims=True)
    return offsets * lax.rsqrt(spread + norm_eps) * gain + shift


def passage_ids(lengths):
    starts = jnp.cumsum(lengths, axis=1) - lengths
    positions = jnp.arange(L, dtype=jnp.int32)
    return jnp.sum((positions[None, :, None] >= starts[:, None, :]).astype(jnp.int32), axis=2) - 1


def row_scores(queries, keys, passage):
    scores = jnp.einsum("qhd,khd->hqk", queries, keys, preferred_element_type=jnp.float32) * HD ** (
        -0.5
    )
    same_passage = passage[:, None] == passage[None, :]
    return jnp.where(same_passage[None], scores, masked_value)


def attend_row(pieces):
    queries, keys, values, passage = pieces
    scores = row_scores(queries, keys, passage)
    highest = jnp.max(scores, axis=-1, keepdims=True)
    weights = jnp.exp(scores - highest)
    totals = jnp.sum(weights, axis=-1, keepdims=True)
    weights_low = (weights / totals).astype(jnp.bfloat16)
    context = jnp.einsum("hqk,khd->qhd", weights_low, values, preferred_element_type=jnp.float32)
    return (context.astype(jnp.bfloat16), (highest + jnp.log(totals))[..., 0])


def attend_back(pieces):
    queries, keys, values, passage, log_totals, context_grad = pieces
    scores = row_scores(queries, keys, passage)
    weights = jnp.exp(scores - log_totals[..., None])
    weight_grad = jnp.einsum(
        "qhd,khd->hqk", context_grad, values, preferred_element_type=jnp.float32
    )
    score_grad = (
        weights * (weight_grad - jnp.sum(weight_grad * weights, axis=-1, keepdims=True))
    ).astype(jnp.bfloat16)
    query_grad = jnp.einsum(
        "hqk,khd->qhd", score_grad, keys, preferred_element_type=jnp.float32
    ) * HD ** (-0.5)
    key_grad = jnp.einsum(
        "hqk,qhd->khd", score_grad, queries, preferred_element_type=jnp.float32
    ) * HD ** (-0.5)
    value_grad = jnp.einsum(
        "hqk,qhd->khd",
        weights.astype(jnp.bfloat16),
        context_grad,
        preferred_element_type=jnp.float32,
    )
    return (
        query_grad.astype(jnp.bfloat16),
        key_grad.astype(jnp.bfloat16),
        value_grad.astype(jnp.bfloat16),
    )


def combine_rows(earlier, later):
    highest = jnp.maximum(earlier[0], later[0])
    return (
        highest,
        earlier[1] * jnp.exp(earlier[0] - highest) + later[1] * jnp.exp(later[0] - highest),
    )


def adapt(grad, earlier, second):
    moment = beta_decay * earlier + (1.0 - beta_decay) * grad
    second_new = beta_decay * second + (1.0 - beta_decay) * grad * grad
    ratio = (
        moment
        / (1.0 - beta_decay**STEP)
        / (jnp.sqrt(second_new / (1.0 - beta_decay**STEP)) + adam_eps)
    )
    return (second_new, ratio)


def shards(
    block_input,
    cotangent,
    lengths,
    partner,
    qkv_weight,
    out_weight,
    up_weight,
    down_weight,
    qkv_first,
    out_first,
    up_first,
    down_first,
    qkv_second,
    out_second,
    up_second,
    down_second,
    vectors,
    vector_first,
    vector_second,
):
    mp_size = lax.axis_size("mp")
    dp_size = lax.axis_size("dp")
    mp_index = lax.axis_index("mp")
    dp_index = lax.axis_index("dp")
    group_tokens = block_input.shape[0]
    local_tokens = cotangent.shape[0]
    local_rows = local_tokens // L
    heads_here = HEADS // mp_size
    width_here = D // mp_size
    units_here = FF // mp_size
    shard_rows = qkv_weight.shape[1]
    qkv_low, out_low, up_low, down_low = (
        lax.all_gather(qkv_weight.astype(jnp.bfloat16), "dp", axis=1, tiled=True),
        lax.all_gather(out_weight.astype(jnp.bfloat16), "dp", axis=1, tiled=True),
        lax.all_gather(up_weight.astype(jnp.bfloat16), "dp", axis=0, tiled=True),
        lax.all_gather(down_weight.astype(jnp.bfloat16), "dp", axis=1, tiled=True),
    )
    offset_tail = 2 * D + FF
    bias_out = vectors[offset_tail : offset_tail + D]
    bias_down = vectors[offset_tail + D : offset_tail + 2 * D]
    gain_first = vectors[offset_tail + 2 * D : offset_tail + 3 * D]
    shift_first = vectors[offset_tail + 3 * D : offset_tail + 4 * D]
    gain_second = vectors[offset_tail + 4 * D : offset_tail + 5 * D]
    shift_second = vectors[offset_tail + 5 * D : offset_tail + 6 * D]
    local_lengths = lax.dynamic_slice_in_dim(lengths, mp_index * local_rows, local_rows, 0)
    local_input_low = lax.dynamic_slice_in_dim(
        block_input, mp_index * local_tokens, local_tokens, 0
    )
    local_input = local_input_low.astype(jnp.float32)
    qkv_use, out_use, up_use, down_use = (qkv_low, out_low, up_low, down_low)
    bias_query = lax.dynamic_slice_in_dim(vectors, mp_index * width_here, width_here)
    bias_value = lax.dynamic_slice_in_dim(vectors, D + mp_index * width_here, width_here)
    bias_up = lax.dynamic_slice_in_dim(vectors, 2 * D + mp_index * units_here, units_here)
    passage_rows = passage_ids(lengths)
    row_shape = (ROWS_DEV, L, heads_here, HD)
    projected = jnp.einsum("td,cdh->cth", block_input, qkv_use, preferred_element_type=jnp.float32)
    queries = (projected[0] + bias_query).astype(jnp.bfloat16)
    keys_low = projected[1].astype(jnp.bfloat16)
    values_low = (projected[2] + bias_value).astype(jnp.bfloat16)
    context_rows, log_totals = lax.map(
        attend_row,
        (
            queries.reshape(row_shape),
            keys_low.reshape(row_shape),
            values_low.reshape(row_shape),
            passage_rows,
        ),
    )
    context = context_rows.reshape(group_tokens, width_here)
    attended = (
        lax.psum_scatter(
            jnp.dot(context, out_use, preferred_element_type=jnp.float32),
            "mp",
            scatter_dimension=0,
            tiled=True,
        )
        + bias_out
    )
    first_sum = local_input + attended
    normed = layer_norm(first_sum, gain_first, shift_first)
    whole_normed = lax.all_gather(normed.astype(jnp.bfloat16), "mp", axis=0, tiled=True)
    hidden = jnp.dot(whole_normed, up_use, preferred_element_type=jnp.float32) + bias_up
    activated = jax.nn.gelu(hidden, approximate=False).astype(jnp.bfloat16)
    branch = (
        lax.psum_scatter(
            jnp.dot(activated, down_use, preferred_element_type=jnp.float32),
            "mp",
            scatter_dimension=0,
            tiled=True,
        )
        + bias_down
    )
    second_sum = normed + branch
    output = layer_norm(second_sum, gain_second, shift_second)
    block_output = output.astype(jnp.bfloat16)
    starts = jnp.cumsum(local_lengths, axis=1) - local_lengths
    marked = jnp.arange(L, dtype=jnp.int32)[None, :, None] == starts[:, None, :]
    picked = jnp.einsum(
        "rtp,rtd->rpd",
        marked.astype(jnp.bfloat16),
        block_output.reshape(local_rows, L, D),
        preferred_element_type=jnp.float32,
    )
    per_device = local_rows * PASS
    local_cls = picked.astype(jnp.bfloat16).reshape(per_device, D)
    every_cls = lax.all_gather(local_cls, ("dp", "mp"), axis=0, tiled=True)
    blocks = every_cls.reshape(dp_size, mp_size, per_device, D)
    row_cls = lax.dynamic_index_in_dim(blocks, dp_index, 0, keepdims=False).reshape(
        mp_size * per_device, D
    )
    column_cls = lax.dynamic_index_in_dim(blocks, mp_index, 1, keepdims=False).reshape(
        dp_size * per_device, D
    )
    scale_grid = 2.0 / math.sqrt(D)
    scores = (
        jnp.einsum("ad,bd->ab", row_cls, column_cls, preferred_element_type=jnp.float32)
        * scale_grid
    )
    row_global = dp_index * (mp_size * per_device) + jnp.arange(
        mp_size * per_device, dtype=jnp.int32
    )
    column_local = jnp.arange(dp_size * per_device, dtype=jnp.int32)
    column_global = (
        column_local // per_device * mp_size + mp_index
    ) * per_device + column_local % per_device
    is_self = row_global[:, None] == column_global[None, :]
    is_pair = partner[:, None] == column_global[None, :]
    masked = jnp.where(is_self, masked_value, scores)
    highest = jnp.max(masked, axis=1)
    totals = jnp.sum(jnp.exp(masked - highest[:, None]), axis=1)
    highest_all, totals_all = merged((highest, totals), "mp", combine_rows)
    log_grid = highest_all + jnp.log(totals_all)
    grid_grad = (
        grid_weight * (jnp.exp(masked - log_grid[:, None]) - is_pair.astype(jnp.float32))
    ).astype(jnp.bfloat16)
    row_grad = jnp.dot(grid_grad, column_cls, preferred_element_type=jnp.float32) * scale_grid
    column_grad = (
        jnp.einsum("ab,ad->bd", grid_grad, row_cls, preferred_element_type=jnp.float32) * scale_grid
    )
    dp_pick = (jnp.arange(dp_size, dtype=jnp.int32) == dp_index).astype(jnp.float32)
    mp_pick = (jnp.arange(mp_size, dtype=jnp.int32) == mp_index).astype(jnp.float32)
    spread = dp_pick[:, None, None, None] * row_grad.reshape(1, mp_size, per_device, D) + mp_pick[
        None, :, None, None
    ] * column_grad.reshape(dp_size, 1, per_device, D)
    cls_grad = lax.psum_scatter(
        spread.reshape(dp_size * mp_size * per_device, D),
        ("dp", "mp"),
        scatter_dimension=0,
        tiled=True,
    )
    added = jnp.einsum(
        "rtp,rpd->rtd",
        marked.astype(jnp.float32),
        cls_grad.reshape(local_rows, PASS, D),
        precision=lax.Precision.HIGHEST,
    )
    output_grad = cotangent.astype(jnp.float32) + added.reshape(local_tokens, D)
    _, second_back = jax.vjp(layer_norm, second_sum, gain_second, shift_second)
    sum_grad, gain_second_grad, shift_second_grad = second_back(output_grad)
    branch_grad = sum_grad.astype(jnp.bfloat16)
    down_bias_grad = jnp.sum(branch_grad.astype(jnp.float32), axis=0)
    whole_branch = lax.all_gather(branch_grad, "mp", axis=0, tiled=True)
    down_grad_local = jnp.einsum(
        "tu,td->ud", activated, whole_branch, preferred_element_type=jnp.float32
    )
    activated_grad = jnp.einsum(
        "td,ud->tu", whole_branch, down_use, preferred_element_type=jnp.float32
    )
    _, gelu_back = jax.vjp(partial(jax.nn.gelu, approximate=False), hidden)
    hidden_grad = gelu_back(activated_grad)[0].astype(jnp.bfloat16)
    up_bias_grad = jnp.sum(hidden_grad.astype(jnp.float32), axis=0)
    up_grad_local = jnp.einsum(
        "td,tu->du", whole_normed, hidden_grad, preferred_element_type=jnp.float32
    )
    normed_grad = sum_grad + lax.psum_scatter(
        jnp.einsum("tu,du->td", hidden_grad, up_use, preferred_element_type=jnp.float32),
        "mp",
        scatter_dimension=0,
        tiled=True,
    )
    _, first_back = jax.vjp(layer_norm, first_sum, gain_first, shift_first)
    first_grad, gain_first_grad, shift_first_grad = first_back(normed_grad)
    attended_grad = first_grad.astype(jnp.bfloat16)
    out_bias_grad = jnp.sum(attended_grad.astype(jnp.float32), axis=0)
    whole_attended = lax.all_gather(attended_grad, "mp", axis=0, tiled=True)
    out_grad_local = jnp.einsum(
        "th,td->hd", context, whole_attended, preferred_element_type=jnp.float32
    )
    context_grad = jnp.einsum(
        "td,hd->th", whole_attended, out_use, preferred_element_type=jnp.float32
    ).astype(jnp.bfloat16)
    query_grad, key_grad, value_grad = lax.map(
        attend_back,
        (
            queries.reshape(row_shape),
            keys_low.reshape(row_shape),
            values_low.reshape(row_shape),
            passage_rows,
            log_totals,
            context_grad.reshape(row_shape),
        ),
    )
    stacked = jnp.stack(
        [
            query_grad.reshape(group_tokens, width_here),
            key_grad.reshape(group_tokens, width_here),
            value_grad.reshape(group_tokens, width_here),
        ]
    )
    qkv_grad_local = jnp.einsum(
        "td,cth->cdh", block_input, stacked, preferred_element_type=jnp.float32
    )
    query_bias_grad = jnp.sum(stacked[0].astype(jnp.float32), axis=0)
    value_bias_grad = jnp.sum(stacked[2].astype(jnp.float32), axis=0)
    input_grad = first_grad + lax.psum_scatter(
        jnp.einsum("cth,cdh->td", stacked, qkv_use, preferred_element_type=jnp.float32),
        "mp",
        scatter_dimension=0,
        tiled=True,
    )
    head_query = lax.dynamic_update_slice_in_dim(
        jnp.zeros((D,), jnp.float32), query_bias_grad, mp_index * width_here, 0
    )
    head_value = lax.dynamic_update_slice_in_dim(
        jnp.zeros((D,), jnp.float32), value_bias_grad, mp_index * width_here, 0
    )
    head_up = lax.dynamic_update_slice_in_dim(
        jnp.zeros((FF,), jnp.float32), up_bias_grad, mp_index * units_here, 0
    )
    local_grads = (qkv_grad_local, out_grad_local, up_grad_local, down_grad_local)
    vector_local = jnp.concatenate(
        [
            head_query,
            head_value,
            head_up,
            out_bias_grad,
            down_bias_grad,
            gain_first_grad,
            shift_first_grad,
            gain_second_grad,
            shift_second_grad,
        ]
    )
    summed = lax.psum((local_grads[0], local_grads[1], local_grads[2], local_grads[3]), "dp")
    qkv_grad = lax.dynamic_slice_in_dim(summed[0], dp_index * shard_rows, shard_rows, 1)
    out_grad = lax.dynamic_slice_in_dim(summed[1], dp_index * shard_rows, shard_rows, 1)
    up_grad = lax.dynamic_slice_in_dim(summed[2], dp_index * shard_rows, shard_rows, 0)
    down_grad = lax.dynamic_slice_in_dim(summed[3], dp_index * shard_rows, shard_rows, 1)
    qkv_second_new, qkv_ratio = adapt(qkv_grad, qkv_first, qkv_second)
    out_second_new, out_ratio = adapt(out_grad, out_first, out_second)
    up_second_new, up_ratio = adapt(up_grad, up_first, up_second)
    down_second_new, down_ratio = adapt(down_grad, down_first, down_second)
    qkv_update = qkv_ratio + weight_decay * qkv_weight
    out_update = out_ratio + weight_decay * out_weight
    up_update = up_ratio + weight_decay * up_weight
    down_update = down_ratio + weight_decay * down_weight
    weight_squares = jnp.concatenate(
        [
            jnp.sum(qkv_weight * qkv_weight, axis=(1, 2)),
            jnp.sum(out_weight * out_weight)[None],
            jnp.sum(up_weight * up_weight)[None],
            jnp.sum(down_weight * down_weight)[None],
        ]
    )
    update_squares = jnp.concatenate(
        [
            jnp.sum(qkv_update * qkv_update, axis=(1, 2)),
            jnp.sum(out_update * out_update)[None],
            jnp.sum(up_update * up_update)[None],
            jnp.sum(down_update * down_update)[None],
        ]
    )
    vector_grad, weight_total, update_total = lax.psum(
        (vector_local, weight_squares, update_squares), ("dp", "mp")
    )
    weight_norms = jnp.sqrt(weight_total)
    update_norms = jnp.sqrt(update_total)
    trust = weight_norms / (update_norms + norm_guard)
    qkv_new = qkv_weight - rate_matrix * trust[0:3, None, None] * qkv_update
    out_new = out_weight - rate_matrix * trust[3] * out_update
    up_new = up_weight - rate_matrix * trust[4] * up_update
    down_new = down_weight - rate_matrix * trust[5] * down_update
    vector_second_new, vector_ratio = adapt(vector_grad, vector_first, vector_second)
    vector_new = vectors - rate_vector * vector_ratio
    norms = jnp.stack([weight_norms, update_norms], axis=1)
    return (
        block_output,
        input_grad,
        qkv_grad,
        out_grad,
        up_grad,
        down_grad,
        qkv_second_new,
        out_second_new,
        up_second_new,
        down_second_new,
        qkv_new,
        out_new,
        up_new,
        down_new,
        qkv_new.astype(jnp.bfloat16),
        out_new.astype(jnp.bfloat16),
        up_new.astype(jnp.bfloat16),
        down_new.astype(jnp.bfloat16),
        vector_grad,
        vector_second_new,
        vector_new,
        norms,
    )


def solution(mesh):
    in_specs = (
        P("dp", None),
        P(("dp", "mp"), None),
        P("dp", None),
        P("dp"),
        P(None, "dp", "mp"),
        P("mp", "dp"),
        P("dp", "mp"),
        P("mp", "dp"),
        P(None, "dp", "mp"),
        P("mp", "dp"),
        P("dp", "mp"),
        P("mp", "dp"),
        P(None, "dp", "mp"),
        P("mp", "dp"),
        P("dp", "mp"),
        P("mp", "dp"),
        P(),
        P(),
        P(),
    )
    out_specs = (
        P(("dp", "mp"), None),
        P(("dp", "mp"), None),
        P(None, "dp", "mp"),
        P("mp", "dp"),
        P("dp", "mp"),
        P("mp", "dp"),
        P(None, "dp", "mp"),
        P("mp", "dp"),
        P("dp", "mp"),
        P("mp", "dp"),
        P(None, "dp", "mp"),
        P("mp", "dp"),
        P("dp", "mp"),
        P("mp", "dp"),
        P(None, "dp", "mp"),
        P("mp", "dp"),
        P("dp", "mp"),
        P("mp", "dp"),
        P(),
        P(),
        P(),
        P(),
    )
    return jax.shard_map(shards, mesh=mesh, in_specs=in_specs, out_specs=out_specs, check_vma=False)
```

profile of v0, /device:TPU:0, one launch (start us, length us, event | category | flops | bytes accessed | tf_op | source)
XLA Modules:
  0.0 1356.9 jit_solution(7338317496588622699)
XLA Ops:
  10.0 38.8 %all_gather.36 = bf16[3,768,192]{2,0,1:T(4,128)(2,1)S(1)} all-gather(bf16[3,96,192]{2,0,1:T(4,128)(2,1)S(1)} %copy.147), channel_id=1, replica_groups=mesh['dp'=8,'mp'=4] {'dp'}, dimensions={1}, use_global_device_ids=true | all-gather | bytes 995328 | tf_op jit(solution)/shard_map/all_gather | solution.py:154
  81.4 43.0 %while.43 = (s32[]{:T(128)}, bf16[8,512,3,64]{1,3,2,0:T(8,128)(2,1)S(1)}, f32[8,3,512]{2,1,0:T(4,128)}, bf16[8,512,3,64]{1,3,2,0:T(8,128)(2,1)}, s32[8,512]{1,0:...) while((s32[]{:T(128)}, ...), condition=%wide.region_5.6_spmd, body=%wide.region_2.5_spmd.sunk | while | flops 211122688 | bytes 11336281 | solution.py:181
  126.1 31.2 %all_gather.37 = bf16[192,768]{0,1:T(8,128)(2,1)S(1)} all-gather(bf16[192,96]{0,1:T(8,128)(2,1)S(1)} %copy.153), channel_id=1, replica_groups=mesh['dp'=8,'mp'=4] {'dp'}, dimensions={1}, use_global_device_ids=true | all-gather | bytes 331776 | tf_op jit(solution)/shard_map/all_gather | solution.py:155
  166.9 95.8 %reduce-scatter.6.cloned.1.call-done = f32[1024,768]{1,0:T(8,128)} async-done(((f32[4096,768]{1,0:T(8,128)}), f32[1024,768]{1,0:T(8,128)}) %reduce-scatter.6.cloned.1.call-update) | async-done | bytes 3145744 | tf_op jit(solution)/shard_map/reduce_scatter | solution.py:192
  269.9 44.8 %all-gather.8.cloned.1.call-done = bf16[4096,768]{1,0:T(8,128)(2,1)} async-done(((bf16[1024,768]{1,0:T(8,128)(2,1)}), bf16[4096,768]{1,0:T(8,128)(2,1)}) %all-gather.8.cloned.1.call-update) | async-done | bytes 6291472 | tf_op jit(solution)/shard_map/all_gather | solution.py:202
  314.8 35.0 %multiply_convert_fusion.1 = (bf16[4096,768]{1,0:T(8,128)(2,1)}, f32[4096,768]{1,0:T(8,128)}, f32[4096,768]{1,0:T(8,128)}) fusion(f32[768]{0:T(1024)S(1)} %get-tuple-element.567, bf16[4096,768]{1,0:T(8,128)(2,1)} %all-gather.8.cloned.1.call-done, bf16[768,768]{1,0:T(8,128)(2,1)} %all-gather.10.cloned.1.call-done), kind=kOutput, calls=%fused_computation.72 | convolution fusion | flops 5039456256 | bytes 38931456 | tf_op jit(solution)/shard_map/dot_general | solution.py:203
  349.8 9.2 all-gather.12.cloned.1.call-done
  358.9 10.3 fusion.142
  373.3 93.4 %reduce-scatter.8.cloned.1.call-done = f32[1024,768]{1,0:T(8,128)} async-done(((f32[4096,768]{1,0:T(8,128)}), f32[1024,768]{1,0:T(8,128)}) %reduce-scatter.8.cloned.1.call-update) | async-done | bytes 3145744 | tf_op jit(solution)/shard_map/reduce_scatter | solution.py:206
  472.8 41.6 %all_gather.41 = bf16[256,768]{1,0:T(8,128)(2,1)S(1)} all-gather(bf16[8,768]{1,0:T(8,128)(2,1)S(1)} %reshape.307), channel_id=1, replica_groups=mesh['dp'=8,'mp'=4] {'dp','mp'}, dimensions={0}, use_global_device_ids=true | all-gather | bytes 405504 | tf_op jit(solution)/shard_map/all_gather | solution.py:227
  537.4 93.0 %reduce-scatter.10.cloned.1.call-done = f32[8,768]{1,0:T(8,128)} async-done(((f32[256,768]{1,0:T(8,128)}), f32[8,768]{1,0:T(8,128)}) %reduce-scatter.10.cloned.1.call-update) | async-done | bytes 24592 | tf_op jit(solution)/shard_map/reduce_scatter | solution.py:266
  643.3 45.5 %all-gather.14.cloned.1.call-done = bf16[4096,768]{1,0:T(8,128)(2,1)} async-done(((bf16[1024,768]{1,0:T(8,128)(2,1)}), bf16[4096,768]{1,0:T(8,128)(2,1)}) %all-gather.14.cloned.1.call-update) | async-done | bytes 6291472 | tf_op jit(solution)/shard_map/all_gather | solution.py:283
  688.8 19.2 %convert_reduce_fusion = (f32[768]{0:T(1024)}, bf16[4096,768]{1,0:T(8,128)(2,1)}) fusion(f32[4096,768]{1,0:T(8,128)} %get-tuple-element.549, f32[4096,768]{1,0:T(8,128)} %get-tuple-element.580, f32[768]{0:T(1024)S(1)} %copy-done.46, bf16[4096,768]{1,0:T(8,128)(2,1)} %all-gather.14.cloned.1.call-done, bf16[768,768]{0,1:T(8,128)(2,1)} %all-gather.12.cloned.1.call-done), kind=kOutput, calls=%fused_computation.70 | convolution fusion | flops 4885314560 | bytes 38934528 | tf_op jit(solution)/shard_map/td,ud->tu/dot_general | solution.py:287
  708.0 10.6 fusion.143
  718.7 99.2 %reduce-scatter.12.cloned.1.call-done = f32[1024,768]{1,0:T(8,128)} async-done(((f32[4096,768]{1,0:T(8,128)}), f32[1024,768]{1,0:T(8,128)}) %reduce-scatter.12.cloned.1.call-update) | async-done | bytes 3145744 | tf_op jit(solution)/shard_map/reduce_scatter | solution.py:296
  827.5 10.3 fusion.146
  837.8 10.3 fusion.145
  848.1 25.7 %all-gather.16.cloned.1.call-done = bf16[4096,768]{1,0:T(8,128)(2,1)} async-done(((bf16[1024,768]{1,0:T(8,128)(2,1)}), bf16[4096,768]{1,0:T(8,128)(2,1)}) %all-gather.16.cloned.1.call-update) | async-done | bytes 6291472 | tf_op jit(solution)/shard_map/all_gather | solution.py:306
  882.8 89.9 %while.45 = (s32[]{:T(128)}, bf16[8,512,3,64]{1,3,2,0:T(8,128)(2,1)S(1)}, bf16[8,512,3,64]{1,3,2,0:T(8,128)(2,1)}, bf16[8,512,3,64]{1,3,2,0:T(8,128)(2,1)S(1)}, ...) while((s32[]{:T(128)}, ...), condition=%wide.region_25.26_spmd, body=%wide.region_23.25_spmd.sunk | while | flops 511146496 | bytes 26125428 | solution.py:313
  997.1 9.8 fusion.68
  1009.2 10.5 convolution_bitcast_fusion
  1040.3 204.0 %all-reduce.7.cloned.1.call-done = (f32[3,768,192]{1,2,0:T(8,128)}, f32[192,768]{1,0:T(8,128)}, f32[768,768]{1,0:T(8,128)}, f32[768,768]{0,1:T(8,128)}) async-done(((f32[3,768,192]{1,2,0:T(8,128)}, f32[192,768]{1,0:T(8,128)}, f32[768,768]{1,0:T(8,128)}, f32[768,768]{0,1:T(8,128)}), (f32[3,768,192]{1,2,0:T(8,128)}, f32[192,768]{1,0:T(8,128)}, f32[768,768]{1,0:T(8,128)}, ...) | async-done | bytes 7077904 | tf_op jit(solution)/shard_map/psum | solution.py:365
  1258.5 40.2 %all-reduce.2 = (f32[6]{0:T(128)S(1)}, f32[6]{0:T(128)S(1)}, f32[9216]{0:T(1024)}) all-reduce(f32[6]{0:T(128)S(1)} %pad_maximum_fusion.2, f32[6]{0:T(128)S(1)} %pad_maximum_fusion.1, f32[9216]{0:T(1024)S(1)} %copy-done.42), channel_id=1, replica_groups=mesh['dp'=8,'mp'=4] {'dp','mp'}, use_global_device_ids=true, to_apply=%region_40.41 | all-reduce | flops 9228 | bytes 73824 | tf_op jit(solution)/shard_map/psum | solution.py:394
  1319.5 26.0 %reduce-scatter.14.cloned.1.call-done = f32[1024,768]{1,0:T(8,128)} async-done(((f32[4096,768]{1,0:T(8,128)}), f32[1024,768]{1,0:T(8,128)}) %reduce-scatter.14.cloned.1.call-update) | async-done | bytes 3145744 | tf_op jit(solution)/shard_map/reduce_scatter | solution.py:336
  (389 shorter events, 338.3 us)
Async XLA Ops:
  8.0 254.7 %reduce-scatter.6.cloned.1.call-start = ((), (), s32[]{:S(2)}) async-start(), calls=%async_computation.5 | async-start | bytes 15728640 | tf_op jit(solution)/shard_map/reduce_scatter | solution.py:192
  164.5 105.4 %all-gather.10.cloned.1.call-start = ((), (), s32[]{:S(2)}) async-start(), calls=%async_computation.7 | async-start | bytes 1327104 | tf_op jit(solution)/shard_map/all_gather | solution.py:156
  166.8 148.0 %all-gather.8.cloned.1.call-start = ((), (), s32[]{:S(2)}) async-start(), calls=%async_computation.6 | async-start | bytes 7864320 | tf_op jit(solution)/shard_map/all_gather | solution.py:202
  166.9 147.9 %copy-start.45 = (f32[768]{0:T(1024)}, f32[768]{0:T(1024)S(1)}, u32[]{:S(2)}) copy-start(f32[768]{0:T(1024)S(1)} %get-tuple-element.567) | copy-start | bytes 9220
  166.9 299.8 %copy-start.27 = (f32[768]{0:T(1024)}, f32[768]{0:T(1024)S(1)}, u32[]{:S(2)}) copy-start(f32[768]{0:T(1024)S(1)} %get-tuple-element.569) | copy-start | bytes 9220
  166.9 303.3 %copy-start.34 = (f32[768]{0:T(1024)}, f32[768]{0:T(1024)S(1)}, u32[]{:S(2)}) copy-start(f32[768]{0:T(1024)S(1)} %get-tuple-element.565) | copy-start | bytes 9220
  265.6 201.1 %copy-start.24 = (f32[1024]{0:T(1024)}, f32[1024]{0:T(1024)S(1)}, u32[]{:S(2)}) copy-start(f32[1024]{0:T(1024)S(1)} %broadcast_multiply_fusion.1) | copy-start | bytes 12292
  266.1 200.6 %copy-start.29 = (f32[1024]{0:T(1024)}, f32[1024]{0:T(1024)S(1)}, u32[]{:S(2)}) copy-start(f32[1024]{0:T(1024)S(1)} %fusion.110) | copy-start | bytes 12292
  268.4 90.5 %all-gather.12.cloned.1.call-start = ((), (), s32[]{:S(2)}) async-start(), calls=%async_computation.8 | async-start | bytes 1327104 | tf_op jit(solution)/shard_map/all_gather | solution.py:157
  269.9 196.9 %reduce-scatter.8.cloned.1.call-start = ((), (), s32[]{:S(2)}) async-start(), calls=%async_computation.9 | async-start | bytes 15728640 | tf_op jit(solution)/shard_map/reduce_scatter | solution.py:206
  369.2 261.2 %reduce-scatter.10.cloned.1.call-start = ((), (), s32[]{:S(2)}) async-start(), calls=%async_computation.10 | async-start | bytes 811008 | tf_op jit(solution)/shard_map/reduce_scatter | solution.py:266
  369.6 101.7 %copy-start.44 = (s32[2,4]{1,0:T(2,128)}, s32[2,4]{1,0:T(2,128)S(1)}, u32[]{:S(2)}) copy-start(s32[2,4]{1,0:T(2,128)S(1)} %copy.154) | copy-start | bytes 100
  537.4 151.4 %all-gather.14.cloned.1.call-start = ((), (), s32[]{:S(2)}) async-start(), calls=%async_computation.11 | async-start | bytes 7864320 | tf_op jit(solution)/shard_map/all_gather | solution.py:283
  643.2 174.6 %reduce-scatter.12.cloned.1.call-start = ((), (), s32[]{:S(2)}) async-start(), calls=%async_computation.12 | async-start | bytes 15728640 | tf_op jit(solution)/shard_map/reduce_scatter | solution.py:296
  718.6 99.3 %copy-start.28 = (f32[768]{0:T(1024)S(1)}, f32[768]{0:T(1024)}, u32[]{:S(2)}) copy-start(f32[768]{0:T(1024)} %copy-done.27) | copy-start | bytes 9220
  718.6 99.3 %copy-start.30 = (f32[1024]{0:T(1024)S(1)}, f32[1024]{0:T(1024)}, u32[]{:S(2)}) copy-start(f32[1024]{0:T(1024)} %copy-done.29) | copy-start | bytes 12292
  718.6 103.5 %copy-start.39 = (f32[1024]{0:T(1024)S(1)}, f32[1024]{0:T(1024)}, u32[]{:S(2)}) copy-start(f32[1024]{0:T(1024)} %copy-done.38) | copy-start | bytes 12292
  718.6 155.1 %all-gather.16.cloned.1.call-start = ((), (), s32[]{:S(2)}) async-start(), calls=%async_computation.13 | async-start | bytes 7864320 | tf_op jit(solution)/shard_map/all_gather | solution.py:306
  827.5 416.8 %all-reduce.7.cloned.1.call-start = ((), (), s32[]{:S(2)}) async-start(), calls=%async_computation.15 | async-start | bytes 14155776 | tf_op jit(solution)/shard_map/psum | solution.py:365
  1009.1 336.4 %reduce-scatter.14.cloned.1.call-start = ((), (), s32[]{:S(2)}) async-start(), calls=%async_computation.14 | async-start | bytes 15728640 | tf_op jit(solution)/shard_map/reduce_scatter | solution.py:336
  1019.7 224.6 %copy-start.21 = (f32[192,96]{1,0:T(8,128)S(1)}, f32[192,96]{1,0:T(8,128)}, u32[]{:S(2)}) copy-start(f32[192,96]{1,0:T(8,128)} %param.30) | copy-start | bytes 221188
  1026.9 225.0 %copy-start.16 = (f32[768,96]{0,1:T(8,128)S(1)}, f32[768,96]{0,1:T(8,128)}, u32[]{:S(2)}) copy-start(f32[768,96]{0,1:T(8,128)} %param.32) | copy-start | bytes 884740
  1026.9 225.0 %copy-start.22 = (f32[768,96]{0,1:T(8,128)S(1)}, f32[768,96]{0,1:T(8,128)}, u32[]{:S(2)}) copy-start(f32[768,96]{0,1:T(8,128)} %param.36) | copy-start | bytes 884740
  1026.9 225.0 %copy-start.23 = (f32[768,96]{0,1:T(8,128)S(1)}, f32[768,96]{0,1:T(8,128)}, u32[]{:S(2)}) copy-start(f32[768,96]{0,1:T(8,128)} %param.40) | copy-start | bytes 884740
  (40 other events, 695.7 us)
Sparse Core Ops, SparseCore 0:
  164.7 98.0 reduce-scatter.5
  537.5 92.8 reduce-scatter.9
  643.3 45.4 all-gather.13
  718.7 99.0 reduce-scatter.11
Sparse Core Ops, SparseCore 1:
  167.8 40.5 all-gather.9
  268.5 46.2 all-gather.7
  317.4 41.5 all-gather.11
  369.3 97.4 reduce-scatter.7
  827.5 46.2 all-gather.15
  1009.2 235.0 all-reduce.6
  1246.9 98.6 reduce-scatter.13
where the time goes:
time: 1360 us
  waiting for transfers between devices  737 us (54%)
  matrix products  243 us (18%)
  blocking collectives  158 us (12%)
  local copies, waits for them, and re-layouts  103 us (8%)
  other arithmetic  97.2 us (7%)
  between operations  16.8 us (1%)
    psum x1, waiting for transfers between devices, shards(): lax.psum((local_grads[0], local_grads[1], local_grads[2], local_grads[3])...  204 us
    reduce_scatter x1, waiting for transfers between devices, shards(): lax.psum_scatter(jnp.einsum('tu,du->td', hidden_grad, up_use, preferred_e...  99.2 us
    reduce_scatter x1, waiting for transfers between devices, shards(): lax.psum_scatter(jnp.dot(context, out_use, preferred_element_type=jnp.flo...  95.8 us
    reduce_scatter x1, waiting for transfers between devices, shards(): lax.psum_scatter(jnp.dot(activated, down_use, preferred_element_type=jnp....  93.4 us
    reduce_scatter x1, waiting for transfers between devices, shards(): lax.psum_scatter(spread.reshape(dp_size * mp_size * per_device, D), ('dp'...  93 us
    unnamed x134, local copies, waits for them, and re-layouts  53.4 us
    all_gather x1, waiting for transfers between devices, shards(): whole_branch = lax.all_gather(branch_grad, 'mp', axis=0, tiled=True)  45.5 us
    all_gather x1, waiting for transfers between devices, shards(): lax.all_gather(normed.astype(jnp.bfloat16), 'mp', axis=0, tiled=True)  44.8 us
  transfers between devices with their start and end apart: 11, of which 10 were waited for; matrix products, arithmetic and copies ran while one was open for 10% of the time, Pallas kernels for 0%

commit v1 on v0

v1 whole, which is shorter than its diff:
```python
from functools import partial
import math

import jax
import jax.numpy as jnp
from jax import lax
from jax.experimental import pallas as pl
from jax.experimental.pallas import tpu as pltpu
from jax.sharding import PartitionSpec as P

D = 768
HEADS = 12
HD = 64
FF = 3072
L = 512
PASS = 4
STEP = 10
ROWS_DEV = 8
MIB = 1 << 20
TAIL = 2 * D + FF


masked_value = -1e30
grid_weight = 4.0
norm_eps = 1e-12
beta_decay = 0.5
adam_eps = 1e-06
norm_guard = 1e-06
weight_decay = 0.01
rate_matrix = 1.0
rate_vector = 0.2


def passage_ids(lengths):
    starts = jnp.cumsum(lengths, axis=1) - lengths
    positions = jnp.arange(L, dtype=jnp.int32)
    return jnp.sum((positions[None, :, None] >= starts[:, None, :]).astype(jnp.int32), axis=2) - 1


def adapt(grad, earlier, second):
    moment = beta_decay * earlier + (1.0 - beta_decay) * grad
    second_new = beta_decay * second + (1.0 - beta_decay) * grad * grad
    ratio = (
        moment
        / (1.0 - beta_decay**STEP)
        / (jnp.sqrt(second_new / (1.0 - beta_decay**STEP)) + adam_eps)
    )
    return (second_new, ratio)


AXES = ("dp", "mp")
GRID = (8, 4)


def links(move):
    pairs = []
    for z in range(4):
        for x in range(2):
            for y in range(2):
                for c in range(2):
                    tz, tx, ty, tc = move(z, x, y, c)
                    pairs.append(
                        ((z * 2 + x) * 4 + y * 2 + c, (tz % 4 * 2 + tx) * 4 + ty * 2 + tc)
                    )
    return pairs


CORE = links(lambda z, x, y, c: (z, x, y, 1 - c))
OVER_X = links(lambda z, x, y, c: (z, 1 - x, y, c))
OVER_Y = links(lambda z, x, y, c: (z, x, 1 - y, c))
UP_Z = [links(lambda z, x, y, c, s=s: (z + s, x, y, c)) for s in range(4)]


def send(value, pairs):
    return lax.ppermute(value, AXES, pairs)


def on_grid():
    return (lax.axis_size("dp"), lax.axis_size("mp")) == GRID


def place():
    dp_index = lax.axis_index("dp")
    mp_index = lax.axis_index("mp")
    return jnp.stack([dp_index // 2, dp_index % 2, mp_index // 2, mp_index % 2])


ITEMS = (
    [(x, 0, z) for x in (0, 1) for z in (0, 1)]
    + [(0, y, z) for y in (0, 1) for z in (2, 3)]
    + [(x, 1, z) for x in (0, 1) for z in (0, 1)]
    + [(1, y, z) for y in (0, 1) for z in (2, 3)]
)


def settle_kernel(where, *refs):
    pieces, out, sems = refs[:8], refs[8], refs[9]
    z0, x0, y0, c0 = where[0], where[1], where[2], where[3]
    copies = []
    for core in range(2):
        for item, (x, y, z) in enumerate(ITEMS):
            source = pieces[core * 4 + item // 4].at[item % 4]
            block = (y0 + y) % 2 * 2 + (c0 + core) % 2
            row = (z0 + 4 - z) % 4 * 2 + (x0 + x) % 2
            copy = pltpu.make_async_copy(source, out.at[block, row], sems.at[core * 16 + item])
            copy.start()
            copies.append(copy)
    for copy in copies:
        copy.wait()


def gather(shard):
    rows, width = shard.shape
    if not on_grid():
        return lax.all_gather(shard, ("mp", "dp"), axis=0, tiled=True).reshape(
            lax.axis_size("mp"), -1, width
        )
    first = jnp.stack([shard, send(shard, UP_Z[1])])
    second = jnp.stack([send(shard, UP_Z[2]), send(shard, UP_Z[3])])
    first = jnp.concatenate([first, send(first, OVER_X)])
    second = jnp.concatenate([second, send(second, OVER_Y)])
    pieces = [first, second, send(first, OVER_Y), send(second, OVER_X)]
    pieces = pieces + [send(piece, CORE) for piece in pieces]
    whole = pl.pallas_call(
        settle_kernel,
        grid_spec=pltpu.PrefetchScalarGridSpec(
            num_scalar_prefetch=1,
            grid=(1,),
            in_specs=[pl.BlockSpec(memory_space=pl.ANY)] * 8,
            out_specs=pl.BlockSpec((4, 8, rows, width), lambda i, where: (0, 0, 0, 0)),
            scratch_shapes=[pltpu.SemaphoreType.DMA((32,))],
        ),
        out_shape=jax.ShapeDtypeStruct((4, 8, rows, width), shard.dtype),
        compiler_params=pltpu.CompilerParams(vmem_limit_bytes=24 * MIB),
        name="settle",
    )(place(), *pieces)
    return whole.reshape(4, 8 * rows, width)


def plus(left, right):
    return (left.astype(jnp.float32) + right.astype(jnp.float32)).astype(jnp.bfloat16)


def scatter_sum(items):
    if not on_grid():
        return lax.psum_scatter(
            items.reshape(-1, items.shape[-1]), ("mp", "dp"), scatter_dimension=0, tiled=True
        ).astype(jnp.float32)
    items = plus(items[0], send(items[1], CORE))
    first = plus(items[0, :, :2], send(items[1, :, :2], OVER_Y))
    second = plus(items[:, 0, 2:], send(items[:, 1, 2:], OVER_X))
    first = plus(first[0], send(first[1], OVER_X))
    second = plus(second[0], send(second[1], OVER_Y))
    parts = [first[0]]
    for step, part in ((1, first[1]), (2, second[0]), (3, second[1])):
        parts.append(send(part, UP_Z[step]))
    return sum(part.astype(jnp.float32) for part in parts)


def summand(mp_size, dp_size):
    rows = D // dp_size
    if not on_grid():

        def write_plain(out, value, where):
            out[0] = value

        return (mp_size, D, D), (1, D, D), lambda g, where: (g, 0, 0), write_plain, lambda g, where: g

    def write(out, value, where):
        z0, x0 = where[0], where[1]
        for index in range(dp_size):
            z, x = index // 2, index % 2
            out[0, 0, (x + x0) % 2, (z + 4 - z0) % 4] = value[index * rows : (index + 1) * rows]

    def block(g, where):
        return ((where[2] + g % 2) % 2) * 2 + (where[3] + g // 2) % 2

    return (
        (2, 2, 2, 4, rows, D),
        (1, 1, 2, 4, rows, D),
        lambda g, where: (g // 2, g % 2, 0, 0, 0, 0),
        write,
        block,
    )


def share(value):
    if not on_grid():
        dp_size, mp_size = lax.axis_size("dp"), lax.axis_size("mp")
        whole = lax.all_gather(value, AXES, axis=0, tiled=True)
        own = lax.axis_index("dp") * mp_size + lax.axis_index("mp")
        return jnp.roll(whole, -own * value.shape[0], axis=0)
    for pairs in (CORE, OVER_X, OVER_Y):
        value = jnp.concatenate([value, send(value, pairs)])
    return jnp.concatenate([value] + [send(value, UP_Z[s]) for s in (1, 2, 3)])


def total(value):
    if not on_grid():
        return lax.psum(value, AXES)
    for pairs in (CORE, OVER_X, OVER_Y):
        value = value + send(value, pairs)
    pair = value + send(value, UP_Z[2])
    return pair + send(pair, UP_Z[1])

LOW = jnp.bfloat16
WIDE = jnp.float32
B1, BO, B2, G1, C1, G2, C2 = 2 * D, TAIL, TAIL + D, TAIL + 2 * D, TAIL + 3 * D, TAIL + 4 * D, TAIL + 5 * D
VEC = 8 * D + FF


def dot(left, right, over=(1, 0)):
    return lax.dot_general(
        left, right, (((over[0],), (over[1],)), ((), ())), preferred_element_type=WIDE
    )


def call(kernel, name, grid, in_specs, out_specs, out_shape, scratch=(), limit=48, flops=0, args=()):
    return pl.pallas_call(
        kernel,
        grid_spec=pltpu.PrefetchScalarGridSpec(
            num_scalar_prefetch=1,
            grid=grid,
            in_specs=in_specs,
            out_specs=out_specs,
            scratch_shapes=list(scratch),
        ),
        out_shape=out_shape,
        compiler_params=pltpu.CompilerParams(vmem_limit_bytes=limit * MIB),
        cost_estimate=pl.CostEstimate(flops=flops, bytes_accessed=MIB, transcendentals=0),
        name=name,
    )(*args)


def whole(*shape):
    zeros = (0,) * len(shape)
    return pl.BlockSpec(shape, lambda *_: zeros)


def once(*shape):
    zeros = (0,) * len(shape)
    return pl.BlockSpec(shape, lambda *_: zeros, pipeline_mode=pl.Buffered(1))


def stepped(place, *shape):
    def index(step, *_):
        return tuple(step if i == place else 0 for i in range(len(shape)))

    return pl.BlockSpec(shape, index)


def array(dtype, *shape):
    return jax.ShapeDtypeStruct(shape, dtype)


def normalize(value):
    center = jnp.mean(value, axis=1, keepdims=True)
    offsets = value - center
    inverse = lax.rsqrt(jnp.mean(offsets * offsets, axis=1, keepdims=True) + norm_eps)
    return offsets * inverse, inverse


def norm_back(grad, unit, inverse, gain):
    scaled = grad * gain
    return inverse * (
        scaled
        - jnp.mean(scaled, axis=1, keepdims=True)
        - unit * jnp.mean(scaled * unit, axis=1, keepdims=True)
    )


def column_sum(value):
    return jnp.sum(value, axis=0, keepdims=True)


def add_to(first, ref, value):
    @pl.when(first)
    def _():
        ref[...] = jnp.zeros_like(ref)

    ref[...] += value


def attend_kernel(
    blocks, where, x_ref, w_ref, bias_ref, vec_ref, seg_ref,
    q_out, k_out, v_out, context_out, unit_out, inverse_out, low_out, sum_ref,
):
    heads = HEADS // blocks
    width = HD * heads
    x = x_ref[...]
    lanes = lax.broadcasted_iota(jnp.int32, (L, 2 * HD), 1)
    passage = jnp.broadcast_to(seg_ref[...], (L, 2 * HD)) + HD
    is_passage = (lanes >= HD) & (lanes < HD + PASS)
    q_mask = jnp.where(is_passage & (lanes != passage), masked_value, 0.0)
    k_mask = jnp.where(
        (lanes == passage) | ((lanes >= HD + PASS) & (lanes < HD + PASS + 3)), 1.0, 0.0
    ).astype(LOW)[:, HD:]
    sum_ref[...] = x.astype(WIDE) + vec_ref[:, BO : BO + D]

    def block(m, carry):
        projected = (dot(x, w_ref[m]) + bias_ref[m]).astype(LOW)
        parts = []
        for h in range(heads):
            at = width + h * HD
            query = projected[:, at : at + HD] * jnp.asarray(HD ** (-0.5), LOW)
            key = projected[:, at + width : at + width + HD]
            value = projected[:, at + 2 * width : at + 2 * width + HD]
            keys = jnp.concatenate([key, k_mask], axis=1)
            queries = jnp.concatenate([query, q_mask[:, HD:].astype(LOW)], axis=1)
            scores = dot(keys, queries, (1, 1))
            highest = jnp.max(scores, axis=0, keepdims=True)
            weights = jnp.exp(scores - highest)
            totals = jnp.sum(weights, axis=0, keepdims=True)
            mixed = dot(value.T, weights.astype(LOW)) * (1.0 / totals)
            left = -(highest + jnp.log(totals))
            high = left.astype(LOW).astype(WIDE)
            middle = (left - high).astype(LOW).astype(WIDE)
            lowest = left - high - middle
            rows = lax.broadcasted_iota(jnp.int32, (HD, L), 0)
            split = jnp.where(rows == PASS, high, 0.0)
            split = jnp.where(rows == PASS + 1, middle, split)
            split = jnp.where(rows == PASS + 2, lowest, split)
            turned = jnp.concatenate([mixed, split], axis=0).T
            parts.append(turned[:, :HD].astype(LOW))
            q_out[m * heads + h] = jnp.concatenate(
                [query, (q_mask + turned)[:, HD:].astype(LOW)], axis=1
            )
            k_out[m * heads + h] = keys
            v_out[m * heads + h] = value
        context = jnp.concatenate(parts, axis=1)
        context_out[m] = context
        sum_ref[...] += dot(context, w_ref[m, :, :width], (1, 1))
        return carry

    lax.fori_loop(0, blocks, block, 0)
    unit, inverse = normalize(sum_ref[...])
    unit_out[...] = unit
    inverse_out[...] = inverse
    low_out[...] = (unit * vec_ref[:, G1 : G1 + D] + vec_ref[:, C1 : C1 + D]).astype(LOW)


def attend(where, inputs, weights, bias, vectors, segments):
    tokens = inputs.shape[0]
    blocks = weights.shape[0]
    width = D // blocks
    return call(
        partial(attend_kernel, blocks),
        "attend",
        (tokens // L,),
        [
            stepped(0, L, D),
            once(blocks, D, D),
            whole(blocks, 1, D),
            whole(1, VEC),
            stepped(0, L, 1),
        ],
        [
            stepped(1, HEADS, L, 2 * HD),
            stepped(1, HEADS, L, 2 * HD),
            stepped(1, HEADS, L, HD),
            stepped(1, blocks, L, width),
            stepped(0, L, D),
            stepped(0, L, 1),
            stepped(0, L, D),
        ],
        [
            array(LOW, HEADS, tokens, 2 * HD),
            array(LOW, HEADS, tokens, 2 * HD),
            array(LOW, HEADS, tokens, HD),
            array(LOW, blocks, tokens, width),
            array(WIDE, tokens, D),
            array(WIDE, tokens, 1),
            array(LOW, tokens, D),
        ],
        [pltpu.VMEM((L, D), WIDE)],
        flops=24 * 10**9,
        args=(where, inputs, weights, bias, vectors, segments),
    )


def widen_kernel(where, h_ref, w_ref, vec_ref, active_out, slope_out):
    step = pl.program_id(0)
    hidden = dot(h_ref[...], w_ref[0]) + vec_ref[0]
    half = 0.5 * (1.0 + lax.erf(hidden * math.sqrt(0.5)))
    active_out[0] = (hidden * half).astype(LOW)
    density = jnp.exp(-0.5 * hidden * hidden) * (1.0 / math.sqrt(2.0 * math.pi))
    slope_out[0] = (half + hidden * density).astype(LOW)


def widen(where, normed_low, weights, bias):
    tokens = normed_low.shape[0]
    blocks = weights.shape[0]
    return call(
        widen_kernel,
        "widen",
        (blocks,),
        [whole(tokens, D), stepped(0, 1, D, D), stepped(0, 1, 1, D)],
        [stepped(0, 1, tokens, D)] * 2,
        [array(LOW, blocks, tokens, D)] * 2,
        flops=10 * 10**9,
        args=(where, normed_low, weights, bias),
    )


def narrow_kernel(blocks, where, active_ref, w_ref, vec_ref, unit_ref, starts_ref, out, unit_out, inverse_out, cls_out, y_ref):
    row = pl.program_id(0)
    total_sum = unit_ref[...] * vec_ref[:, G1 : G1 + D] + (
        vec_ref[:, C1 : C1 + D] + vec_ref[:, B2 : B2 + D]
    )
    for m in range(blocks):
        total_sum += dot(active_ref[m], w_ref[m], (1, 1))
    unit, inverse = normalize(total_sum)
    unit_out[...] = unit
    inverse_out[...] = inverse
    output = unit * vec_ref[:, G2 : G2 + D] + vec_ref[:, C2 : C2 + D]
    out[...] = output.astype(LOW)
    y_ref[...] = output
    for p in range(PASS):
        cls_out[pl.ds(row * PASS + p, 1), :] = y_ref[pl.ds(starts_ref[row * PASS + p], 1), :]


def narrow(where, active, weights, vectors, unit, starts):
    blocks, tokens, _ = active.shape
    rows = tokens // L
    return call(
        partial(narrow_kernel, blocks),
        "narrow",
        (rows,),
        [
            stepped(1, blocks, L, D),
            once(blocks, D, D),
            whole(1, VEC),
            stepped(0, L, D),
            pl.BlockSpec(memory_space=pltpu.SMEM),
        ],
        [stepped(0, L, D), stepped(0, L, D), stepped(0, L, 1), whole(rows * PASS, D)],
        [
            array(LOW, tokens, D),
            array(WIDE, tokens, D),
            array(WIDE, tokens, 1),
            array(WIDE, rows * PASS, D),
        ],
        [pltpu.VMEM((L, D), WIDE)],
        flops=5 * 10**9,
        args=(where, active, weights, vectors, unit, starts),
    )


def contrast_kernel(
    where, cot_ref, unit_ref, inverse_ref, vec_ref, starts_ref,
    own_ref, all_ref, ids_ref, partners_ref, ids_own_ref, partners_own_ref,
    grad_out, low_out, bias_out, gain_out, shift_out, cls_ref, y_ref,
):
    row = pl.program_id(0)
    scale = 2.0 / math.sqrt(D)

    @pl.when(row == 0)
    def _():
        everyone = all_ref[...]
        own = own_ref[...].astype(LOW)
        count = everyone.shape[0]
        scores = dot(everyone, everyone, (1, 1)) * scale
        diagonal = lax.broadcasted_iota(jnp.int32, (count, count), 0) == lax.broadcasted_iota(
            jnp.int32, (count, count), 1
        )
        scores = jnp.where(diagonal, masked_value, scores)
        highest = jnp.max(scores, axis=0, keepdims=True)
        log_all = highest + jnp.log(jnp.sum(jnp.exp(scores - highest), axis=0, keepdims=True))
        here = dot(own, everyone, (1, 1)) * scale
        ids = ids_ref[...]
        here = jnp.where(ids_own_ref[...] == ids, masked_value, here)
        top = jnp.max(here, axis=1, keepdims=True)
        log_own = top + jnp.log(jnp.sum(jnp.exp(here - top), axis=1, keepdims=True))
        out_pair = (partners_own_ref[...] == ids).astype(WIDE)
        in_pair = (ids_own_ref[...] == partners_ref[...]).astype(WIDE)
        out_grad = grid_weight * (jnp.exp(here - log_own) - out_pair)
        in_grad = grid_weight * (jnp.exp(here - log_all) - in_pair)
        cls_ref[...] = scale * (
            dot(out_grad.astype(LOW), everyone) + dot(in_grad.astype(LOW), everyone)
        )

    y_ref[...] = cot_ref[...].astype(WIDE)
    for p in range(PASS):
        y_ref[pl.ds(starts_ref[row * PASS + p], 1), :] += cls_ref[pl.ds(row * PASS + p, 1), :]
    grad = y_ref[...]
    unit = unit_ref[...]
    first = row == 0
    add_to(first, gain_out, column_sum(grad * unit))
    add_to(first, shift_out, column_sum(grad))
    back = norm_back(grad, unit, inverse_ref[...], vec_ref[:, G2 : G2 + D])
    grad_out[...] = back
    low = back.astype(LOW)
    low_out[...] = low
    add_to(first, bias_out, column_sum(low.astype(WIDE)))


def contrast(where, cotangent, unit, inverse, vectors, starts, own, everyone, ids, partners, ids_own, partners_own):
    tokens = cotangent.shape[0]
    count = everyone.shape[0]
    few = own.shape[0]
    return call(
        contrast_kernel,
        "contrast",
        (tokens // L,),
        [
            stepped(0, L, D),
            stepped(0, L, D),
            stepped(0, L, 1),
            whole(1, VEC),
            pl.BlockSpec(memory_space=pltpu.SMEM),
            whole(few, D),
            whole(count, D),
            whole(1, count),
            whole(1, count),
            whole(few, 1),
            whole(few, 1),
        ],
        [stepped(0, L, D), stepped(0, L, D), whole(1, D), whole(1, D), whole(1, D)],
        [
            array(WIDE, tokens, D),
            array(LOW, tokens, D),
            array(WIDE, 1, D),
            array(WIDE, 1, D),
            array(WIDE, 1, D),
        ],
        [pltpu.VMEM((few, D), WIDE), pltpu.VMEM((L, D), WIDE)],
        args=(where, cotangent, unit, inverse, vectors, starts, own, everyone, ids, partners, ids_own, partners_own),
    )


def down_grad_kernel(write, where, grad_ref, active_ref, out, turned):
    @pl.when(pl.program_id(0) == 0)
    def _():
        turned[...] = grad_ref[...].T

    write(out, dot(turned[...], active_ref[0]).astype(LOW), where)


def grad_of_down(where, grad_low, active, dp_size):
    blocks, tokens, _ = active.shape
    shape, block, index, write, pick = summand(blocks, dp_size)
    return call(
        partial(down_grad_kernel, write),
        "grad_of_down",
        (blocks,),
        [
            whole(tokens, D),
            pl.BlockSpec((1, tokens, D), lambda g, where: (pick(g, where), 0, 0)),
        ],
        pl.BlockSpec(block, index),
        array(LOW, *shape),
        [pltpu.VMEM((D, tokens), LOW)],
        flops=5 * 10**9,
        args=(where, grad_low, active),
    )


def up_grad_kernel(write, where, grad_ref, w_ref, slope_ref, h_ref, grad_out, bias_out, out, turned):
    @pl.when(pl.program_id(0) == 0)
    def _():
        turned[...] = h_ref[...].T

    hidden_grad = (dot(grad_ref[...], w_ref[0]) * slope_ref[0].astype(WIDE)).astype(LOW)
    grad_out[0] = hidden_grad
    bias_out[0] = column_sum(hidden_grad.astype(WIDE))
    write(out, dot(turned[...], hidden_grad).astype(LOW), where)


def grad_of_up(where, grad_low, down, slope, normed_low, dp_size):
    blocks, tokens, _ = slope.shape
    shape, block, index, write, pick = summand(blocks, dp_size)

    def at(*shape):
        return pl.BlockSpec(shape, lambda g, where: (pick(g, where), 0, 0))

    return call(
        partial(up_grad_kernel, write),
        "grad_of_up",
        (blocks,),
        [whole(tokens, D), at(1, D, D), at(1, tokens, D), whole(tokens, D)],
        [at(1, tokens, D), at(1, 1, D), pl.BlockSpec(block, index)],
        [array(LOW, blocks, tokens, D), array(WIDE, blocks, 1, D), array(LOW, *shape)],
        [pltpu.VMEM((D, tokens), LOW)],
        flops=10 * 10**9,
        args=(where, grad_low, down, slope, normed_low),
    )


def middle_kernel(
    blocks, where, hidden_ref, up_ref, sum_ref, unit_ref, inverse_ref, vec_ref, w_ref,
    grad_out, low_out, bias_out, gain_out, shift_out, context_out,
):
    first = pl.program_id(0) == 0
    width = D // blocks
    grad = sum_ref[...]
    for m in range(blocks):
        grad += dot(hidden_ref[m], up_ref[m], (1, 1))
    unit = unit_ref[...]
    add_to(first, gain_out, column_sum(grad * unit))
    add_to(first, shift_out, column_sum(grad))
    back = norm_back(grad, unit, inverse_ref[...], vec_ref[:, G1 : G1 + D])
    grad_out[...] = back
    low = back.astype(LOW)
    low_out[...] = low
    add_to(first, bias_out, column_sum(low.astype(WIDE)))
    for m in range(blocks):
        context_out[m] = dot(low, w_ref[m, :, :width]).astype(LOW)


def middle(where, hidden_grad, up, sum_grad, unit, inverse, vectors, weights):
    blocks, tokens, _ = hidden_grad.shape
    width = D // blocks
    return call(
        partial(middle_kernel, blocks),
        "middle",
        (tokens // L,),
        [
            stepped(1, blocks, L, D),
            once(blocks, D, D),
            stepped(0, L, D),
            stepped(0, L, D),
            stepped(0, L, 1),
            whole(1, VEC),
            once(blocks, D, D),
        ],
        [
            stepped(0, L, D),
            stepped(0, L, D),
            whole(1, D),
            whole(1, D),
            whole(1, D),
            stepped(1, blocks, L, width),
        ],
        [
            array(WIDE, tokens, D),
            array(LOW, tokens, D),
            array(WIDE, 1, D),
            array(WIDE, 1, D),
            array(WIDE, 1, D),
            array(LOW, blocks, tokens, width),
        ],
        flops=6 * 10**9,
        args=(where, hidden_grad, up, sum_grad, unit, inverse, vectors, weights),
    )


def attend_back_kernel(blocks, where, q_ref, k_ref, v_ref, grad_ref, out):
    heads = HEADS // blocks
    width = HD * heads

    def block(m, carry):
        out[m, :, :width] = jnp.zeros((L, width), LOW)
        for h in range(heads):
            queries, keys, value = q_ref[m * heads + h], k_ref[m * heads + h], v_ref[m * heads + h]
            grad = grad_ref[m, :, h * HD : (h + 1) * HD]
            weights = jnp.exp(dot(keys, queries, (1, 1)))
            weight_grad = dot(value, grad, (1, 1))
            middle_sum = jnp.sum(weight_grad * weights, axis=0, keepdims=True)
            score_grad = (weights * (weight_grad - middle_sum)).astype(LOW)
            at = width + h * HD
            query_grad = (dot(keys.T, score_grad)[:HD] * HD ** (-0.5)).T
            out[m, :, at : at + HD] = query_grad.astype(LOW)
            out[m, :, at + width : at + width + HD] = dot(score_grad, queries)[:, :HD].astype(LOW)
            out[m, :, at + 2 * width : at + 2 * width + HD] = dot(
                weights.astype(LOW), grad
            ).astype(LOW)
        return carry

    lax.fori_loop(0, blocks, block, 0)


def attend_back(where, queries, keys, values, context_grad):
    blocks, tokens, width = context_grad.shape
    return call(
        partial(attend_back_kernel, blocks),
        "attend_back",
        (tokens // L,),
        [
            stepped(1, HEADS, L, 2 * HD),
            stepped(1, HEADS, L, 2 * HD),
            stepped(1, HEADS, L, HD),
            stepped(1, blocks, L, width),
        ],
        stepped(1, blocks, L, D),
        array(LOW, blocks, tokens, D),
        flops=30 * 10**9,
        args=(where, queries, keys, values, context_grad),
    )


def attention_grad_kernel(write, where, x_ref, low_ref, grad_ref, context_ref, bias_out, out, x_turned, low_turned):
    @pl.when(pl.program_id(0) == 0)
    def _():
        x_turned[...] = x_ref[...].T
        low_turned[...] = low_ref[...].T

    width = context_ref.shape[2]
    grads = grad_ref[0]
    bias_out[0] = column_sum(grads.astype(WIDE))
    value = dot(x_turned[...], grads)
    own = dot(low_turned[...], context_ref[0])
    write(out, jnp.concatenate([own, value[:, width:]], axis=1).astype(LOW), where)


def grad_of_attention(where, inputs, grad_low, grads, context, dp_size):
    blocks, tokens, _ = grads.shape
    width = context.shape[2]
    shape, block, index, write, pick = summand(blocks, dp_size)

    def at(*shape):
        return pl.BlockSpec(shape, lambda g, where: (pick(g, where), 0, 0))

    return call(
        partial(attention_grad_kernel, write),
        "grad_of_attention",
        (blocks,),
        [whole(tokens, D), whole(tokens, D), at(1, tokens, D), at(1, tokens, width)],
        [at(1, 1, D), pl.BlockSpec(block, index)],
        [array(WIDE, blocks, 1, D), array(LOW, *shape)],
        [pltpu.VMEM((D, tokens), LOW)] * 2,
        flops=5 * 10**9,
        args=(where, inputs, grad_low, grads, context),
    )


def input_grad_kernel(blocks, where, grads_ref, w_ref, first_ref, out):
    total_sum = first_ref[...]
    for m in range(blocks):
        total_sum += dot(grads_ref[m], w_ref[m], (1, 1))
    out[...] = total_sum


def grad_of_input(where, grads, weights, first_grad):
    blocks, tokens, _ = grads.shape
    return call(
        partial(input_grad_kernel, blocks),
        "grad_of_input",
        (tokens // L,),
        [stepped(1, blocks, L, D), once(blocks, D, D), stepped(0, L, D)],
        stepped(0, L, D),
        array(WIDE, tokens, D),
        flops=5 * 10**9,
        args=(where, grads, weights, first_grad),
    )


def shards(
    block_input,
    cotangent,
    lengths,
    partner,
    qkv_weight,
    out_weight,
    up_weight,
    down_weight,
    qkv_first,
    out_first,
    up_first,
    down_first,
    qkv_second,
    out_second,
    up_second,
    down_second,
    vectors,
    vector_first,
    vector_second,
):
    mp_size = lax.axis_size("mp")
    dp_size = lax.axis_size("dp")
    mp_index = lax.axis_index("mp")
    dp_index = lax.axis_index("dp")
    tokens = cotangent.shape[0]
    rows = tokens // L
    own_rows = rows * PASS
    width = D // mp_size
    where = place()
    weights = gather(
        jnp.concatenate(
            [out_weight.T, qkv_weight[0], qkv_weight[1], qkv_weight[2]], axis=1
        ).astype(LOW)
    )
    up = gather(up_weight.astype(LOW))
    down = gather(down_weight.T.astype(LOW))
    local_lengths = lax.dynamic_slice_in_dim(lengths, mp_index * rows, rows, 0)
    inputs = lax.dynamic_slice_in_dim(block_input, mp_index * tokens, tokens, 0)
    segments = passage_ids(local_lengths).reshape(tokens, 1)
    starts = (jnp.cumsum(local_lengths, axis=1) - local_lengths).reshape(own_rows)
    partner_own = lax.dynamic_slice_in_dim(partner, mp_index * own_rows, own_rows, 0)
    ids_own = (dp_index * mp_size + mp_index) * own_rows + jnp.arange(own_rows, dtype=jnp.int32)
    partner_all = share(partner_own)
    ids_all = share(ids_own)
    vec = vectors.reshape(1, VEC)
    none = jnp.zeros((mp_size, width), WIDE)
    bias = jnp.concatenate(
        [none, vectors[:D].reshape(mp_size, width), none, vectors[D : 2 * D].reshape(mp_size, width)],
        axis=1,
    ).reshape(mp_size, 1, D)
    bias_up = vectors[2 * D : TAIL].reshape(mp_size, 1, D)

    queries, keys, values, context, unit_first, inverse_first, normed_low = attend(
        where, inputs, weights, bias, vec, segments
    )
    active, slope = widen(where, normed_low, up, bias_up)
    block_output, unit_second, inverse_second, cls_own = narrow(
        where, active, down, vec, unit_first, starts
    )
    cls_all = share(cls_own.astype(LOW))
    sum_grad, branch_low, down_bias_grad, gain_second_grad, shift_second_grad = contrast(
        where, cotangent, unit_second, inverse_second, vec, starts, cls_own, cls_all,
        ids_all[None, :], partner_all[None, :], ids_own[:, None], partner_own[:, None],
    )
    down_grad = scatter_sum(grad_of_down(where, branch_low, active, dp_size)).T
    hidden_grad, up_bias_grad, up_part = grad_of_up(where, branch_low, down, slope, normed_low, dp_size)
    up_grad = scatter_sum(up_part)
    first_grad, attended_low, out_bias_grad, gain_first_grad, shift_first_grad, context_grad = middle(
        where, hidden_grad, up, sum_grad, unit_first, inverse_first, vec, weights
    )
    grads = attend_back(where, queries, keys, values, context_grad)
    bias_grad, attention_part = grad_of_attention(
        where, inputs, attended_low, grads, context, dp_size
    )
    mixed = scatter_sum(attention_part)
    input_grad = grad_of_input(where, grads, weights, first_grad)
    qkv_grad = jnp.stack([mixed[:, i * width : (i + 1) * width] for i in (1, 2, 3)])
    out_grad = mixed[:, :width].T
    bias_grad = bias_grad.reshape(mp_size, D)
    vector_local = jnp.concatenate(
        [
            bias_grad[:, width : 2 * width].reshape(D),
            bias_grad[:, 3 * width :].reshape(D),
            up_bias_grad.reshape(FF),
            out_bias_grad[0],
            down_bias_grad[0],
            gain_first_grad[0],
            shift_first_grad[0],
            gain_second_grad[0],
            shift_second_grad[0],
        ]
    )
    vector_grad = total(vector_local)
    qkv_second_new, qkv_ratio = adapt(qkv_grad, qkv_first, qkv_second)
    out_second_new, out_ratio = adapt(out_grad, out_first, out_second)
    up_second_new, up_ratio = adapt(up_grad, up_first, up_second)
    down_second_new, down_ratio = adapt(down_grad, down_first, down_second)
    qkv_update = qkv_ratio + weight_decay * qkv_weight
    out_update = out_ratio + weight_decay * out_weight
    up_update = up_ratio + weight_decay * up_weight
    down_update = down_ratio + weight_decay * down_weight
    weight_squares = jnp.concatenate(
        [
            jnp.sum(qkv_weight * qkv_weight, axis=(1, 2)),
            jnp.sum(out_weight * out_weight)[None],
            jnp.sum(up_weight * up_weight)[None],
            jnp.sum(down_weight * down_weight)[None],
        ]
    )
    update_squares = jnp.concatenate(
        [
            jnp.sum(qkv_update * qkv_update, axis=(1, 2)),
            jnp.sum(out_update * out_update)[None],
            jnp.sum(up_update * up_update)[None],
            jnp.sum(down_update * down_update)[None],
        ]
    )
    weight_norms = jnp.sqrt(total(weight_squares))
    update_norms = jnp.sqrt(total(update_squares))
    trust = weight_norms / (update_norms + norm_guard)
    qkv_new = qkv_weight - rate_matrix * trust[0:3, None, None] * qkv_update
    out_new = out_weight - rate_matrix * trust[3] * out_update
    up_new = up_weight - rate_matrix * trust[4] * up_update
    down_new = down_weight - rate_matrix * trust[5] * down_update
    vector_second_new, vector_ratio = adapt(vector_grad, vector_first, vector_second)
    vector_new = vectors - rate_vector * vector_ratio
    norms = jnp.stack([weight_norms, update_norms], axis=1)
    return (
        block_output,
        input_grad,
        qkv_grad,
        out_grad,
        up_grad,
        down_grad,
        qkv_second_new,
        out_second_new,
        up_second_new,
        down_second_new,
        qkv_new,
        out_new,
        up_new,
        down_new,
        qkv_new.astype(jnp.bfloat16),
        out_new.astype(jnp.bfloat16),
        up_new.astype(jnp.bfloat16),
        down_new.astype(jnp.bfloat16),
        vector_grad,
        vector_second_new,
        vector_new,
        norms,
    )


def solution(mesh):
    in_specs = (
        P("dp", None),
        P(("dp", "mp"), None),
        P("dp", None),
        P("dp"),
        P(None, "dp", "mp"),
        P("mp", "dp"),
        P("dp", "mp"),
        P("mp", "dp"),
        P(None, "dp", "mp"),
        P("mp", "dp"),
        P("dp", "mp"),
        P("mp", "dp"),
        P(None, "dp", "mp"),
        P("mp", "dp"),
        P("dp", "mp"),
        P("mp", "dp"),
        P(),
        P(),
        P(),
    )
    out_specs = (
        P(("dp", "mp"), None),
        P(("dp", "mp"), None),
        P(None, "dp", "mp"),
        P("mp", "dp"),
        P("dp", "mp"),
        P("mp", "dp"),
        P(None, "dp", "mp"),
        P("mp", "dp"),
        P("dp", "mp"),
        P("mp", "dp"),
        P(None, "dp", "mp"),
        P("mp", "dp"),
        P("dp", "mp"),
        P("mp", "dp"),
        P(None, "dp", "mp"),
        P("mp", "dp"),
        P("dp", "mp"),
        P("mp", "dp"),
        P(),
        P(),
        P(),
        P(),
    )
    return jax.shard_map(shards, mesh=mesh, in_specs=in_specs, out_specs=out_specs, check_vma=False)
```

time: 1360 us -> 473 us (0.35)
  waiting for transfers between devices: 737 us -> 117 us
  matrix products: 243 us -> 0 us
  Pallas kernels: 0 us -> 172 us
  blocking collectives: 158 us -> 0 us
  starting transfers between devices: 0.47 us -> 93.9 us
  local copies, waits for them, and re-layouts: 103 us -> 39.2 us
  other arithmetic: 97.2 us -> 40.1 us
  between operations: 16.8 us -> 2.16 us
    reduce_scatter x5 -> x0, waiting for transfers between devices: 407 us -> none  [the longest x1 99.2 us: shards(): lax.psum_scatter(jnp.einsum('tu,du->td', hidden_grad, up_use, preferred_e...]
    dot_general x73 -> x0, matrix products: 243 us -> none  [the longest x1 35 us: shards(): jnp.dot(whole_normed, up_use, preferred_element_type=jnp.float32) + bias_up]
    psum x1 -> x0, waiting for transfers between devices: 204 us -> none  [shards(): lax.psum((local_grads[0], local_grads[1], local_grads[2], local_grads[3])...]
    pallas_call x0 -> x13, Pallas kernels: none -> 172 us  [the longest x10 152 us: call(): pl.pallas_call(kernel, grid_spec=pltpu.PrefetchScalarGridSpec(num_scalar_...]
    all_gather x5 -> x0, waiting for transfers between devices: 125 us -> none  [the longest x1 45.5 us: shards(): whole_branch = lax.all_gather(branch_grad, 'mp', axis=0, tiled=True)]
    ppermute x0 -> x90, waiting for transfers between devices: none -> 117 us  [send(): return lax.ppermute(value, AXES, pairs)]
    all_gather x3 -> x0, blocking collectives: 112 us -> none  [the longest x1 41.6 us: shards(): every_cls = lax.all_gather(local_cls, ('dp', 'mp'), axis=0, tiled=True)]
    ppermute x0 -> x90, starting transfers between devices: none -> 93.9 us  [send(): return lax.ppermute(value, AXES, pairs)]
  transfers between devices with their start and end apart: 11 -> 90, of which waited for: 10 -> 38; matrix products, arithmetic and copies ran while one was open for 10% -> 11% of each run, Pallas kernels for 0% -> 34%
where the time goes in v1:
time: 473 us; the launch traced here: 464 us
  Pallas kernels  172 us (36%)
  waiting for transfers between devices  117 us (25%)
  starting transfers between devices  93.9 us (20%)
  other arithmetic  40.1 us (8%)
  local copies, waits for them, and re-layouts  39.2 us (8%)
    pallas_call x10, Pallas kernels, call(): pl.pallas_call(kernel, grid_spec=pltpu.PrefetchScalarGridSpec(num_scalar_...  152 us
    ppermute x90, waiting for transfers between devices, send(): return lax.ppermute(value, AXES, pairs)  117 us
    ppermute x90, starting transfers between devices, send(): return lax.ppermute(value, AXES, pairs)  93.9 us
    unnamed x131, local copies, waits for them, and re-layouts  21 us
    pallas_call x3, Pallas kernels, gather(): pl.pallas_call(settle_kernel, grid_spec=pltpu.PrefetchScalarGridSpec(num_...  19.6 us
    squeeze x3, local copies, waits for them, and re-layouts, scatter_sum(): items = plus(items[0], send(items[1], CORE))  10.1 us
  transfers between devices with their start and end apart: 90, of which 38 were waited for; matrix products, arithmetic and copies ran while one was open for 11% of the time, Pallas kernels for 34%

profile of v1, /device:TPU:0, one launch (start us, length us, event | category | flops | bytes accessed | tf_op | source)
XLA Modules:
  0.0 464.0 jit_solution(15936216963756530358)
XLA Ops:
  37.1 8.3 %collective-permute-done.24 = bf16[96,768]{1,0:T(8,128)(2,1)S(1)} collective-permute-done((bf16[96,768]{1,0:T(8,128)(2,1)}, bf16[96,768]{1,0:T(8,128)(2,1)S(1)}, u32[]{:S(2)}, u32[]{:S(2)}) %collective-permute-start.24) | collective-permute-done | bytes 147488 | tf_op jit(solution)/shard_map/ppermute | solution.py:75
  49.2 6.2 %collective-permute-done.40 = s32[16]{0:T(128)S(1)} collective-permute-done((s32[16]{0:T(128)S(1)}, s32[16]{0:T(128)S(1)}, u32[]{:S(2)}, u32[]{:S(2)}) %collective-permute-start.40) | collective-permute-done | bytes 96 | tf_op jit(solution)/shard_map/ppermute | solution.py:75
  69.0 6.3 %collective-permute-done.23 = bf16[2,96,768]{2,1,0:T(8,128)(2,1)} collective-permute-done((bf16[2,96,768]{2,1,0:T(8,128)(2,1)}, bf16[2,96,768]{2,1,0:T(8,128)(2,1)}, u32[]{:S(2)}, u32[]{:S(2)}) %collective-permute-start.23) | collective-permute-done | bytes 294944 | tf_op jit(solution)/shard_map/ppermute | solution.py:75
  81.4 4.3 settle.3
  94.2 29.3 %attend.1 = (bf16[12,1024,128]{2,1,0:T(8,128)(2,1)}, bf16[12,1024,128]{2,1,0:T(8,128)(2,1)}, bf16[12,1024,64]{2,1,0:T(8,128)(2,1)}, bf16[4,1024,192]{2,1,0:T(8,1...) custom-call(s32[4]{0:T(128)S(1)} %pad_add_fusion.where, ...), custom_call_target="tpu_custom_call" | custom-call | flops 24000000000 | bytes 1048576 | tf_op jit(solution)/shard_map/attend/pallas_call | solution.py:219
  125.8 7.7 %settle.4 = bf16[4,8,96,768]{3,2,1,0:T(8,128)(2,1)S(1)} custom-call(s32[4]{0:T(128)S(1)} %pad_add_fusion.where, bf16[4,96,768]{2,1,0:T(8,128)(2,1)S(1)} %pad_maximum_fusion.2.refs_0_, bf16[4,96,768]{2,1,0:T(8,128)(2,1)S(1)} %pad_maximum_fusion.3.refs_1_, bf16[4,96,768]{2,1,0:T(8,128)(2,1)S(1)} %collective-permute-done.16.refs_2_, ...), custom_call_target="tpu_custom_call" | custom-call | tf_op jit(solution)/shard_map/settle/pallas_call | solution.py:124
  135.7 12.2 %widen.1 = (bf16[4,1024,768]{2,1,0:T(8,128)(2,1)}, bf16[4,1024,768]{2,1,0:T(8,128)(2,1)}) custom-call(s32[4]{0:T(128)S(1)} %pad_add_fusion.where, bf16[1024,768]{1,0:T(8,128)(2,1)S(1)} %get-tuple-element.51.h_ref, bf16[4,768,768]{2,1,0:T(8,128)(2,1)} %bitcast.221, f32[4,1,768]{2,1,0:T(1,128)S(1)} %bitcast.230), custom_call_target="tpu_custom_call" | custom-call | flops 10000000000 | bytes 1048576 | tf_op jit(solution)/shard_map/widen/pallas_call | solution.py:219
  154.0 7.7 %settle.5 = bf16[4,8,96,768]{3,2,1,0:T(8,128)(2,1)S(1)} custom-call(s32[4]{0:T(128)S(1)} %pad_add_fusion.where, bf16[4,96,768]{2,1,0:T(8,128)(2,1)S(1)} %pad_maximum_fusion.4.refs_0_, bf16[4,96,768]{2,1,0:T(8,128)(2,1)S(1)} %pad_maximum_fusion.5.refs_1_, bf16[4,96,768]{2,1,0:T(8,128)(2,1)S(1)} %collective-permute-done.27.refs_2_, ...), custom_call_target="tpu_custom_call" | custom-call | tf_op jit(solution)/shard_map/settle/pallas_call | solution.py:124
  163.8 11.5 %narrow.1 = (bf16[1024,768]{1,0:T(8,128)(2,1)}, f32[1024,768]{1,0:T(8,128)S(1)}, f32[1024,1]{1,0:T(8,128)S(1)}, f32[8,768]{1,0:T(8,128)S(1)}) custom-call(s32[4]{0:T(128)S(1)} %pad_add_fusion.where, bf16[4,1024,768]{2,1,0:T(8,128)(2,1)} %get-tuple-element.52.active_ref, bf16[4,768,768]{2,1,0:T(8,128)(2,1)} %bitcast.223, f32[1,9216]{1,0:T(1,128)S(1)} %bitcast.227, ...), custom_call_target="tpu_custom_call" | custom-call | flops 5000000000 | bytes 1048576 | tf_op jit(solution)/shard_map/narrow/pallas_call | solution.py:219
  205.4 6.3 %contrast.1 = (f32[1024,768]{1,0:T(8,128)}, bf16[1024,768]{1,0:T(8,128)(2,1)S(1)}, f32[1,768]{1,0:T(1,128)S(1)}, f32[1,768]{1,0:T(1,128)S(1)}, f32[1,768]{1,0:T(1,128)S(1)}) custom-call(s32[4]{0:T(128)S(1)} %pad_add_fusion.where, bf16[1024,768]{1,0:T(8,128)(2,1)S(1)} %copy-done.4, f32[1024,768]{1,0:T(8,128)} %copy-done.3, f32[1024,1]{1,0:T(8,128)S(1)} %copy-done.8, ...), custom_call_target="tpu_custom_call" | custom-call | bytes 1048576 | tf_op jit(solution)/shard_map/contrast/pallas_call | solution.py:219
  211.8 9.6 %grad_of_down.1 = bf16[2,2,2,4,96,768]{5,4,3,2,1,0:T(8,128)(2,1)} custom-call(s32[4]{0:T(128)S(1)} %pad_add_fusion.where, bf16[1024,768]{1,0:T(8,128)(2,1)S(1)} %get-tuple-element.61.grad_ref, bf16[4,1024,768]{2,1,0:T(8,128)(2,1)} %get-tuple-element.52.active_ref), custom_call_target="tpu_custom_call" | custom-call | flops 5000000000 | bytes 1048576 | tf_op jit(solution)/shard_map/grad_of_down/pallas_call | solution.py:219
  224.8 14.9 %grad_of_up.1 = (bf16[4,1024,768]{2,1,0:T(8,128)(2,1)}, f32[4,1,768]{2,1,0:T(1,128)S(1)}, bf16[2,2,2,4,96,768]{5,4,3,2,1,0:T(8,128)(2,1)}) custom-call(s32[4]{0:T(128)S(1)} %pad_add_fusion.where, bf16[1024,768]{1,0:T(8,128)(2,1)S(1)} %get-tuple-element.61.grad_ref, bf16[4,768,768]{2,1,0:T(8,128)(2,1)} %bitcast.224, ...), custom_call_target="tpu_custom_call" | custom-call | flops 10000000000 | bytes 1048576 | tf_op jit(solution)/shard_map/grad_of_up/pallas_call | solution.py:219
  239.7 18.8 %middle.1 = (f32[1024,768]{1,0:T(8,128)}, bf16[1024,768]{1,0:T(8,128)(2,1)S(1)}, f32[1,768]{1,0:T(1,128)S(1)}, f32[1,768]{1,0:T(1,128)S(1)}, f32[1,768]{1,0:T(1,128)S(1)}, /*index=5*/bf16[4,1024,192]{2,1,0:T(8,128)(2,1)S(1)}) custom-call(s32[4]{0:T(128)S(1)} %pad_add_fusion.where, bf16[4,1024,768]{2,1,0:T(8,128)(2,1)} %get-tuple-element.63.hidden_ref, ...), custom_call_target="tpu_custom_call" | custom-call | flops 6000000000 | bytes 1048576 | tf_op jit(solution)/shard_map/middle/pallas_call | solution.py:219
  258.6 27.3 %attend_back.1.grads_ref.grad_ref = bf16[4,1024,768]{2,1,0:T(8,128)(2,1)} custom-call(s32[4]{0:T(128)S(1)} %pad_add_fusion.where, bf16[12,1024,128]{2,1,0:T(8,128)(2,1)S(1)} %copy-done.16, bf16[12,1024,128]{2,1,0:T(8,128)(2,1)} %get-tuple-element.56.k_ref, bf16[12,1024,64]{2,1,0:T(8,128)(2,1)} %get-tuple-element.57.v_ref, ...), custom_call_target="tpu_custom_call" | custom-call | flops 30000001024 | bytes 1048576 | tf_op jit(solution)/shard_map/attend_back/pallas_call | solution.py:219
  285.9 11.4 %grad_of_attention.1 = (f32[4,1,768]{2,1,0:T(1,128)S(1)}, bf16[2,2,2,4,96,768]{5,4,3,2,1,0:T(8,128)(2,1)}) custom-call(s32[4]{0:T(128)S(1)} %pad_add_fusion.where, bf16[1024,768]{1,0:T(8,128)(2,1)S(1)} %constant_dynamic-slice_fusion.1.x_ref, bf16[1024,768]{1,0:T(8,128)(2,1)S(1)} %get-tuple-element.68.low_ref, ...), custom_call_target="tpu_custom_call" | custom-call | flops 5000000000 | bytes 1048576 | tf_op jit(solution)/shard_map/grad_of_attention/pallas_call | solution.py:219
  316.5 10.5 %grad_of_input.1 = f32[1024,768]{1,0:T(8,128)} custom-call(s32[4]{0:T(128)S(1)} %pad_add_fusion.where, bf16[4,1024,768]{2,1,0:T(8,128)(2,1)} %attend_back.1.grads_ref.grad_ref, bf16[4,768,768]{2,1,0:T(8,128)(2,1)} %bitcast.220, f32[1024,768]{1,0:T(8,128)S(1)} %copy-done.12), custom_call_target="tpu_custom_call" | custom-call | flops 5000000000 | bytes 1048576 | tf_op jit(solution)/shard_map/grad_of_input/pallas_call | solution.py:219
  340.5 5.9 %collective-permute-done.68 = bf16[2,2,96,768]{3,2,1,0:T(8,128)(2,1)S(1)} collective-permute-done((bf16[2,2,96,768]{3,2,1,0:T(8,128)(2,1)S(1)}, bf16[2,2,96,768]{3,2,1,0:T(8,128)(2,1)S(1)}, u32[]{:S(2)}, u32[]{:S(2)}) %collective-permute-start.68) | collective-permute-done | bytes 589856 | tf_op jit(solution)/shard_map/ppermute | solution.py:75
  348.8 10.2 %collective-permute-done.60 = bf16[2,2,96,768]{3,2,1,0:T(8,128)(2,1)S(1)} collective-permute-done((bf16[2,2,96,768]{3,2,1,0:T(8,128)(2,1)S(1)}, bf16[2,2,96,768]{3,2,1,0:T(8,128)(2,1)S(1)}, u32[]{:S(2)}, u32[]{:S(2)}) %collective-permute-start.60) | collective-permute-done | bytes 589856 | tf_op jit(solution)/shard_map/ppermute | solution.py:75
  360.9 10.8 %collective-permute-done.52 = bf16[2,2,96,768]{3,2,1,0:T(8,128)(2,1)S(1)} collective-permute-done((bf16[2,2,96,768]{3,2,1,0:T(8,128)(2,1)S(1)}, bf16[2,2,96,768]{3,2,1,0:T(8,128)(2,1)S(1)}, u32[]{:S(2)}, u32[]{:S(2)}) %collective-permute-start.52) | collective-permute-done | bytes 589856 | tf_op jit(solution)/shard_map/ppermute | solution.py:75
  373.6 5.6 %collective-permute-done.69 = bf16[2,96,768]{2,1,0:T(8,128)(2,1)S(1)} collective-permute-done((bf16[2,96,768]{2,1,0:T(8,128)(2,1)S(1)}, bf16[2,96,768]{2,1,0:T(8,128)(2,1)S(1)}, u32[]{:S(2)}, u32[]{:S(2)}) %collective-permute-start.69) | collective-permute-done | bytes 294944 | tf_op jit(solution)/shard_map/ppermute | solution.py:75
  381.4 9.3 %collective-permute-done.53 = bf16[2,96,768]{2,1,0:T(8,128)(2,1)S(1)} collective-permute-done((bf16[2,96,768]{2,1,0:T(8,128)(2,1)S(1)}, bf16[2,96,768]{2,1,0:T(8,128)(2,1)S(1)}, u32[]{:S(2)}, u32[]{:S(2)}) %collective-permute-start.53) | collective-permute-done | bytes 294944 | tf_op jit(solution)/shard_map/ppermute | solution.py:75
  401.3 7.4 %collective-permute-done.57 = bf16[96,768]{1,0:T(8,128)(2,1)S(1)} collective-permute-done((bf16[96,768]{1,0:T(8,128)(2,1)S(1)}, bf16[96,768]{1,0:T(8,128)(2,1)S(1)}, u32[]{:S(2)}, u32[]{:S(2)}) %collective-permute-start.57) | collective-permute-done | bytes 147488 | tf_op jit(solution)/shard_map/ppermute | solution.py:75
  408.7 4.9 %collective-permute-start.62 = (bf16[96,768]{1,0:T(8,128)(2,1)S(1)}, bf16[96,768]{1,0:T(8,128)(2,1)S(1)}, u32[]{:S(2)}, u32[]{:S(2)}) collective-permute-start(bf16[96,768]{1,0:T(8,128)(2,1)S(1)} %slice_bitcast_fusion.34), channel_id=1, source_target_pairs={{0,8},{1,9},{2,10},{3,11},{4,12},{5,13},{6,14},{7,15},{8,16},{9,17... | collective-permute-start | bytes 442376 | tf_op jit(solution)/shard_map/ppermute | solution.py:75
  422.3 4.3 collective-permute-done.65
  (427 shorter events, 211.0 us)
Async XLA Ops:
  2.8 24.2 %collective-permute-start.2 = (bf16[96,768]{1,0:T(8,128)(2,1)S(1)}, bf16[96,768]{1,0:T(8,128)(2,1)S(1)}, u32[]{:S(2)}, u32[]{:S(2)}) collective-permute-start(bf16[96,768]{1,0:T(8,128)(2,1)S(1)} %pad_maximum_fusion.13), channel_id=1, source_target_pairs={{0,16},{1,17},{2,18},{3,19},{4,20},{5,21},{6,22},{7,23},{8,24},{9,... | collective-permute-start | bytes 442376 | tf_op jit(solution)/shard_map/ppermute | solution.py:75
  31.4 29.1 %collective-permute-start.22 = (bf16[96,768]{1,0:T(8,128)(2,1)}, bf16[96,768]{1,0:T(8,128)(2,1)S(1)}, u32[]{:S(2)}, u32[]{:S(2)}) collective-permute-start(bf16[96,768]{1,0:T(8,128)(2,1)} %get-tuple-element.185), channel_id=1, source_target_pairs={{0,8},{1,9},{2,10},{3,11},{4,12},{5,13},{6,14},{7,15},{8,16},{9,17... | collective-permute-start | bytes 442376 | tf_op jit(solution)/shard_map/ppermute | solution.py:75
  80.9 43.4 %collective-permute-start.18 = (bf16[4,96,768]{2,1,0:T(8,128)(2,1)S(1)}, bf16[4,96,768]{2,1,0:T(8,128)(2,1)S(1)}, u32[]{:S(2)}, u32[]{:S(2)}) collective-permute-start(bf16[4,96,768]{2,1,0:T(8,128)(2,1)S(1)} %pad_maximum_fusion.2.refs_0_), channel_id=1, source_target_pairs={{0,1},{1,0},{2,3},{3,2},{4,5},{5,4},{6,7},{7,6},{8,9},{9,8},{10,11... | collective-permute-start | bytes 1769480 | tf_op jit(solution)/shard_map/ppermute | solution.py:75
  81.4 43.4 %collective-permute-start.28 = (bf16[4,96,768]{2,1,0:T(8,128)(2,1)S(1)}, bf16[4,96,768]{2,1,0:T(8,128)(2,1)S(1)}, u32[]{:S(2)}, u32[]{:S(2)}) collective-permute-start(bf16[4,96,768]{2,1,0:T(8,128)(2,1)S(1)} %pad_maximum_fusion.5.refs_1_), channel_id=1, source_target_pairs={{0,4},{1,5},{2,6},{3,7},{4,0},{5,1},{6,2},{7,3},{8,12},{9,13},{10,... | collective-permute-start | bytes 1769480 | tf_op jit(solution)/shard_map/ppermute | solution.py:75
  91.7 33.1 %collective-permute-start.27 = (bf16[4,96,768]{2,1,0:T(8,128)(2,1)S(1)}, bf16[4,96,768]{2,1,0:T(8,128)(2,1)S(1)}, u32[]{:S(2)}, u32[]{:S(2)}) collective-permute-start(bf16[4,96,768]{2,1,0:T(8,128)(2,1)S(1)} %pad_maximum_fusion.4.refs_0_), channel_id=1, source_target_pairs={{0,2},{1,3},{2,0},{3,1},{4,6},{5,7},{6,4},{7,5},{8,10},{9,11},{10,... | collective-permute-start | bytes 1769480 | tf_op jit(solution)/shard_map/ppermute | solution.py:75
  93.7 31.6 %collective-permute-start.21 = (bf16[4,96,768]{2,1,0:T(8,128)(2,1)S(1)}, bf16[4,96,768]{2,1,0:T(8,128)(2,1)S(1)}, u32[]{:S(2)}, u32[]{:S(2)}) collective-permute-start(bf16[4,96,768]{2,1,0:T(8,128)(2,1)S(1)} %collective-permute-done.17.refs_3_), channel_id=1, source_target_pairs={{0,1},{1,0},{2,3},{3,2},{4,5},{5,4},{6,7},{7,6},{8,9},{9,8},{10,11... | collective-permute-start | bytes 1769480 | tf_op jit(solution)/shard_map/ppermute | solution.py:75
  93.7 31.7 %collective-permute-start.20 = (bf16[4,96,768]{2,1,0:T(8,128)(2,1)S(1)}, bf16[4,96,768]{2,1,0:T(8,128)(2,1)S(1)}, u32[]{:S(2)}, u32[]{:S(2)}) collective-permute-start(bf16[4,96,768]{2,1,0:T(8,128)(2,1)S(1)} %collective-permute-done.16.refs_2_), channel_id=1, source_target_pairs={{0,1},{1,0},{2,3},{3,2},{4,5},{5,4},{6,7},{7,6},{8,9},{9,8},{10,11... | collective-permute-start | bytes 1769480 | tf_op jit(solution)/shard_map/ppermute | solution.py:75
  124.3 54.2 %collective-permute-start.41 = (s32[32]{0:T(128)S(1)}, s32[32]{0:T(128)S(1)}, u32[]{:S(2)}, u32[]{:S(2)}) collective-permute-start(s32[32]{0:T(128)S(1)} %pad_add_fusion.2), channel_id=1, source_target_pairs={{0,2},{1,3},{2,0},{3,1},{4,6},{5,7},{6,4},{7,5},{8,10},{9,11},{10,... | collective-permute-start | bytes 392 | tf_op jit(solution)/shard_map/ppermute | solution.py:75
  124.8 26.6 %collective-permute-start.29 = (bf16[4,96,768]{2,1,0:T(8,128)(2,1)S(1)}, bf16[4,96,768]{2,1,0:T(8,128)(2,1)S(1)}, u32[]{:S(2)}, u32[]{:S(2)}) collective-permute-start(bf16[4,96,768]{2,1,0:T(8,128)(2,1)S(1)} %pad_maximum_fusion.4.refs_0_), channel_id=1, source_target_pairs={{0,1},{1,0},{2,3},{3,2},{4,5},{5,4},{6,7},{7,6},{8,9},{9,8},{10,11... | collective-permute-start | bytes 1769480 | tf_op jit(solution)/shard_map/ppermute | solution.py:75
  125.3 26.6 %collective-permute-start.32 = (bf16[4,96,768]{2,1,0:T(8,128)(2,1)S(1)}, bf16[4,96,768]{2,1,0:T(8,128)(2,1)S(1)}, u32[]{:S(2)}, u32[]{:S(2)}) collective-permute-start(bf16[4,96,768]{2,1,0:T(8,128)(2,1)S(1)} %collective-permute-done.28.refs_3_), channel_id=1, source_target_pairs={{0,1},{1,0},{2,3},{3,2},{4,5},{5,4},{6,7},{7,6},{8,9},{9,8},{10,11... | collective-permute-start | bytes 1769480 | tf_op jit(solution)/shard_map/ppermute | solution.py:75
  125.4 28.6 %collective-permute-start.31 = (bf16[4,96,768]{2,1,0:T(8,128)(2,1)S(1)}, bf16[4,96,768]{2,1,0:T(8,128)(2,1)S(1)}, u32[]{:S(2)}, u32[]{:S(2)}) collective-permute-start(bf16[4,96,768]{2,1,0:T(8,128)(2,1)S(1)} %collective-permute-done.27.refs_2_), channel_id=1, source_target_pairs={{0,1},{1,0},{2,3},{3,2},{4,5},{5,4},{6,7},{7,6},{8,9},{9,8},{10,11... | collective-permute-start | bytes 1769480 | tf_op jit(solution)/shard_map/ppermute | solution.py:75
  147.8 30.9 %collective-permute-start.48 = (s32[64]{0:T(128)S(1)}, s32[64]{0:T(128)S(1)}, u32[]{:S(2)}, u32[]{:S(2)}) collective-permute-start(s32[64]{0:T(128)S(1)} %pad_add_fusion.6), channel_id=1, source_target_pairs={{0,8},{1,9},{2,10},{3,11},{4,12},{5,13},{6,14},{7,15},{8,16},{9,17... | collective-permute-start | bytes 776 | tf_op jit(solution)/shard_map/ppermute | solution.py:75
  151.4 29.7 %collective-permute-start.49 = (s32[64]{0:T(128)S(1)}, s32[64]{0:T(128)S(1)}, u32[]{:S(2)}, u32[]{:S(2)}) collective-permute-start(s32[64]{0:T(128)S(1)} %pad_add_fusion.6), channel_id=1, source_target_pairs={{0,16},{1,17},{2,18},{3,19},{4,20},{5,21},{6,22},{7,23},{8,24},{9,... | collective-permute-start | bytes 776 | tf_op jit(solution)/shard_map/ppermute | solution.py:75
  151.9 30.6 %collective-permute-start.50 = (s32[64]{0:T(128)S(1)}, s32[64]{0:T(128)S(1)}, u32[]{:S(2)}, u32[]{:S(2)}) collective-permute-start(s32[64]{0:T(128)S(1)} %pad_add_fusion.6), channel_id=1, source_target_pairs={{0,24},{1,25},{2,26},{3,27},{4,28},{5,29},{6,30},{7,31},{8,0},{9,1... | collective-permute-start | bytes 776 | tf_op jit(solution)/shard_map/ppermute | solution.py:75
  224.8 103.0 %collective-permute-start.67 = (bf16[2,2,4,96,768]{4,3,2,1,0:T(8,128)(2,1)}, bf16[2,2,4,96,768]{4,3,2,1,0:T(8,128)(2,1)}, u32[]{:S(2)}, u32[]{:S(2)}) collective-permute-start(bf16[2,2,4,96,768]{4,3,2,1,0:T(8,128)(2,1)} %slice_bitcast_fusion), channel_id=1, source_target_pairs={{0,1},{1,0},{2,3},{3,2},{4,5},{5,4},{6,7},{7,6},{8,9},{9,8},{10,11... | collective-permute-start | bytes 7077896 | tf_op jit(solution)/shard_map/ppermute | solution.py:75
  301.6 30.1 %collective-permute-start.59 = (bf16[2,2,4,96,768]{4,3,2,1,0:T(8,128)(2,1)}, bf16[2,2,4,96,768]{4,3,2,1,0:T(8,128)(2,1)}, u32[]{:S(2)}, u32[]{:S(2)}) collective-permute-start(bf16[2,2,4,96,768]{4,3,2,1,0:T(8,128)(2,1)} %slice_bitcast_fusion.2), channel_id=1, source_target_pairs={{0,1},{1,0},{2,3},{3,2},{4,5},{5,4},{6,7},{7,6},{8,9},{9,8},{10,11... | collective-permute-start | bytes 7077896 | tf_op jit(solution)/shard_map/ppermute | solution.py:75
  334.3 24.7 %collective-permute-start.60 = (bf16[2,2,96,768]{3,2,1,0:T(8,128)(2,1)S(1)}, bf16[2,2,96,768]{3,2,1,0:T(8,128)(2,1)S(1)}, u32[]{:S(2)}, u32[]{:S(2)}) collective-permute-start(bf16[2,2,96,768]{3,2,1,0:T(8,128)(2,1)S(1)} %slice_bitcast_fusion.10), channel_id=1, source_target_pairs={{0,2},{1,3},{2,0},{3,1},{4,6},{5,7},{6,4},{7,5},{8,10},{9,11},{10,... | collective-permute-start | bytes 1769480 | tf_op jit(solution)/shard_map/ppermute | solution.py:75
  335.3 24.9 %collective-permute-start.63 = (bf16[2,2,96,768]{3,2,1,0:T(8,128)(2,1)S(1)}, bf16[2,2,96,768]{3,2,1,0:T(8,128)(2,1)S(1)}, u32[]{:S(2)}, u32[]{:S(2)}) collective-permute-start(bf16[2,2,96,768]{3,2,1,0:T(8,128)(2,1)S(1)} %slice_bitcast_fusion.8), channel_id=1, source_target_pairs={{0,4},{1,5},{2,6},{3,7},{4,0},{5,1},{6,2},{7,3},{8,12},{9,13},{10,... | collective-permute-start | bytes 1769480 | tf_op jit(solution)/shard_map/ppermute | solution.py:75
  339.5 32.2 %collective-permute-start.52 = (bf16[2,2,96,768]{3,2,1,0:T(8,128)(2,1)S(1)}, bf16[2,2,96,768]{3,2,1,0:T(8,128)(2,1)S(1)}, u32[]{:S(2)}, u32[]{:S(2)}) collective-permute-start(bf16[2,2,96,768]{3,2,1,0:T(8,128)(2,1)S(1)} %slice_bitcast_fusion.14), channel_id=1, source_target_pairs={{0,2},{1,3},{2,0},{3,1},{4,6},{5,7},{6,4},{7,5},{8,10},{9,11},{10,... | collective-permute-start | bytes 1769480 | tf_op jit(solution)/shard_map/ppermute | solution.py:75
  346.4 26.4 %collective-permute-start.55 = (bf16[2,2,96,768]{3,2,1,0:T(8,128)(2,1)S(1)}, bf16[2,2,96,768]{3,2,1,0:T(8,128)(2,1)S(1)}, u32[]{:S(2)}, u32[]{:S(2)}) collective-permute-start(bf16[2,2,96,768]{3,2,1,0:T(8,128)(2,1)S(1)} %slice_bitcast_fusion.12), channel_id=1, source_target_pairs={{0,4},{1,5},{2,6},{3,7},{4,0},{5,1},{6,2},{7,3},{8,12},{9,13},{10,... | collective-permute-start | bytes 1769480 | tf_op jit(solution)/shard_map/ppermute | solution.py:75
  347.8 31.3 %collective-permute-start.69 = (bf16[2,96,768]{2,1,0:T(8,128)(2,1)S(1)}, bf16[2,96,768]{2,1,0:T(8,128)(2,1)S(1)}, u32[]{:S(2)}, u32[]{:S(2)}) collective-permute-start(bf16[2,96,768]{2,1,0:T(8,128)(2,1)S(1)} %slice_bitcast_fusion.18), channel_id=1, source_target_pairs={{0,4},{1,5},{2,6},{3,7},{4,0},{5,1},{6,2},{7,3},{8,12},{9,13},{10,... | collective-permute-start | bytes 884744 | tf_op jit(solution)/shard_map/ppermute | solution.py:75
  360.5 34.0 %collective-permute-start.61 = (bf16[2,96,768]{2,1,0:T(8,128)(2,1)S(1)}, bf16[2,96,768]{2,1,0:T(8,128)(2,1)S(1)}, u32[]{:S(2)}, u32[]{:S(2)}) collective-permute-start(bf16[2,96,768]{2,1,0:T(8,128)(2,1)S(1)} %slice_bitcast_fusion.22), channel_id=1, source_target_pairs={{0,4},{1,5},{2,6},{3,7},{4,0},{5,1},{6,2},{7,3},{8,12},{9,13},{10,... | collective-permute-start | bytes 884744 | tf_op jit(solution)/shard_map/ppermute | solution.py:75
  380.3 38.0 %collective-permute-start.70 = (bf16[96,768]{1,0:T(8,128)(2,1)S(1)}, bf16[96,768]{1,0:T(8,128)(2,1)S(1)}, u32[]{:S(2)}, u32[]{:S(2)}) collective-permute-start(bf16[96,768]{1,0:T(8,128)(2,1)S(1)} %slice_bitcast_fusion.30), channel_id=1, source_target_pairs={{0,8},{1,9},{2,10},{3,11},{4,12},{5,13},{6,14},{7,15},{8,16},{9,17... | collective-permute-start | bytes 442376 | tf_op jit(solution)/shard_map/ppermute | solution.py:75
  390.7 27.5 %collective-permute-start.73 = (bf16[96,768]{1,0:T(8,128)(2,1)S(1)}, bf16[96,768]{1,0:T(8,128)(2,1)S(1)}, u32[]{:S(2)}, u32[]{:S(2)}) collective-permute-start(bf16[96,768]{1,0:T(8,128)(2,1)S(1)} %get-tuple-element.186), channel_id=1, source_target_pairs={{0,16},{1,17},{2,18},{3,19},{4,20},{5,21},{6,22},{7,23},{8,24},{9,... | collective-permute-start | bytes 442376 | tf_op jit(solution)/shard_map/ppermute | solution.py:75
  (120 other events, 1511.5 us)

commit v2 on v1

v2 whole, which is shorter than its diff:
```python
from functools import partial
import math

import jax
import jax.numpy as jnp
from jax import lax
from jax.experimental import pallas as pl
from jax.experimental.pallas import tpu as pltpu
from jax.sharding import PartitionSpec as P

D = 768
HEADS = 12
HD = 64
FF = 3072
L = 512
PASS = 4
STEP = 10
ROWS_DEV = 8
MIB = 1 << 20
PART = 256
TAIL = 2 * D + FF


masked_value = -1e30
grid_weight = 4.0
norm_eps = 1e-12
beta_decay = 0.5
adam_eps = 1e-06
norm_guard = 1e-06
weight_decay = 0.01
rate_matrix = 1.0
rate_vector = 0.2


def passage_ids(lengths):
    starts = jnp.cumsum(lengths, axis=1) - lengths
    positions = jnp.arange(L, dtype=jnp.int32)
    return jnp.sum((positions[None, :, None] >= starts[:, None, :]).astype(jnp.int32), axis=2) - 1


AXES = ("dp", "mp")
GRID = (8, 4)


def links(move):
    pairs = []
    for z in range(4):
        for x in range(2):
            for y in range(2):
                for c in range(2):
                    tz, tx, ty, tc = move(z, x, y, c)
                    pairs.append(
                        ((z * 2 + x) * 4 + y * 2 + c, (tz % 4 * 2 + tx) * 4 + ty * 2 + tc)
                    )
    return pairs


CORE = links(lambda z, x, y, c: (z, x, y, 1 - c))
OVER_X = links(lambda z, x, y, c: (z, 1 - x, y, c))
OVER_Y = links(lambda z, x, y, c: (z, x, 1 - y, c))
OVER_XY = links(lambda z, x, y, c: (z, 1 - x, 1 - y, c))
UP_Z = [links(lambda z, x, y, c, s=s: (z + s, x, y, c)) for s in range(4)]


def after(value, *earlier):
    return lax.optimization_barrier((value, earlier))[0] if earlier else value


def send(value, pairs, *beside):
    return after(lax.ppermute(value, AXES, pairs), *beside)


def on_grid():
    return (lax.axis_size("dp"), lax.axis_size("mp")) == GRID


def place():
    dp_index = lax.axis_index("dp")
    mp_index = lax.axis_index("mp")
    return jnp.stack([dp_index // 2, dp_index % 2, mp_index // 2, mp_index % 2, mp_index])


ITEMS = (
    [(x, 0, z) for x in (0, 1) for z in (0, 1)]
    + [(0, y, z) for y in (0, 1) for z in (2, 3)]
    + [(x, 1, z) for x in (0, 1) for z in (0, 1)]
    + [(1, y, z) for y in (0, 1) for z in (2, 3)]
)


def gather_z(shard, *beside):
    return [shard] + [send(shard, UP_Z[s], *beside) for s in (1, 2, 3)]


def gather_near(parts, *beside):
    first, second = jnp.stack(parts[:2]), jnp.stack(parts[2:])
    return [
        jnp.concatenate([first, send(first, OVER_X, *beside)]),
        jnp.concatenate([second, send(second, OVER_Y, *beside)]),
    ]


def gather_far(near, *beside):
    return [send(near[0], OVER_Y, *beside), send(near[1], OVER_X, *beside)]


def gather_core(parts, *beside):
    return [send(part, CORE, *beside) for part in parts]


def gather_plain(shard):
    mp_size = lax.axis_size("mp")
    return lax.all_gather(shard, ("mp", "dp"), axis=0, tiled=True).reshape(mp_size, D, D)


def block_of(g, where):
    if not on_grid():
        return g
    return ((where[2] + g % 2) % 2) * 2 + (where[3] + g // 2) % 2


def scatter_plain(parts):
    whole = parts[0]
    return lax.psum_scatter(
        whole.reshape(-1, whole.shape[-1]), ("mp", "dp"), scatter_dimension=0, tiled=True
    )


class Summand:
    def __init__(self, blocks, dp_size):
        rows = D // dp_size
        self.groups = dp_size
        self.rows = rows
        self.blocks = blocks
        self.split = on_grid()
        if self.split:
            self.shapes = [jax.ShapeDtypeStruct((2, 2, 2, 2, rows, D), jnp.bfloat16)] * 2
        else:
            self.shapes = [jax.ShapeDtypeStruct((blocks, D, D), jnp.bfloat16)]

    def write(self, outs, value, g, where):
        if not self.split:
            outs[0][g] = value
            return
        core, y = g // 2, g % 2
        for index in range(self.groups):
            x = (index % 2 + where[1]) % 2
            z = (index // 2 + 4 - where[0]) % 4
            half = z // 2
            over_y = half == 0
            first, second = jnp.where(over_y, y, x), jnp.where(over_y, x, y)
            outs[core][half, first, second, z % 2] = value[
                index * self.rows : (index + 1) * self.rows
            ]


def share(value):
    if not on_grid():
        dp_size, mp_size = lax.axis_size("dp"), lax.axis_size("mp")
        whole = lax.all_gather(value, AXES, axis=0, tiled=True)
        own = lax.axis_index("dp") * mp_size + lax.axis_index("mp")
        return jnp.roll(whole, -own * value.shape[0], axis=0)
    value = jnp.concatenate([value, send(value, CORE)])
    value = jnp.concatenate([value] + [send(value, pairs) for pairs in (OVER_X, OVER_Y, OVER_XY)])
    return jnp.concatenate([value] + [send(value, UP_Z[s]) for s in (1, 2, 3)])


def shared_ids(own_rows):
    dp_size, mp_size = lax.axis_size("dp"), lax.axis_size("mp")
    dp_index, mp_index = lax.axis_index("dp"), lax.axis_index("mp")
    count = dp_size * mp_size * own_rows
    n = jnp.arange(count, dtype=jnp.int32)
    if not on_grid():
        return (n + (dp_index * mp_size + mp_index) * own_rows) % count
    item = n // own_rows
    core, side, up = item % 2, item // 2 % 4, item // 8
    z, x = (dp_index // 2 + 4 - up) % 4, (dp_index + side) % 2
    y, c = (mp_index // 2 + side // 2) % 2, (mp_index + core) % 2
    return ((z * 2 + x) * mp_size + y * 2 + c) * own_rows + n % own_rows


def total(value):
    if not on_grid():
        return lax.psum(value, AXES)
    value = value + send(value, CORE)
    value = value + sum(send(value, pairs) for pairs in (OVER_X, OVER_Y, OVER_XY))
    return value + sum(send(value, UP_Z[s]) for s in (1, 2, 3))


LOW = jnp.bfloat16
WIDE = jnp.float32
B1, BO, B2, G1, C1, G2, C2 = 2 * D, TAIL, TAIL + D, TAIL + 2 * D, TAIL + 3 * D, TAIL + 4 * D, TAIL + 5 * D
VEC = 8 * D + FF


def dot(left, right, over=(1, 0)):
    return lax.dot_general(
        left, right, (((over[0],), (over[1],)), ((), ())), preferred_element_type=WIDE
    )


def call(kernel, name, where, operands, outs, scratch=(), limit=24, wait_for=()):
    count = len(operands)
    many = len(outs)

    def body(where, *refs):
        results = refs[count + len(wait_for) :]
        results[many][...] = jnp.zeros((8, 128), WIDE)
        kernel(where, *refs[:count], *results[:many], *results[many + 1 :])

    def spec(operand):
        integers = operand.dtype == jnp.int32 and operand.ndim == 1
        return pl.BlockSpec(memory_space=pltpu.SMEM if integers else pltpu.VMEM)

    return pl.pallas_call(
        body,
        in_specs=[pl.BlockSpec(memory_space=pltpu.SMEM)]
        + [spec(operand) for operand in operands]
        + [pl.BlockSpec(memory_space=pl.ANY)] * len(wait_for),
        out_specs=[pl.BlockSpec(memory_space=pltpu.VMEM)] * (many + 1),
        out_shape=list(outs) + [array(WIDE, 8, 128)],
        scratch_shapes=list(scratch),
        compiler_params=pltpu.CompilerParams(vmem_limit_bytes=limit * MIB),
        cost_estimate=pl.CostEstimate(flops=3 * 10**10, bytes_accessed=MIB, transcendentals=0),
        name=name,
    )(where, *operands, *wait_for)


def array(dtype, *shape):
    return jax.ShapeDtypeStruct(shape, dtype)


def normalize(value):
    center = jnp.mean(value, axis=1, keepdims=True)
    offsets = value - center
    inverse = lax.rsqrt(jnp.mean(offsets * offsets, axis=1, keepdims=True) + norm_eps)
    return offsets * inverse, inverse


def norm_back(grad, unit, inverse, gain):
    scaled = grad * gain
    return inverse * (
        scaled
        - jnp.mean(scaled, axis=1, keepdims=True)
        - unit * jnp.mean(scaled * unit, axis=1, keepdims=True)
    )


def column_sum(value):
    return jnp.sum(value, axis=0, keepdims=True)


def settle_kernel(where, *refs):
    pieces, out = refs[:8], refs[8]
    for core in range(2):
        for item, (x, y, z) in enumerate(ITEMS):
            block = (where[2] + y) % 2 * 2 + (where[3] + core) % 2
            row = (where[0] + 4 - z) % 4 * 2 + (where[1] + x) % 2
            out[block, row] = pieces[core * 4 + item // 4][item % 4]


def settle(where, pieces):
    rows = pieces[0].shape[1]
    whole = call(settle_kernel, "settle", where, pieces, [array(LOW, 4, 8, rows, D)], limit=8)[0]
    return whole.reshape(4, D, D)


def add_kernel(plan, where, *refs):
    count = max(max(pair[0], pair[2]) for pair in plan) + 1
    for out, (left, left_at, right, right_at) in zip(refs[count:], plan):
        out[...] = (
            refs[left][left_at].astype(WIDE) + refs[right][right_at].astype(WIDE)
        ).astype(LOW)


def add(where, operands, plan):
    outs = []
    for left, left_at, _, _ in plan:
        outs.append(array(LOW, *operands[left].shape[len(left_at) :]))
    return call(partial(add_kernel, plan), "add", where, operands, outs, limit=8)


def scatter_core(where, parts, *beside):
    arrived = send(parts[1], CORE, *beside)
    plan = [(0, (half, near), 1, (half, near)) for half in (0, 1) for near in (0, 1)]
    return add(where, [parts[0], arrived], plan)


def scatter_far(where, sums, *beside):
    arrived = [send(sums[1], OVER_Y, *beside), send(sums[3], OVER_X, *beside)]
    plan = [(half, (far,), half + 2, (far,)) for half in (0, 1) for far in (0, 1)]
    return add(where, [sums[0], sums[2], *arrived], plan)


def scatter_near(where, sums, *beside):
    arrived = [send(sums[1], OVER_X, *beside), send(sums[3], OVER_Y, *beside)]
    plan = [(half, (z,), half + 2, (z,)) for half in (0, 1) for z in (0, 1)]
    return add(where, [sums[0], sums[2], *arrived], plan)


def scatter_z(sums, *beside):
    return [sums[0]] + [send(sums[s], UP_Z[s], *beside) for s in (1, 2, 3)]


def attend_kernel(blocks, where, x_ref, w_ref, bias_ref, vec_ref, seg_ref, *refs):
    q_out, k_out, v_out, context_out, unit_out, inverse_out, low_out, sum_ref = refs
    heads = HEADS // blocks
    width = HD * heads
    x = x_ref[...]
    lanes = lax.broadcasted_iota(jnp.int32, (L, 2 * HD), 1)
    passage = jnp.broadcast_to(seg_ref[...], (L, 2 * HD)) + HD
    is_passage = (lanes >= HD) & (lanes < HD + PASS)
    q_tail = jnp.where(is_passage & (lanes != passage), masked_value, 0.0)
    k_tail = (lanes == passage) | ((lanes >= HD + PASS) & (lanes < HD + PASS + 3))
    k_tail = jnp.where(k_tail, 1.0, 0.0).astype(LOW)
    k_scale = jnp.where(lanes < HD, 1.0, 0.0).astype(LOW)
    q_scale = jnp.where(lanes < HD, HD ** (-0.5), 0.0).astype(LOW)
    q_tail = q_tail.astype(LOW)
    sum_ref[...] = x.astype(WIDE) + vec_ref[:, BO : BO + D]

    def block(m, carry):
        projected = (dot(x, w_ref[m]) + bias_ref[m]).astype(LOW)
        parts = []
        for h in range(heads):
            at = width + h * HD
            query = projected[:, at : at + 2 * HD] * q_scale + q_tail
            keys = projected[:, at + width : at + width + 2 * HD] * k_scale + k_tail
            value = projected[:, at + 2 * width : at + 2 * width + HD]
            scores = dot(keys, query, (1, 1))
            highest = jnp.max(scores, axis=0, keepdims=True)
            weights = jnp.exp(scores - highest)
            totals = jnp.sum(weights, axis=0, keepdims=True)
            mixed = dot(value.T, weights.astype(LOW)) * (1.0 / totals)
            left = -(highest + jnp.log(totals))
            high = left.astype(LOW).astype(WIDE)
            middle = (left - high).astype(LOW).astype(WIDE)
            rows = lax.broadcasted_iota(jnp.int32, (HD, L), 0)
            split = jnp.where(rows == PASS, high, 0.0)
            split = jnp.where(rows == PASS + 1, middle, split)
            split = jnp.where(rows == PASS + 2, left - high - middle, split)
            turned = jnp.concatenate([mixed, split], axis=0).T.astype(LOW)
            parts.append(turned[:, :HD])
            q_out[m * heads + h] = jnp.where(lanes < HD, query, query + turned)
            k_out[m * heads + h] = keys
            v_out[m * heads + h] = value
        context = jnp.concatenate(parts, axis=1)
        context_out[m] = context
        sum_ref[...] += dot(context, w_ref[m, :, :width], (1, 1))
        return carry

    lax.fori_loop(0, blocks, block, 0)
    unit, inverse = normalize(sum_ref[...])
    unit_out[...] = unit
    inverse_out[...] = inverse
    low_out[...] = (unit * vec_ref[:, G1 : G1 + D] + vec_ref[:, C1 : C1 + D]).astype(LOW)


def attend(where, inputs, weight, bias, vectors, segments, wait_for=()):
    blocks = bias.shape[0]
    return call(
        partial(attend_kernel, blocks),
        "attend",
        where,
        [inputs, weight, bias, vectors, segments],
        [
            array(LOW, HEADS, L, 2 * HD),
            array(LOW, HEADS, L, 2 * HD),
            array(LOW, HEADS, L, HD),
            array(LOW, blocks, L, D // blocks),
            array(WIDE, L, D),
            array(WIDE, L, 1),
            array(LOW, L, D),
        ],
        [pltpu.VMEM((L, D), WIDE)],
        wait_for=wait_for,
    )


def widen_kernel(rows, where, *refs):
    lows, (w_ref, bias_ref, active_out, slope_out) = refs[:rows], refs[rows:]

    def block(m, carry):
        for row in range(rows):
            hidden = dot(lows[row][...], w_ref[m]) + bias_ref[m]
            half = 0.5 * (1.0 + lax.erf(hidden * math.sqrt(0.5)))
            active_out[m, row * L : (row + 1) * L] = (hidden * half).astype(LOW)
            density = jnp.exp(-0.5 * hidden * hidden) * (1.0 / math.sqrt(2.0 * math.pi))
            slope_out[m, row * L : (row + 1) * L] = (half + hidden * density).astype(LOW)
        return carry

    lax.fori_loop(0, w_ref.shape[0], block, 0)


def widen(where, lows, weight, bias, wait_for=()):
    blocks = bias.shape[0]
    rows = len(lows)
    return call(
        partial(widen_kernel, rows),
        "widen",
        where,
        [*lows, weight, bias],
        [array(LOW, blocks, rows * L, D)] * 2,
        wait_for=wait_for,
    )


def narrow_kernel(rows, where, active_ref, w_ref, vec_ref, starts_ref, *refs):
    units, (out, unit_out, inverse_out, cls_out, y_ref) = refs[:rows], refs[rows:]
    for row in range(rows):
        at = slice(row * L, (row + 1) * L)
        y_ref[at] = units[row][...] * vec_ref[:, G1 : G1 + D] + (
            vec_ref[:, C1 : C1 + D] + vec_ref[:, B2 : B2 + D]
        )

        def block(m, carry):
            y_ref[at] += dot(active_ref[m, at], w_ref[m], (1, 1))
            return carry

        lax.fori_loop(0, w_ref.shape[0], block, 0)
        unit, inverse = normalize(y_ref[at])
        unit_out[at] = unit
        inverse_out[at] = inverse
        output = unit * vec_ref[:, G2 : G2 + D] + vec_ref[:, C2 : C2 + D]
        out[at] = output.astype(LOW)
        y_ref[at] = output
    for p in range(cls_out.shape[0]):
        cls_out[p : p + 1, :] = y_ref[pl.ds(starts_ref[p], 1), :]


def narrow(where, active, weight, vectors, starts, units):
    tokens = active.shape[1]
    few = starts.shape[0]
    return call(
        partial(narrow_kernel, len(units)),
        "narrow",
        where,
        [active, weight, vectors, starts, *units],
        [
            array(LOW, tokens, D),
            array(WIDE, tokens, D),
            array(WIDE, tokens, 1),
            array(WIDE, few, D),
        ],
        [pltpu.VMEM((tokens, D), WIDE)],
    )


def contrast_kernel(
    where, cot_ref, unit_ref, inverse_ref, vec_ref, starts_ref,
    own_ref, all_ref, ids_ref, ids_own_ref, partners_own_ref,
    grad_out, low_out, bias_out, gain_out, shift_out, y_ref,
):
    scale = 2.0 / math.sqrt(D)
    everyone = all_ref[...]
    own = own_ref[...].astype(LOW)
    count = everyone.shape[0]
    scores = dot(everyone, everyone, (1, 1)) * scale
    diagonal = lax.broadcasted_iota(jnp.int32, (count, count), 0) == lax.broadcasted_iota(
        jnp.int32, (count, count), 1
    )
    scores = jnp.where(diagonal, masked_value, scores)
    highest = jnp.max(scores, axis=0, keepdims=True)
    log_all = highest + jnp.log(jnp.sum(jnp.exp(scores - highest), axis=0, keepdims=True))
    here = dot(own, everyone, (1, 1)) * scale
    ids = ids_ref[...]
    here = jnp.where(ids_own_ref[...] == ids, masked_value, here)
    top = jnp.max(here, axis=1, keepdims=True)
    log_own = top + jnp.log(jnp.sum(jnp.exp(here - top), axis=1, keepdims=True))
    pair = (partners_own_ref[...] == ids).astype(WIDE)
    out_grad = grid_weight * (jnp.exp(here - log_own) - pair)
    in_grad = grid_weight * (jnp.exp(here - log_all) - pair)
    cls_grad = scale * (dot(out_grad.astype(LOW), everyone) + dot(in_grad.astype(LOW), everyone))
    y_ref[...] = cot_ref[...].astype(WIDE)
    for p in range(cls_grad.shape[0]):
        y_ref[pl.ds(starts_ref[p], 1), :] += cls_grad[p : p + 1]
    for ref in (bias_out, gain_out, shift_out):
        ref[...] = jnp.zeros_like(ref)
    for part in range(y_ref.shape[0] // PART):
        at = slice(part * PART, (part + 1) * PART)
        grad = y_ref[at]
        unit = unit_ref[at]
        gain_out[...] += column_sum(grad * unit)
        shift_out[...] += column_sum(grad)
        back = norm_back(grad, unit, inverse_ref[at], vec_ref[:, G2 : G2 + D])
        grad_out[at] = back
        low = back.astype(LOW)
        low_out[at] = low
        bias_out[...] += column_sum(low.astype(WIDE))


def contrast(where, cotangent, unit, inverse, vectors, starts, own, everyone, ids, ids_own, partners_own):
    tokens = cotangent.shape[0]
    return call(
        contrast_kernel,
        "contrast",
        where,
        [
            cotangent, unit, inverse, vectors, starts, own, everyone, ids, ids_own, partners_own,
        ],
        [
            array(WIDE, tokens, D),
            array(LOW, tokens, D),
            array(WIDE, 1, D),
            array(WIDE, 1, D),
            array(WIDE, 1, D),
        ],
        [pltpu.VMEM((tokens, D), WIDE)],
    )


def down_grad_kernel(summand, where, grad_ref, active_ref, *refs):
    outs, turned = refs[:-1], refs[-1]
    turned[...] = grad_ref[...].T
    for g in range(summand.blocks):
        value = dot(turned[...], active_ref[block_of(g, where)]).astype(LOW)
        summand.write(outs, value, g, where)


def grad_of_down(where, grad_low, active, summand):
    tokens = active.shape[1]
    return call(
        partial(down_grad_kernel, summand),
        "grad_of_down",
        where,
        [grad_low, active],
        summand.shapes,
        [pltpu.VMEM((D, tokens), LOW)],
    )


def up_grad_kernel(summand, rows, where, grad_ref, w_ref, slope_ref, *refs):
    lows, (grad_out, bias_out), refs = refs[:rows], refs[rows : rows + 2], refs[rows + 2 :]
    outs, turned = refs[:-1], refs[-1]
    for row in range(rows):
        turned[:, row * L : (row + 1) * L] = lows[row][...].T
    for g in range(summand.blocks):
        m = block_of(g, where)
        bias = jnp.zeros((1, D), WIDE)
        for row in range(rows):
            at = slice(row * L, (row + 1) * L)
            grad = dot(grad_ref[at], w_ref[m]) * slope_ref[m, at].astype(WIDE)
            grad = grad.astype(LOW)
            grad_out[m, at] = grad
            bias += column_sum(grad.astype(WIDE))
        bias_out[m] = bias
        summand.write(outs, dot(turned[...], grad_out[m]).astype(LOW), g, where)


def grad_of_up(where, grad_low, weight, slope, lows, summand, wait_for=()):
    blocks, tokens, _ = slope.shape
    return call(
        partial(up_grad_kernel, summand, len(lows)),
        "grad_of_up",
        where,
        [grad_low, weight, slope, *lows],
        [array(LOW, blocks, tokens, D), array(WIDE, blocks, 1, D)] + summand.shapes,
        [pltpu.VMEM((D, tokens), LOW)],
        wait_for=wait_for,
    )


def middle_kernel(blocks, rows, where, hidden_ref, up_ref, sum_ref, vec_ref, w_ref, *refs):
    units, inverses, refs = refs[:rows], refs[rows : 2 * rows], refs[2 * rows :]
    grad_out, low_out, bias_out, gain_out, shift_out, context_out = refs
    width = D // blocks
    for ref in (bias_out, gain_out, shift_out):
        ref[...] = jnp.zeros_like(ref)
    for row in range(rows):
        at = slice(row * L, (row + 1) * L)
        grad_out[at] = sum_ref[at]

        def block(m, carry):
            grad_out[at] += dot(hidden_ref[m, at], up_ref[m], (1, 1))
            return carry

        lax.fori_loop(0, blocks, block, 0)
        for part in range(L // PART):
            inner = slice(part * PART, (part + 1) * PART)
            outer = slice(row * L + part * PART, row * L + (part + 1) * PART)
            grad = grad_out[outer]
            unit = units[row][inner]
            gain_out[...] += column_sum(grad * unit)
            shift_out[...] += column_sum(grad)
            back = norm_back(grad, unit, inverses[row][inner], vec_ref[:, G1 : G1 + D])
            grad_out[outer] = back
            low = back.astype(LOW)
            low_out[outer] = low
            bias_out[...] += column_sum(low.astype(WIDE))
        for m in range(blocks):
            context_out[row * blocks + m] = dot(low_out[at], w_ref[m, :, :width]).astype(LOW)


def middle(where, hidden_grad, up, sum_grad, units, inverses, vectors, weight, wait_for=()):
    blocks, tokens, _ = hidden_grad.shape
    rows = len(units)
    return call(
        partial(middle_kernel, blocks, rows),
        "middle",
        where,
        [hidden_grad, up, sum_grad, vectors, weight, *units, *inverses],
        [
            array(WIDE, tokens, D),
            array(LOW, tokens, D),
            array(WIDE, 1, D),
            array(WIDE, 1, D),
            array(WIDE, 1, D),
            array(LOW, rows * blocks, L, D // blocks),
        ],
        wait_for=wait_for,
    )


def attend_back_kernel(blocks, row, where, q_ref, k_ref, v_ref, grad_ref, out):
    heads = HEADS // blocks
    width = HD * heads

    def block(m, carry):
        out[m, :, :width] = jnp.zeros((L, width), LOW)
        for h in range(heads):
            queries, keys, value = q_ref[m * heads + h], k_ref[m * heads + h], v_ref[m * heads + h]
            grad = grad_ref[row * blocks + m, :, h * HD : (h + 1) * HD]
            weights = jnp.exp(dot(keys, queries, (1, 1)))
            weight_grad = dot(value, grad, (1, 1))
            middle_sum = jnp.sum(weight_grad * weights, axis=0, keepdims=True)
            score_grad = (weights * (weight_grad - middle_sum)).astype(LOW)
            at = width + h * HD
            query_grad = (dot(keys.T, score_grad)[:HD] * HD ** (-0.5)).T
            out[m, :, at : at + HD] = query_grad.astype(LOW)
            out[m, :, at + width : at + width + HD] = dot(score_grad, queries)[:, :HD].astype(LOW)
            out[m, :, at + 2 * width : at + 2 * width + HD] = dot(
                weights.astype(LOW), grad
            ).astype(LOW)
        return carry

    lax.fori_loop(0, blocks, block, 0)


def attend_back(where, row, blocks, queries, keys, values, context_grad, wait_for=()):
    return call(
        partial(attend_back_kernel, blocks, row),
        "attend_back",
        where,
        [queries, keys, values, context_grad],
        [array(LOW, blocks, L, D)],
        wait_for=wait_for,
    )


def attention_grad_kernel(summand, rows, where, x_ref, low_ref, *refs):
    grads, contexts, refs = refs[:rows], refs[rows : 2 * rows], refs[2 * rows :]
    bias_out, outs, (x_turned, low_turned) = refs[0], refs[1:-2], refs[-2:]
    x_turned[...] = x_ref[...].T
    low_turned[...] = low_ref[...].T
    width = contexts[0].shape[2]
    for g in range(summand.blocks):
        m = block_of(g, where)
        bias = jnp.zeros((1, D), WIDE)
        value = jnp.zeros((D, D), WIDE)
        own = jnp.zeros((D, width), WIDE)
        for row in range(rows):
            at = slice(row * L, (row + 1) * L)
            grad = grads[row][m]
            bias += column_sum(grad.astype(WIDE))
            value += dot(x_turned[:, at], grad)
            own += dot(low_turned[:, at], contexts[row][m])
        bias_out[m] = bias
        value = jnp.concatenate([own, value[:, width:]], axis=1).astype(LOW)
        summand.write(outs, value, g, where)


def grad_of_attention(where, inputs, grad_low, grads, contexts, summand, wait_for=()):
    tokens = inputs.shape[0]
    return call(
        partial(attention_grad_kernel, summand, len(grads)),
        "grad_of_attention",
        where,
        [inputs, grad_low, *grads, *contexts],
        [array(WIDE, summand.blocks, 1, D)] + summand.shapes,
        [pltpu.VMEM((D, tokens), LOW)] * 2,
        wait_for=wait_for,
    )


def input_grad_kernel(rows, where, w_ref, first_ref, *refs):
    grads, out = refs[:rows], refs[rows]
    for row in range(rows):
        at = slice(row * L, (row + 1) * L)
        out[at] = first_ref[at]

        def block(m, carry):
            out[at] += dot(grads[row][m], w_ref[m], (1, 1))
            return carry

        lax.fori_loop(0, w_ref.shape[0], block, 0)


def grad_of_input(where, grads, weight, first_grad, wait_for=()):
    return call(
        partial(input_grad_kernel, len(grads)),
        "grad_of_input",
        where,
        [weight, first_grad, *grads],
        [array(WIDE, *first_grad.shape)],
        wait_for=wait_for,
    )


def pack_kernel(where, bias_ref, up_ref, *refs):
    out = refs[-1]
    blocks = bias_ref.shape[0]
    width = D // blocks
    rows = [bias_ref[m] for m in range(blocks)]
    out[:, :D] = jnp.concatenate([row[:, width : 2 * width] for row in rows], axis=1)
    out[:, D : 2 * D] = jnp.concatenate([row[:, 3 * width :] for row in rows], axis=1)
    units = FF // blocks
    for m in range(blocks):
        out[:, 2 * D + m * units : 2 * D + (m + 1) * units] = up_ref[m]
    for i, ref in enumerate(refs[:-1]):
        out[:, TAIL + i * D : TAIL + (i + 1) * D] = ref[...]


def pack(where, bias_grad, up_bias_grad, *others):
    return call(
        pack_kernel, "pack", where, [bias_grad, up_bias_grad, *others], [array(WIDE, 1, VEC)], limit=8
    )[0]


def ratio_of(grad, first, second):
    moment = beta_decay * first + (1.0 - beta_decay) * grad
    second_new = beta_decay * second + (1.0 - beta_decay) * grad * grad
    ratio = (
        moment
        / (1.0 - beta_decay**STEP)
        / (jnp.sqrt(second_new / (1.0 - beta_decay**STEP)) + adam_eps)
    )
    return second_new, ratio


def squares(value):
    return jnp.sum(jnp.sum(value * value, axis=0, keepdims=True), axis=1, keepdims=True)


def adapt_kernel(cut, parts, where, *refs):
    total_sum = refs[0][...].astype(WIDE)
    for ref in refs[1:parts]:
        total_sum += ref[...].astype(WIDE)
    refs = refs[parts:]
    count = len(cut)
    firsts, seconds, weights = refs[:count], refs[count : 2 * count], refs[2 * count : 3 * count]
    outs = refs[3 * count :]
    lines = []
    for i, pick in enumerate(cut):
        for part, grad in pick(total_sum):
            def at(ref):
                return ref if part is None else ref.at[part]

            second_new, ratio = ratio_of(grad, at(firsts[i])[...], at(seconds[i])[...])
            weight = at(weights[i])[...]
            update = ratio + weight_decay * weight
            at(outs[3 * i])[...] = grad
            at(outs[3 * i + 1])[...] = second_new
            at(outs[3 * i + 2])[...] = update
            lines.append((squares(weight), squares(update)))
    lanes = lax.broadcasted_iota(jnp.int32, (1, 128), 1)
    held = jnp.zeros((1, 128), WIDE)
    for i, (weight_square, update_square) in enumerate(lines):
        held = jnp.where(lanes == 2 * i, weight_square, held)
        held = jnp.where(lanes == 2 * i + 1, update_square, held)
    outs[-1][...] = held


def adapt(name, where, parts, cut, firsts, seconds, weights):
    outs = [array(WIDE, *w.shape) for w in weights for _ in range(3)] + [array(WIDE, 1, 128)]
    operands = [*parts, *firsts, *seconds, *weights]
    return call(
        partial(adapt_kernel, cut, len(parts)),
        name,
        where,
        operands,
        outs,
    )[:-1]


def renew_kernel(counts, where, sums_ref, grad_ref, first_ref, second_ref, vec_ref, *refs):
    many = len(counts)
    weights, updates, outs = refs[:many], refs[many : 2 * many], refs[2 * many :]
    norms = jnp.sqrt(sums_ref[...])
    outs[-1][...] = norms
    slot = 0
    for i, count in enumerate(counts):
        for part in range(count):
            trust = norms[:, 2 * slot : 2 * slot + 1] / (
                norms[:, 2 * slot + 1 : 2 * slot + 2] + norm_guard
            )
            slot += 1

            def at(ref):
                return ref if count == 1 else ref.at[part]

            new = at(weights[i])[...] - rate_matrix * trust * at(updates[i])[...]
            at(outs[2 * i])[...] = new
            at(outs[2 * i + 1])[...] = new.astype(LOW)
    second_new, ratio = ratio_of(grad_ref[...], first_ref[...], second_ref[...])
    outs[-3][...] = second_new
    outs[-2][...] = vec_ref[...] - rate_vector * ratio


def renew(where, sums, vector_grad, vector_first, vector_second, vectors, weights, updates):
    counts = [3 if w.ndim == 3 else 1 for w in weights]
    outs = [array(dtype, *w.shape) for w in weights for dtype in (WIDE, LOW)]
    outs += [array(WIDE, 1, VEC), array(WIDE, 1, VEC), array(WIDE, 1, 128)]
    operands = [sums, vector_grad, vector_first, vector_second, vectors, *weights, *updates]
    return call(
        partial(renew_kernel, counts),
        "renew",
        where,
        operands,
        outs,
    )[:-1]


def shards(
    block_input,
    cotangent,
    lengths,
    partner,
    qkv_weight,
    out_weight,
    up_weight,
    down_weight,
    qkv_first,
    out_first,
    up_first,
    down_first,
    qkv_second,
    out_second,
    up_second,
    down_second,
    vectors,
    vector_first,
    vector_second,
):
    mp_size = lax.axis_size("mp")
    dp_size = lax.axis_size("dp")
    mp_index = lax.axis_index("mp")
    dp_index = lax.axis_index("dp")
    tokens = cotangent.shape[0]
    rows = tokens // L
    own_rows = rows * PASS
    width = D // mp_size
    where = place()
    weight_shard = jnp.concatenate(
        [out_weight.T, qkv_weight[0], qkv_weight[1], qkv_weight[2]], axis=1
    ).astype(LOW)
    up_shard = up_weight.astype(LOW)
    down_shard = down_weight.T.astype(LOW)
    local_lengths = lax.dynamic_slice_in_dim(lengths, mp_index * rows, rows, 0)
    inputs = lax.dynamic_slice_in_dim(block_input, mp_index * tokens, tokens, 0)
    segments = passage_ids(local_lengths).reshape(tokens, 1)
    starts = jnp.cumsum(local_lengths, axis=1) - local_lengths
    starts = (starts + L * jnp.arange(rows, dtype=jnp.int32)[:, None]).reshape(own_rows)
    partner_own = lax.dynamic_slice_in_dim(partner, mp_index * own_rows, own_rows, 0)
    ids_own = (dp_index * mp_size + mp_index) * own_rows + jnp.arange(own_rows, dtype=jnp.int32)
    ids_all = shared_ids(own_rows)
    vec = vectors.reshape(1, VEC)
    none = jnp.zeros((mp_size, width), WIDE)
    bias = jnp.concatenate(
        [none, vectors[:D].reshape(mp_size, width), none, vectors[D : 2 * D].reshape(mp_size, width)],
        axis=1,
    ).reshape(mp_size, 1, D)
    bias_up = vectors[2 * D : TAIL].reshape(mp_size, 1, D)

    summand = Summand(mp_size, dp_size)

    def attend_row(row, weight, *wait_for):
        at = slice(row * L, (row + 1) * L)
        return attend(where, inputs[at], weight, bias, vec, segments[at], wait_for=wait_for)

    if on_grid():
        weight_z = gather_z(weight_shard)
        weight_near = gather_near(weight_z)
        up_z = gather_z(after(up_shard, *weight_z))
        weight_far = gather_far(weight_near)
        weight_parts = weight_near + weight_far
        weight = settle(where, weight_parts + gather_core(weight_parts))
        up_z = after(up_z, *weight_far)
        kept = [attend_row(0, weight, *up_z)]
        up_near = gather_near(up_z, kept[0][-1])
        down_z = gather_z(after(down_shard, *up_z), kept[0][-1])
        kept.append(attend_row(1, weight, *up_near, *down_z))
        up_far = gather_far(up_near, kept[1][-1])
        up_parts = up_near + up_far
        up = settle(where, up_parts + gather_core(up_parts))
        down_near = gather_near(down_z, kept[1][-1])
    else:
        weight = gather_plain(weight_shard)
        up = gather_plain(up_shard)
        down_near = []
        kept = [attend_row(row, weight) for row in range(rows)]
    queries, keys, values, contexts, units_first, inverses_first, lows, _ = zip(*kept)
    active, slope, widened = widen(where, lows, up, bias_up, wait_for=down_near)
    if on_grid():
        down_far = gather_far(after(down_near, *up_far), widened)
        down_parts = down_near + down_far
        down = settle(where, down_parts + gather_core(down_near, widened) + gather_core(down_far))
    else:
        down = gather_plain(down_shard)
    block_output, unit_second, inverse_second, cls_own, _ = narrow(
        where, active, down, vec, starts, units_first
    )
    cls_all = share(cls_own.astype(LOW))
    sum_grad, branch_low, down_bias_grad, gain_second_grad, shift_second_grad, _ = contrast(
        where, cotangent, unit_second, inverse_second, vec, starts, cls_own, cls_all,
        ids_all[None, :], ids_own[:, None], partner_own[:, None],
    )
    *down_part, ended = grad_of_down(where, branch_low, active, summand)
    hidden_grad, up_bias_grad, *up_part, _ = grad_of_up(
        where, branch_low, down, slope, lows, summand, wait_for=(ended,)
    )
    if on_grid():
        *down_sum, added = scatter_core(where, down_part)
    (
        first_grad, attended_low, out_bias_grad, gain_first_grad, shift_first_grad, context_grad, _,
    ) = middle(
        where, hidden_grad, up, sum_grad, units_first, inverses_first, vec, weight,
        wait_for=(added,) if on_grid() else (),
    )

    def back_row(row, *wait_for):
        return attend_back(
            where, row, mp_size, queries[row], keys[row], values[row], context_grad, wait_for=wait_for
        )

    if on_grid():
        *down_sum, down_added = scatter_far(where, down_sum)
        *up_sum, up_added = scatter_core(where, up_part)
        first_row, ended = back_row(0, down_added, up_added)
        *down_sum, down_added = scatter_near(where, down_sum, ended)
        second_row, ended = back_row(1, down_added)
        *up_sum, up_added = scatter_far(where, up_sum, ended)
        grads = [first_row, second_row]
        ties = (up_added,)
    else:
        grads = [back_row(row)[0] for row in range(rows)]
        ties = ()
    bias_grad, *attention_part, ended = grad_of_attention(
        where, inputs, attended_low, grads, contexts, summand, wait_for=ties
    )
    if on_grid():
        down_parts = scatter_z(down_sum, ended)
        *up_sum, up_added = scatter_near(where, up_sum, ended)
        *attention_sum, added = scatter_core(where, attention_part)
        input_grad, ended = grad_of_input(
            where, grads, weight, first_grad, wait_for=(added, up_added)
        )
        up_parts = scatter_z(up_sum, ended)
        *attention_sum, _ = scatter_far(where, attention_sum, ended)
        *attention_sum, _ = scatter_near(where, attention_sum)
        attention_parts = scatter_z(attention_sum)
    else:
        down_parts = [scatter_plain(down_part)]
        up_parts = [scatter_plain(up_part)]
        attention_parts = [scatter_plain(attention_part)]
        input_grad, _ = grad_of_input(where, grads, weight, first_grad)
    vector_local = pack(
        where,
        bias_grad,
        up_bias_grad,
        out_bias_grad,
        down_bias_grad,
        gain_first_grad,
        shift_first_grad,
        gain_second_grad,
        shift_second_grad,
    )
    down_grad, down_second_new, down_update, down_squares = adapt(
        "adapt_down", where, down_parts, [lambda g: [(None, g.T)]],
        [down_first], [down_second], [down_weight],
    )
    up_grad, up_second_new, up_update, up_squares = adapt(
        "adapt_up", where, up_parts, [lambda g: [(None, g)]], [up_first], [up_second], [up_weight]
    )
    (
        qkv_grad, qkv_second_new, qkv_update,
        out_grad, out_second_new, out_update, attention_squares,
    ) = adapt(
        "adapt_attention",
        where,
        attention_parts,
        [
            lambda g: [(i, g[:, (i + 1) * width : (i + 2) * width]) for i in range(3)],
            lambda g: [(None, g[:, :width].T)],
        ],
        [qkv_first, out_first],
        [qkv_second, out_second],
        [qkv_weight, out_weight],
    )
    summed = total(
        jnp.concatenate(
            [
                vector_local,
                attention_squares[:, :8],
                up_squares[:, :2],
                down_squares[:, :2],
                jnp.zeros((1, 116), WIDE),
            ],
            axis=1,
        )
    )
    vector_grad, sums = summed[:, :VEC], summed[:, VEC:]
    weights = [qkv_weight, out_weight, up_weight, down_weight]
    updates = [qkv_update, out_update, up_update, down_update]
    (
        qkv_new, qkv_copy, out_new, out_copy, up_new, up_copy, down_new, down_copy,
        vector_second_new, vector_new, norms,
    ) = renew(
        where, sums, vector_grad, vector_first.reshape(1, VEC), vector_second.reshape(1, VEC), vec,
        weights, updates,
    )
    return (
        block_output,
        input_grad,
        qkv_grad,
        out_grad,
        up_grad,
        down_grad,
        qkv_second_new,
        out_second_new,
        up_second_new,
        down_second_new,
        qkv_new,
        out_new,
        up_new,
        down_new,
        qkv_copy,
        out_copy,
        up_copy,
        down_copy,
        vector_grad.reshape(VEC),
        vector_second_new.reshape(VEC),
        vector_new.reshape(VEC),
        norms[0, :12].reshape(6, 2),
    )


def solution(mesh):
    in_specs = (
        P("dp", None),
        P(("dp", "mp"), None),
        P("dp", None),
        P("dp"),
        P(None, "dp", "mp"),
        P("mp", "dp"),
        P("dp", "mp"),
        P("mp", "dp"),
        P(None, "dp", "mp"),
        P("mp", "dp"),
        P("dp", "mp"),
        P("mp", "dp"),
        P(None, "dp", "mp"),
        P("mp", "dp"),
        P("dp", "mp"),
        P("mp", "dp"),
        P(),
        P(),
        P(),
    )
    out_specs = (
        P(("dp", "mp"), None),
        P(("dp", "mp"), None),
        P(None, "dp", "mp"),
        P("mp", "dp"),
        P("dp", "mp"),
        P("mp", "dp"),
        P(None, "dp", "mp"),
        P("mp", "dp"),
        P("dp", "mp"),
        P("mp", "dp"),
        P(None, "dp", "mp"),
        P("mp", "dp"),
        P("dp", "mp"),
        P("mp", "dp"),
        P(None, "dp", "mp"),
        P("mp", "dp"),
        P("dp", "mp"),
        P("mp", "dp"),
        P(),
        P(),
        P(),
        P(),
    )
    return jax.shard_map(shards, mesh=mesh, in_specs=in_specs, out_specs=out_specs, check_vma=False)
```

time: 473 us -> 336 us (0.71); the launches traced: 464 us -> 332 us
  waiting for transfers between devices: 117 us -> 74 us
  other arithmetic: 40.1 us -> 1.89 us
  Pallas kernels: 172 us -> 146 us
  starting transfers between devices: 93.9 us -> 72.4 us
    ppermute x90 -> x71, waiting for transfers between devices: 117 us -> 74 us  [send(): return after(lax.ppermute(value, AXES, pairs), *beside)]
    pallas_call x13 -> x29, Pallas kernels: 172 us -> 146 us  [call(): pl.pallas_call(body, in_specs=[pl.BlockSpec(memory_space=pltpu.SMEM)] + [...]
    ppermute x90 -> x71, starting transfers between devices: 93.9 us -> 72.4 us  [send(): return after(lax.ppermute(value, AXES, pairs), *beside)]
    convert_element_type x16 -> x2, other arithmetic: 13 us -> 0.03 us  [the longest x1 0.02 us: shards(): up_shard = up_weight.astype(LOW)]
    squeeze x21 -> x0, local copies, waits for them, and re-layouts: 10.5 us -> none  [the longest x3 10.1 us: scatter_sum(): items = plus(items[0], send(items[1], CORE))]
    reduce_sum x7 -> x0, other arithmetic: 9.86 us -> none  [the longest x1 2.42 us: shards(): jnp.sum(down_weight * down_weight)[None]]
    concatenate x17 -> x6, other arithmetic: 9.01 us -> 0.4 us  [the longest x3 0.28 us: gather_near(): jnp.concatenate([first, send(first, OVER_X, *beside)])]
    unnamed x131 -> x159, local copies, waits for them, and re-layouts: 21 us -> 29.2 us
  transfers between devices with their start and end apart: 90 -> 71, of which waited for: 38 -> 26; matrix products, arithmetic and copies ran while one was open for 11% -> 3% of each run, Pallas kernels for 34% -> 35%
where the time goes in v2:
time: 336 us; the launch traced here: 332 us
  Pallas kernels  146 us (43%)
  waiting for transfers between devices  74 us (22%)
  starting transfers between devices  72.4 us (22%)
  local copies, waits for them, and re-layouts  36.1 us (11%)
    pallas_call x29, Pallas kernels, call(): pl.pallas_call(body, in_specs=[pl.BlockSpec(memory_space=pltpu.SMEM)] + [...  146 us
    ppermute x71, waiting for transfers between devices, send(): return after(lax.ppermute(value, AXES, pairs), *beside)  74 us
    ppermute x71, starting transfers between devices, send(): return after(lax.ppermute(value, AXES, pairs), *beside)  72.4 us
    unnamed x159, local copies, waits for them, and re-layouts  29.2 us
  transfers between devices with their start and end apart: 71, of which 26 were waited for; matrix products, arithmetic and copies ran while one was open for 3% of the time, Pallas kernels for 35%

profile of v2, /device:TPU:0, one launch (start us, length us, event | category | flops | bytes accessed | tf_op | source)
XLA Modules:
  0.0 332.4 jit_solution(1571438196435547509)
XLA Ops:
  2.8 3.1 collective-permute-start
  14.5 6.7 %collective-permute-done.2 = bf16[96,768]{1,0:T(8,128)(2,1)S(1)} collective-permute-done((bf16[96,768]{1,0:T(8,128)(2,1)S(1)}, bf16[96,768]{1,0:T(8,128)(2,1)S(1)}, u32[]{:S(2)}, u32[]{:S(2)}) %collective-permute-start.2) | collective-permute-done | bytes 147488 | tf_op jit(solution)/shard_map/ppermute | solution.py:70
  24.2 7.0 %collective-permute-done.4 = bf16[2,96,768]{2,1,0:T(8,128)(2,1)S(1)} collective-permute-done((bf16[2,96,768]{2,1,0:T(8,128)(2,1)S(1)}, bf16[2,96,768]{2,1,0:T(8,128)(2,1)S(1)}, u32[]{:S(2)}, u32[]{:S(2)}) %collective-permute-start.4) | collective-permute-done | bytes 294944 | tf_op jit(solution)/shard_map/ppermute | solution.py:70
  35.9 4.5 %collective-permute-done.11.refs_6_ = bf16[96,768]{1,0:T(8,128)(2,1)S(1)} collective-permute-done((bf16[96,768]{1,0:T(8,128)(2,1)S(1)}, bf16[96,768]{1,0:T(8,128)(2,1)S(1)}, u32[]{:S(2)}, u32[]{:S(2)}) %collective-permute-start.11) | collective-permute-done | bytes 147488 | tf_op jit(solution)/shard_map/ppermute | solution.py:70
  46.6 4.7 %collective-permute-done.13.refs_8_ = bf16[96,768]{1,0:T(8,128)(2,1)S(1)} collective-permute-done((bf16[96,768]{1,0:T(8,128)(2,1)S(1)}, bf16[96,768]{1,0:T(8,128)(2,1)S(1)}, u32[]{:S(2)}, u32[]{:S(2)}) %collective-permute-start.13) | collective-permute-done | bytes 147488 | tf_op jit(solution)/shard_map/ppermute | solution.py:70
  60.4 14.3 %attend.2 = (bf16[12,512,128]{2,1,0:T(8,128)(2,1)S(1)}, bf16[12,512,128]{2,1,0:T(8,128)(2,1)S(1)}, bf16[12,512,64]{2,1,0:T(8,128)(2,1)S(1)}, bf16[4,512,192]{2,1...) custom-call(s32[5]{0:T(128)S(1)} %stack.75.where, ...), custom_call_target="tpu_custom_call" | custom-call | flops 30000001024 | bytes 1048576 | tf_op jit(solution)/shard_map/attend/pallas_call | solution.py:215
  81.4 14.2 %attend.3 = (bf16[12,512,128]{2,1,0:T(8,128)(2,1)S(1)}, bf16[12,512,128]{2,1,0:T(8,128)(2,1)S(1)}, bf16[12,512,64]{2,1,0:T(8,128)(2,1)S(1)}, bf16[4,512,192]{2,1...) custom-call(s32[5]{0:T(128)S(1)} %stack.75.where, ...), custom_call_target="tpu_custom_call" | custom-call | flops 30000001024 | bytes 1048576 | tf_op jit(solution)/shard_map/attend/pallas_call | solution.py:215
  96.2 4.8 %collective-permute-done.25 = bf16[2,96,768]{2,1,0:T(8,128)(2,1)S(1)} collective-permute-done((bf16[2,96,768]{2,1,0:T(8,128)(2,1)S(1)}, bf16[2,96,768]{2,1,0:T(8,128)(2,1)S(1)}, u32[]{:S(2)}, u32[]{:S(2)}) %collective-permute-start.25) | collective-permute-done | bytes 294944 | tf_op jit(solution)/shard_map/ppermute | solution.py:70
  102.6 7.1 %collective-permute-done.26 = bf16[2,96,768]{2,1,0:T(8,128)(2,1)S(1)} collective-permute-done((bf16[2,96,768]{2,1,0:T(8,128)(2,1)S(1)}, bf16[2,96,768]{2,1,0:T(8,128)(2,1)S(1)}, u32[]{:S(2)}, u32[]{:S(2)}) %collective-permute-start.26) | collective-permute-done | bytes 294944 | tf_op jit(solution)/shard_map/ppermute | solution.py:70
  114.0 10.3 %widen.1 = (bf16[4,1024,768]{2,1,0:T(8,128)(2,1)S(1)}, bf16[4,1024,768]{2,1,0:T(8,128)(2,1)S(1)}, f32[8,128]{1,0:T(8,128)}) custom-call(s32[5]{0:T(128)S(1)} %stack.75.where, bf16[512,768]{1,0:T(8,128)(2,1)S(1)} %get-tuple-element.187.refs_0_.refs_3_, bf16[512,768]{1,0:T(8,128)(2,1)S(1)} %get-tuple-element.195.refs_1_.refs_4_, ...), custom_call_target="tpu_custom_call" | custom-call | flops 30000001024 | bytes 1048576 | tf_op jit(solution)/shard_map/widen/pallas_call | solution.py:215
  137.4 10.1 %narrow.1 = (bf16[1024,768]{1,0:T(8,128)(2,1)}, f32[1024,768]{1,0:T(8,128)S(1)}, f32[1024,1]{1,0:T(8,128)S(1)}, f32[8,768]{1,0:T(8,128)S(1)}, f32[8,128]{1,0:T(8,128)}) custom-call(s32[5]{0:T(128)S(1)} %stack.75.where, bf16[4,1024,768]{2,1,0:T(8,128)(2,1)S(1)} %bitcast.91, bf16[4,768,768]{2,1,0:T(8,128)(2,1)S(1)} %bitcast.88, f32[1,9216]{1,0:T(1,128)S(1)} %bitcast.67, ...), custom_call_target="tpu_custom_call" | custom-call | flops 30000001024 | bytes 1048576 | tf_op jit(solution)/shard_map/narrow/pallas_call | solution.py:215
  165.2 3.3 contrast.1
  170.2 5.7 %grad_of_down.1 = (bf16[2,2,2,2,96,768]{5,4,3,2,1,0:T(8,128)(2,1)S(1)}, bf16[2,2,2,2,96,768]{5,4,3,2,1,0:T(8,128)(2,1)S(1)}, f32[8,128]{1,0:T(8,128)S(1)}) custom-call(s32[5]{0:T(128)S(1)} %stack.75.where, bf16[1024,768]{1,0:T(8,128)(2,1)S(1)} %get-tuple-element.217.refs_0_, bf16[4,1024,768]{2,1,0:T(8,128)(2,1)S(1)} %bitcast.91), custom_call_target="tpu_custom_call" | custom-call | flops 30000001024 | bytes 1048576 | tf_op jit(solution)/shard_map/grad_of_down/pallas_call | solution.py:215
  182.4 11.6 %grad_of_up.1 = (bf16[4,1024,768]{2,1,0:T(8,128)(2,1)S(1)}, f32[4,1,768]{2,1,0:T(1,128)S(1)}, bf16[2,2,2,2,96,768]{5,4,3,2,1,0:T(8,128)(2,1)S(1)}, bf16[2,2,2,2,96,768]{5,4,3,2,1,0:T(8,128)(2,1)S(1)}, f32[8,128]{1,0:T(8,128)}) custom-call(s32[5]{0:T(128)S(1)} %stack.75.where, bf16[1024,768]{1,0:T(8,128)(2,1)S(1)} %get-tuple-element.217.refs_0_, ...), custom_call_target="tpu_custom_call" | custom-call | flops 30000001024 | bytes 1048576 | tf_op jit(solution)/shard_map/grad_of_up/pallas_call | solution.py:215
  204.7 11.0 %middle.1 = (f32[1024,768]{1,0:T(8,128)S(1)}, bf16[1024,768]{1,0:T(8,128)(2,1)S(1)}, f32[1,768]{1,0:T(1,128)S(1)}, f32[1,768]{1,0:T(1,128)S(1)}, f32[1,768]{1,0:...) custom-call(s32[5]{0:T(128)S(1)} %stack.75.where, bf16[4,1024,768]{2,1,0:T(8,128)(2,1)S(1)} %copy-done.23, ...), custom_call_target="tpu_custom_call" | custom-call | flops 30000001024 | bytes 1048576 | tf_op jit(solution)/shard_map/middle/pallas_call | solution.py:215
  218.7 12.0 %attend_back.2 = (bf16[4,512,768]{2,1,0:T(8,128)(2,1)S(1)}, f32[8,128]{1,0:T(8,128)}) custom-call(s32[5]{0:T(128)S(1)} %stack.75.where, bf16[12,512,128]{2,1,0:T(8,128)(2,1)S(1)} %copy-done.44, bf16[12,512,128]{2,1,0:T(8,128)(2,1)S(1)} %copy-done.46, bf16[12,512,64]{2,1,0:T(8,128)(2,1)S(1)} %copy-done.48, ...), custom_call_target="tpu_custom_call" | custom-call | flops 30000001024 | bytes 1048576 | tf_op jit(solution)/shard_map/attend_back/pallas_call | solution.py:215
  235.6 12.0 %attend_back.3 = (bf16[4,512,768]{2,1,0:T(8,128)(2,1)S(1)}, f32[8,128]{1,0:T(8,128)}) custom-call(s32[5]{0:T(128)S(1)} %stack.75.where, bf16[12,512,128]{2,1,0:T(8,128)(2,1)S(1)} %copy-done.38, bf16[12,512,128]{2,1,0:T(8,128)(2,1)S(1)} %copy-done.40, bf16[12,512,64]{2,1,0:T(8,128)(2,1)S(1)} %copy-done.42, ...), custom_call_target="tpu_custom_call" | custom-call | flops 30000001024 | bytes 1048576 | tf_op jit(solution)/shard_map/attend_back/pallas_call | solution.py:215
  255.0 7.9 %grad_of_attention.1 = (f32[4,1,768]{2,1,0:T(1,128)S(1)}, bf16[2,2,2,2,96,768]{5,4,3,2,1,0:T(8,128)(2,1)S(1)}, bf16[2,2,2,2,96,768]{5,4,3,2,1,0:T(8,128)(2,1)S(1)}, f32[8,128]{1,0:T(8,128)}) custom-call(s32[5]{0:T(128)S(1)} %stack.75.where, bf16[1024,768]{1,0:T(8,128)(2,1)S(1)} %constant_dynamic-slice_fusion.3.refs_0_, ...), custom_call_target="tpu_custom_call" | custom-call | flops 30000001024 | bytes 1048576 | tf_op jit(solution)/shard_map/grad_of_attention/pallas_call | solution.py:215
  264.7 3.2 collective-permute-start.58
  274.5 9.0 %grad_of_input.1 = (f32[1024,768]{1,0:T(8,128)}, f32[8,128]{1,0:T(8,128)}) custom-call(s32[5]{0:T(128)S(1)} %stack.75.where, bf16[4,768,768]{2,1,0:T(8,128)(2,1)S(1)} %bitcast.83, f32[1024,768]{1,0:T(8,128)S(1)} %get-tuple-element.227.refs_1_, bf16[4,512,768]{2,1,0:T(8,128)(2,1)S(1)} %get-tuple-element.240.refs_2_, ...), custom_call_target="tpu_custom_call" | custom-call | flops 30000001024 | bytes 1048576 | tf_op jit(solution)/shard_map/grad_of_input/pallas_call | solution.py:215
  292.1 3.6 %collective-permute-done.53.refs_2_ = bf16[2,96,768]{2,1,0:T(8,128)(2,1)S(1)} collective-permute-done((bf16[2,96,768]{2,1,0:T(8,128)(2,1)S(1)}, bf16[2,96,768]{2,1,0:T(8,128)(2,1)S(1)}, u32[]{:S(2)}, u32[]{:S(2)}) %collective-permute-start.53) | collective-permute-done | bytes 294944 | tf_op jit(solution)/shard_map/ppermute | solution.py:70
  306.1 3.1 collective-permute-done.56.refs_2_
  318.8 3.3 %collective-permute-start.70 = (f32[1,9344]{1,0:T(1,128)S(1)}, f32[1,9344]{1,0:T(1,128)S(1)}, u32[]{:S(2)}, u32[]{:S(2)}) collective-permute-start(f32[1,9344]{1,0:T(1,128)S(1)} %add_add_fusion.1), channel_id=1, source_target_pairs={{0,24},{1,25},{2,26},{3,27},{4,28},{5,29},{6,30},{7,31},{8,0},{9,1... | collective-permute-start | bytes 112136 | tf_op jit(solution)/shard_map/ppermute | solution.py:70
  324.7 3.2 collective-permute-done.68
  (364 shorter events, 154.8 us)
Async XLA Ops:
  23.6 19.3 %collective-permute-start.5 = (bf16[4,96,768]{2,1,0:T(8,128)(2,1)S(1)}, bf16[4,96,768]{2,1,0:T(8,128)(2,1)S(1)}, u32[]{:S(2)}, u32[]{:S(2)}) collective-permute-start(bf16[4,96,768]{2,1,0:T(8,128)(2,1)S(1)} %pad_maximum_fusion.refs_0_), channel_id=1, source_target_pairs={{0,2},{1,3},{2,0},{3,1},{4,6},{5,7},{6,4},{7,5},{8,10},{9,11},{10,... | collective-permute-start | bytes 1769480 | tf_op jit(solution)/shard_map/ppermute | solution.py:70
  51.3 27.6 %collective-permute-start.16 = (bf16[96,768]{1,0:T(8,128)(2,1)S(1)}, bf16[96,768]{1,0:T(8,128)(2,1)S(1)}, u32[]{:S(2)}, u32[]{:S(2)}) collective-permute-start(bf16[96,768]{1,0:T(8,128)(2,1)S(1)} %convert_bitcast_fusion.refs_7_), channel_id=1, source_target_pairs={{0,8},{1,9},{2,10},{3,11},{4,12},{5,13},{6,14},{7,15},{8,16},{9,17... | collective-permute-start | bytes 442376 | tf_op jit(solution)/shard_map/ppermute | solution.py:70
  51.4 28.2 %collective-permute-start.17 = (bf16[96,768]{1,0:T(8,128)(2,1)S(1)}, bf16[96,768]{1,0:T(8,128)(2,1)S(1)}, u32[]{:S(2)}, u32[]{:S(2)}) collective-permute-start(bf16[96,768]{1,0:T(8,128)(2,1)S(1)} %convert_bitcast_fusion.refs_7_), channel_id=1, source_target_pairs={{0,16},{1,17},{2,18},{3,19},{4,20},{5,21},{6,22},{7,23},{8,24},{9,... | collective-permute-start | bytes 442376 | tf_op jit(solution)/shard_map/ppermute | solution.py:70
  54.1 25.7 %collective-permute-start.18 = (bf16[96,768]{1,0:T(8,128)(2,1)S(1)}, bf16[96,768]{1,0:T(8,128)(2,1)S(1)}, u32[]{:S(2)}, u32[]{:S(2)}) collective-permute-start(bf16[96,768]{1,0:T(8,128)(2,1)S(1)} %convert_bitcast_fusion.refs_7_), channel_id=1, source_target_pairs={{0,24},{1,25},{2,26},{3,27},{4,28},{5,29},{6,30},{7,31},{8,0},{9,1... | collective-permute-start | bytes 442376 | tf_op jit(solution)/shard_map/ppermute | solution.py:70
  55.3 22.9 %collective-permute-start.14 = (bf16[2,96,768]{2,1,0:T(8,128)(2,1)S(1)}, bf16[2,96,768]{2,1,0:T(8,128)(2,1)S(1)}, u32[]{:S(2)}, u32[]{:S(2)}) collective-permute-start(bf16[2,96,768]{2,1,0:T(8,128)(2,1)S(1)} %pad_maximum_fusion.8), channel_id=1, source_target_pairs={{0,4},{1,5},{2,6},{3,7},{4,0},{5,1},{6,2},{7,3},{8,12},{9,13},{10,... | collective-permute-start | bytes 884744 | tf_op jit(solution)/shard_map/ppermute | solution.py:70
  56.8 22.0 %collective-permute-start.15 = (bf16[2,96,768]{2,1,0:T(8,128)(2,1)S(1)}, bf16[2,96,768]{2,1,0:T(8,128)(2,1)S(1)}, u32[]{:S(2)}, u32[]{:S(2)}) collective-permute-start(bf16[2,96,768]{2,1,0:T(8,128)(2,1)S(1)} %pad_maximum_fusion.9), channel_id=1, source_target_pairs={{0,2},{1,3},{2,0},{3,1},{4,6},{5,7},{6,4},{7,5},{8,10},{9,11},{10,... | collective-permute-start | bytes 884744 | tf_op jit(solution)/shard_map/ppermute | solution.py:70
  78.3 17.3 %collective-permute-start.19 = (bf16[4,96,768]{2,1,0:T(8,128)(2,1)S(1)}, bf16[4,96,768]{2,1,0:T(8,128)(2,1)S(1)}, u32[]{:S(2)}, u32[]{:S(2)}) collective-permute-start(bf16[4,96,768]{2,1,0:T(8,128)(2,1)S(1)} %pad_maximum_fusion.2.refs_5_.refs_0_), channel_id=1, source_target_pairs={{0,2},{1,3},{2,0},{3,1},{4,6},{5,7},{6,4},{7,5},{8,10},{9,11},{10,... | collective-permute-start | bytes 1769480 | tf_op jit(solution)/shard_map/ppermute | solution.py:70
  78.9 31.0 %collective-permute-start.21 = (bf16[4,96,768]{2,1,0:T(8,128)(2,1)S(1)}, bf16[4,96,768]{2,1,0:T(8,128)(2,1)S(1)}, u32[]{:S(2)}, u32[]{:S(2)}) collective-permute-start(bf16[4,96,768]{2,1,0:T(8,128)(2,1)S(1)} %pad_maximum_fusion.2.refs_5_.refs_0_), channel_id=1, source_target_pairs={{0,1},{1,0},{2,3},{3,2},{4,5},{5,4},{6,7},{7,6},{8,9},{9,8},{10,11... | collective-permute-start | bytes 1769480 | tf_op jit(solution)/shard_map/ppermute | solution.py:70
  78.9 16.8 %collective-permute-start.20 = (bf16[4,96,768]{2,1,0:T(8,128)(2,1)S(1)}, bf16[4,96,768]{2,1,0:T(8,128)(2,1)S(1)}, u32[]{:S(2)}, u32[]{:S(2)}) collective-permute-start(bf16[4,96,768]{2,1,0:T(8,128)(2,1)S(1)} %pad_maximum_fusion.3.refs_6_.refs_1_), channel_id=1, source_target_pairs={{0,4},{1,5},{2,6},{3,7},{4,0},{5,1},{6,2},{7,3},{8,12},{9,13},{10,... | collective-permute-start | bytes 1769480 | tf_op jit(solution)/shard_map/ppermute | solution.py:70
  79.5 30.8 %collective-permute-start.22 = (bf16[4,96,768]{2,1,0:T(8,128)(2,1)S(1)}, bf16[4,96,768]{2,1,0:T(8,128)(2,1)S(1)}, u32[]{:S(2)}, u32[]{:S(2)}) collective-permute-start(bf16[4,96,768]{2,1,0:T(8,128)(2,1)S(1)} %pad_maximum_fusion.3.refs_6_.refs_1_), channel_id=1, source_target_pairs={{0,1},{1,0},{2,3},{3,2},{4,5},{5,4},{6,7},{7,6},{8,9},{9,8},{10,11... | collective-permute-start | bytes 1769480 | tf_op jit(solution)/shard_map/ppermute | solution.py:70
  79.8 21.3 %collective-permute-start.25 = (bf16[2,96,768]{2,1,0:T(8,128)(2,1)S(1)}, bf16[2,96,768]{2,1,0:T(8,128)(2,1)S(1)}, u32[]{:S(2)}, u32[]{:S(2)}) collective-permute-start(bf16[2,96,768]{2,1,0:T(8,128)(2,1)S(1)} %pad_maximum_fusion.10), channel_id=1, source_target_pairs={{0,4},{1,5},{2,6},{3,7},{4,0},{5,1},{6,2},{7,3},{8,12},{9,13},{10,... | collective-permute-start | bytes 884744 | tf_op jit(solution)/shard_map/ppermute | solution.py:70
  95.7 16.7 %collective-permute-start.24 = (bf16[4,96,768]{2,1,0:T(8,128)(2,1)S(1)}, bf16[4,96,768]{2,1,0:T(8,128)(2,1)S(1)}, u32[]{:S(2)}, u32[]{:S(2)}) collective-permute-start(bf16[4,96,768]{2,1,0:T(8,128)(2,1)S(1)} %collective-permute-done.20.refs_3_), channel_id=1, source_target_pairs={{0,1},{1,0},{2,3},{3,2},{4,5},{5,4},{6,7},{7,6},{8,9},{9,8},{10,11... | collective-permute-start | bytes 1769480 | tf_op jit(solution)/shard_map/ppermute | solution.py:70
  109.8 24.0 %collective-permute-start.29 = (bf16[4,96,768]{2,1,0:T(8,128)(2,1)S(1)}, bf16[4,96,768]{2,1,0:T(8,128)(2,1)S(1)}, u32[]{:S(2)}, u32[]{:S(2)}) collective-permute-start(bf16[4,96,768]{2,1,0:T(8,128)(2,1)S(1)} %get-tuple-element.203.refs_4_.refs_0_), channel_id=1, source_target_pairs={{0,1},{1,0},{2,3},{3,2},{4,5},{5,4},{6,7},{7,6},{8,9},{9,8},{10,11... | collective-permute-start | bytes 1769480 | tf_op jit(solution)/shard_map/ppermute | solution.py:70
  109.9 23.9 %collective-permute-start.30 = (bf16[4,96,768]{2,1,0:T(8,128)(2,1)S(1)}, bf16[4,96,768]{2,1,0:T(8,128)(2,1)}, u32[]{:S(2)}, u32[]{:S(2)}) collective-permute-start(bf16[4,96,768]{2,1,0:T(8,128)(2,1)S(1)} %get-tuple-element.206.refs_5_.refs_1_), channel_id=1, source_target_pairs={{0,1},{1,0},{2,3},{3,2},{4,5},{5,4},{6,7},{7,6},{8,9},{9,8},{10,11... | collective-permute-start | bytes 1769480 | tf_op jit(solution)/shard_map/ppermute | solution.py:70
  110.4 19.3 %collective-permute-start.27 = (bf16[4,96,768]{2,1,0:T(8,128)(2,1)S(1)}, bf16[4,96,768]{2,1,0:T(8,128)(2,1)}, u32[]{:S(2)}, u32[]{:S(2)}) collective-permute-start(bf16[4,96,768]{2,1,0:T(8,128)(2,1)S(1)} %get-tuple-element.203.refs_4_.refs_0_), channel_id=1, source_target_pairs={{0,2},{1,3},{2,0},{3,1},{4,6},{5,7},{6,4},{7,5},{8,10},{9,11},{10,... | collective-permute-start | bytes 1769480 | tf_op jit(solution)/shard_map/ppermute | solution.py:70
  111.9 17.8 %collective-permute-start.28 = (bf16[4,96,768]{2,1,0:T(8,128)(2,1)S(1)}, bf16[4,96,768]{2,1,0:T(8,128)(2,1)}, u32[]{:S(2)}, u32[]{:S(2)}) collective-permute-start(bf16[4,96,768]{2,1,0:T(8,128)(2,1)S(1)} %get-tuple-element.206.refs_5_.refs_1_), channel_id=1, source_target_pairs={{0,4},{1,5},{2,6},{3,7},{4,0},{5,1},{6,2},{7,3},{8,12},{9,13},{10,... | collective-permute-start | bytes 1769480 | tf_op jit(solution)/shard_map/ppermute | solution.py:70
  177.3 17.3 %collective-permute-start.40 = (bf16[2,2,2,2,96,768]{5,4,3,2,1,0:T(8,128)(2,1)S(1)}, bf16[2,2,2,2,96,768]{5,4,3,2,1,0:T(8,128)(2,1)S(1)}, u32[]{:S(2)}, u32[]{:S(2)}) collective-permute-start(bf16[2,2,2,2,96,768]{5,4,3,2,1,0:T(8,128)(2,1)S(1)} %get-tuple-element.225), channel_id=1, source_target_pairs={{0,1},{1,0},{2,3},{3,2},{4,5},{5,4},{6,7},{7,6},{8,9},{9,8},{10,11... | collective-permute-start | bytes 7077896 | tf_op jit(solution)/shard_map/ppermute | solution.py:70
  197.0 18.7 %collective-permute-start.41 = (bf16[2,2,96,768]{3,2,1,0:T(8,128)(2,1)S(1)}, bf16[2,2,96,768]{3,2,1,0:T(8,128)(2,1)S(1)}, u32[]{:S(2)}, u32[]{:S(2)}) collective-permute-start(bf16[2,2,96,768]{3,2,1,0:T(8,128)(2,1)S(1)} %get-tuple-element.234), channel_id=1, source_target_pairs={{0,2},{1,3},{2,0},{3,1},{4,6},{5,7},{6,4},{7,5},{8,10},{9,11},{10,... | collective-permute-start | bytes 1769480 | tf_op jit(solution)/shard_map/ppermute | solution.py:70
  198.5 17.2 %collective-permute-start.42 = (bf16[2,2,96,768]{3,2,1,0:T(8,128)(2,1)S(1)}, bf16[2,2,96,768]{3,2,1,0:T(8,128)(2,1)S(1)}, u32[]{:S(2)}, u32[]{:S(2)}) collective-permute-start(bf16[2,2,96,768]{3,2,1,0:T(8,128)(2,1)S(1)} %get-tuple-element.235), channel_id=1, source_target_pairs={{0,4},{1,5},{2,6},{3,7},{4,0},{5,1},{6,2},{7,3},{8,12},{9,13},{10,... | collective-permute-start | bytes 1769480 | tf_op jit(solution)/shard_map/ppermute | solution.py:70
  201.8 45.7 %collective-permute-start.46 = (bf16[2,2,96,768]{3,2,1,0:T(8,128)(2,1)}, bf16[2,2,96,768]{3,2,1,0:T(8,128)(2,1)}, u32[]{:S(2)}, u32[]{:S(2)}) collective-permute-start(bf16[2,2,96,768]{3,2,1,0:T(8,128)(2,1)} %get-tuple-element.258), channel_id=1, source_target_pairs={{0,2},{1,3},{2,0},{3,1},{4,6},{5,7},{6,4},{7,5},{8,10},{9,11},{10,... | collective-permute-start | bytes 1769480 | tf_op jit(solution)/shard_map/ppermute | solution.py:70
  203.0 44.5 %collective-permute-start.47 = (bf16[2,2,96,768]{3,2,1,0:T(8,128)(2,1)}, bf16[2,2,96,768]{3,2,1,0:T(8,128)(2,1)}, u32[]{:S(2)}, u32[]{:S(2)}) collective-permute-start(bf16[2,2,96,768]{3,2,1,0:T(8,128)(2,1)} %get-tuple-element.261), channel_id=1, source_target_pairs={{0,4},{1,5},{2,6},{3,7},{4,0},{5,1},{6,2},{7,3},{8,12},{9,13},{10,... | collective-permute-start | bytes 1769480 | tf_op jit(solution)/shard_map/ppermute | solution.py:70
  264.7 27.4 %collective-permute-start.58 = (bf16[96,768]{1,0:T(8,128)(2,1)S(1)}, bf16[96,768]{1,0:T(8,128)(2,1)S(1)}, u32[]{:S(2)}, u32[]{:S(2)}) collective-permute-start(bf16[96,768]{1,0:T(8,128)(2,1)S(1)} %get-tuple-element.294), channel_id=1, source_target_pairs={{0,8},{1,9},{2,10},{3,11},{4,12},{5,13},{6,14},{7,15},{8,16},{9,17... | collective-permute-start | bytes 442376 | tf_op jit(solution)/shard_map/ppermute | solution.py:70
  267.9 24.2 %collective-permute-start.59 = (bf16[96,768]{1,0:T(8,128)(2,1)S(1)}, bf16[96,768]{1,0:T(8,128)(2,1)S(1)}, u32[]{:S(2)}, u32[]{:S(2)}) collective-permute-start(bf16[96,768]{1,0:T(8,128)(2,1)S(1)} %get-tuple-element.296), channel_id=1, source_target_pairs={{0,16},{1,17},{2,18},{3,19},{4,20},{5,21},{6,22},{7,23},{8,24},{9,... | collective-permute-start | bytes 442376 | tf_op jit(solution)/shard_map/ppermute | solution.py:70
  268.7 23.4 %collective-permute-start.60 = (bf16[96,768]{1,0:T(8,128)(2,1)S(1)}, bf16[96,768]{1,0:T(8,128)(2,1)S(1)}, u32[]{:S(2)}, u32[]{:S(2)}) collective-permute-start(bf16[96,768]{1,0:T(8,128)(2,1)S(1)} %get-tuple-element.298), channel_id=1, source_target_pairs={{0,24},{1,25},{2,26},{3,27},{4,28},{5,29},{6,30},{7,31},{8,0},{9,1... | collective-permute-start | bytes 442376 | tf_op jit(solution)/shard_map/ppermute | solution.py:70
  (119 other events, 1206.3 us)

commit v3 on v2

--- a/solution.py
+++ b/solution.py
@@ -149,20 +149,28 @@
             half = z // 2
             over_y = half == 0
             first, second = jnp.where(over_y, y, x), jnp.where(over_y, x, y)
-            outs[core][half, first, second, z % 2] = value[
+            outs[core % len(outs)][half, first, second, z % 2] = value[
                 index * self.rows : (index + 1) * self.rows
             ]
 
 
-def share(value):
-    if not on_grid():
-        dp_size, mp_size = lax.axis_size("dp"), lax.axis_size("mp")
-        whole = lax.all_gather(value, AXES, axis=0, tiled=True)
-        own = lax.axis_index("dp") * mp_size + lax.axis_index("mp")
-        return jnp.roll(whole, -own * value.shape[0], axis=0)
-    value = jnp.concatenate([value, send(value, CORE)])
-    value = jnp.concatenate([value] + [send(value, pairs) for pairs in (OVER_X, OVER_Y, OVER_XY)])
-    return jnp.concatenate([value] + [send(value, UP_Z[s]) for s in (1, 2, 3)])
+def share_plain(value):
+    whole = lax.all_gather(value, AXES, axis=0, tiled=True)
+    own = lax.axis_index("dp") * lax.axis_size("mp") + lax.axis_index("mp")
+    return jnp.roll(whole, -own * value.shape[0], axis=0)
+
+
+def share_core(value, *beside):
+    return jnp.concatenate([value, send(value, CORE, *beside)])
+
+
+def share_plane(value, *beside):
+    sides = [send(value, pairs, *beside) for pairs in (OVER_X, OVER_Y, OVER_XY)]
+    return jnp.concatenate([value] + sides)
+
+
+def share_line(value, *beside):
+    return jnp.concatenate([value] + [send(value, UP_Z[s], *beside) for s in (1, 2, 3)])
 
 
 def shared_ids(own_rows):
@@ -199,7 +207,7 @@
     )
 
 
-def call(kernel, name, where, operands, outs, scratch=(), limit=24, wait_for=()):
+def call(kernel, name, where, operands, outs, scratch=(), limit=14, wait_for=()):
     count = len(operands)
     many = len(outs)
 
@@ -273,15 +281,16 @@
         ).astype(LOW)
 
 
-def add(where, operands, plan):
+def add(where, operands, plan, wait_for=()):
     outs = []
     for left, left_at, _, _ in plan:
         outs.append(array(LOW, *operands[left].shape[len(left_at) :]))
-    return call(partial(add_kernel, plan), "add", where, operands, outs, limit=8)
-
-
-def scatter_core(where, parts, *beside):
-    arrived = send(parts[1], CORE, *beside)
+    return call(partial(add_kernel, plan), "add", where, operands, outs, limit=8, wait_for=wait_for)
+
+
+def scatter_core(where, parts, *beside, arrived=None):
+    if arrived is None:
+        arrived = send(parts[1], CORE, *beside)
     plan = [(0, (half, near), 1, (half, near)) for half in (0, 1) for near in (0, 1)]
     return add(where, [parts[0], arrived], plan)
 
@@ -292,86 +301,147 @@
     return add(where, [sums[0], sums[2], *arrived], plan)
 
 
-def scatter_near(where, sums, *beside):
+def scatter_near(where, sums, *beside, wait_for=()):
     arrived = [send(sums[1], OVER_X, *beside), send(sums[3], OVER_Y, *beside)]
     plan = [(half, (z,), half + 2, (z,)) for half in (0, 1) for z in (0, 1)]
-    return add(where, [sums[0], sums[2], *arrived], plan)
+    return add(where, [sums[0], sums[2], *arrived], plan, wait_for)
 
 
 def scatter_z(sums, *beside):
     return [sums[0]] + [send(sums[s], UP_Z[s], *beside) for s in (1, 2, 3)]
 
 
-def attend_kernel(blocks, where, x_ref, w_ref, bias_ref, vec_ref, seg_ref, *refs):
-    q_out, k_out, v_out, context_out, unit_out, inverse_out, low_out, sum_ref = refs
-    heads = HEADS // blocks
-    width = HD * heads
+TILE = 2 * HD
+HEADS_BLOCK = 3
+SIDES = (0, 1, 0)
+KEYS = 3 * TILE
+OUT = 4 * TILE
+
+
+def join_columns(query, key, value, out):
+    q, v = [[part[:, h * HD : (h + 1) * HD] for h in range(3)] for part in (query, value)]
+    return jnp.concatenate([q[0], v[0], v[1], q[1], q[2], v[2], key, out], axis=1)
+
+
+def query_columns(part):
+    return jnp.concatenate([part[:, :HD], part[:, 3 * HD : 5 * HD]], axis=1)
+
+
+def value_columns(part):
+    return jnp.concatenate([part[:, HD : 3 * HD], part[:, 5 * HD : 6 * HD]], axis=1)
+
+
+def arrange_kernel(where, qkv_ref, out_ref, held):
+    parts = [qkv_ref[0], qkv_ref[1], qkv_ref[2], out_ref[...].T]
+    held[...] = join_columns(*parts).astype(LOW)
+
+
+def arrange(where, qkv_weight, out_weight):
+    outs = [array(LOW, qkv_weight.shape[1], D)]
+    return call(arrange_kernel, "arrange", where, [qkv_weight, out_weight], outs, limit=8)[0]
+
+
+def arrange_bias_kernel(where, vec_ref, held):
+    blocks = held.shape[0]
+    width = D // blocks
+    none = jnp.zeros((1, width), WIDE)
+    for m in range(blocks):
+        query = vec_ref[:, m * width : (m + 1) * width]
+        value = vec_ref[:, D + m * width : D + (m + 1) * width]
+        held[m] = join_columns(query, none, value, none)
+
+
+def arrange_bias(where, vectors, blocks):
+    outs = [array(WIDE, blocks, 1, D)]
+    return call(arrange_bias_kernel, "arrange_bias", where, [vectors], outs, limit=8)[0]
+
+
+def attend_kernel(blocks, chosen, last, where, x_ref, w_ref, bias_ref, vec_ref, seg_ref, *refs):
+    if chosen[0] == 0:
+        held = None
+    else:
+        held, refs = refs[0], refs[1:]
+    q_out, k_out, v_out, log_out, context_out, *refs = refs
+    if last:
+        unit_out, inverse_out, low_out, sum_ref = refs
+    else:
+        (sum_ref,) = refs
     x = x_ref[...]
-    lanes = lax.broadcasted_iota(jnp.int32, (L, 2 * HD), 1)
-    passage = jnp.broadcast_to(seg_ref[...], (L, 2 * HD)) + HD
-    is_passage = (lanes >= HD) & (lanes < HD + PASS)
-    q_tail = jnp.where(is_passage & (lanes != passage), masked_value, 0.0)
-    k_tail = (lanes == passage) | ((lanes >= HD + PASS) & (lanes < HD + PASS + 3))
-    k_tail = jnp.where(k_tail, 1.0, 0.0).astype(LOW)
-    k_scale = jnp.where(lanes < HD, 1.0, 0.0).astype(LOW)
-    q_scale = jnp.where(lanes < HD, HD ** (-0.5), 0.0).astype(LOW)
-    q_tail = q_tail.astype(LOW)
-    sum_ref[...] = x.astype(WIDE) + vec_ref[:, BO : BO + D]
-
-    def block(m, carry):
+    lanes = lax.broadcasted_iota(jnp.int32, (L, TILE), 1)
+    passage = jnp.broadcast_to(seg_ref[...], (L, TILE))
+    sides = []
+    for side in SIDES:
+        mine = (lanes >= HD) == side
+        column = lanes - (0 if side else HD)
+        foreign = (column >= 0) & (column < PASS) & (column != passage)
+        same = (column >= 0) & (column < PASS) & (column == passage)
+        sides.append(
+            (
+                jnp.where(mine, HD ** (-0.5), 0.0).astype(LOW),
+                jnp.where(foreign, masked_value, 0.0).astype(LOW),
+                jnp.where(mine, 1.0, 0.0).astype(LOW),
+                jnp.where(same, 1.0, 0.0).astype(LOW),
+                jnp.where(mine, 0.0, 1.0).astype(LOW),
+            )
+        )
+    sum_ref[...] = held[...] if held is not None else x.astype(WIDE) + vec_ref[:, BO : BO + D]
+
+    def block(i, carry):
+        m = block_of(chosen[0] + i, where)
         projected = (dot(x, w_ref[m]) + bias_ref[m]).astype(LOW)
-        parts = []
-        for h in range(heads):
-            at = width + h * HD
-            query = projected[:, at : at + 2 * HD] * q_scale + q_tail
-            keys = projected[:, at + width : at + width + 2 * HD] * k_scale + k_tail
-            value = projected[:, at + 2 * width : at + 2 * width + HD]
+        parts = [jnp.zeros((HD, L), LOW)]
+        for h in range(HEADS_BLOCK):
+            q_scale, q_tail, k_scale, k_tail, v_scale = sides[h]
+            tile = projected[:, h * TILE : (h + 1) * TILE]
+            query = tile * q_scale + q_tail
+            at = KEYS + h // 2 * TILE
+            keys = projected[:, at : at + TILE] * k_scale + k_tail
+            value = tile.T[: HD] if SIDES[h] else tile.T[HD:]
             scores = dot(keys, query, (1, 1))
             highest = jnp.max(scores, axis=0, keepdims=True)
             weights = jnp.exp(scores - highest)
             totals = jnp.sum(weights, axis=0, keepdims=True)
-            mixed = dot(value.T, weights.astype(LOW)) * (1.0 / totals)
-            left = -(highest + jnp.log(totals))
-            high = left.astype(LOW).astype(WIDE)
-            middle = (left - high).astype(LOW).astype(WIDE)
-            rows = lax.broadcasted_iota(jnp.int32, (HD, L), 0)
-            split = jnp.where(rows == PASS, high, 0.0)
-            split = jnp.where(rows == PASS + 1, middle, split)
-            split = jnp.where(rows == PASS + 2, left - high - middle, split)
-            turned = jnp.concatenate([mixed, split], axis=0).T.astype(LOW)
-            parts.append(turned[:, :HD])
-            q_out[m * heads + h] = jnp.where(lanes < HD, query, query + turned)
-            k_out[m * heads + h] = keys
-            v_out[m * heads + h] = value
-        context = jnp.concatenate(parts, axis=1)
-        context_out[m] = context
-        sum_ref[...] += dot(context, w_ref[m, :, :width], (1, 1))
+            mixed = dot(value, weights.astype(LOW)) * (1.0 / totals)
+            parts.append(mixed.astype(LOW))
+            q_out[i * HEADS_BLOCK + h] = query
+            k_out[i * HEADS_BLOCK + h] = keys
+            v_out[i * HEADS_BLOCK + h] = tile * v_scale
+            log_out[i * HEADS_BLOCK + h] = highest + jnp.log(totals)
+        context = jnp.concatenate(parts, axis=0).T
+        context_out[i] = context
+        sum_ref[...] += dot(context, w_ref[m, :, OUT:], (1, 1))
         return carry
 
-    lax.fori_loop(0, blocks, block, 0)
-    unit, inverse = normalize(sum_ref[...])
-    unit_out[...] = unit
-    inverse_out[...] = inverse
-    low_out[...] = (unit * vec_ref[:, G1 : G1 + D] + vec_ref[:, C1 : C1 + D]).astype(LOW)
-
-
-def attend(where, inputs, weight, bias, vectors, segments, wait_for=()):
+    lax.fori_loop(0, len(chosen), block, 0)
+    if last:
+        unit, inverse = normalize(sum_ref[...])
+        unit_out[...] = unit
+        inverse_out[...] = inverse
+        low_out[...] = (unit * vec_ref[:, G1 : G1 + D] + vec_ref[:, C1 : C1 + D]).astype(LOW)
+
+
+def attend(where, chosen, held, inputs, weight, bias, vectors, segments, wait_for=()):
     blocks = bias.shape[0]
-    return call(
-        partial(attend_kernel, blocks),
+    heads = len(chosen) * HEADS // blocks
+    last = chosen[-1] == blocks - 1
+    outs = [
+        array(LOW, heads, L, TILE),
+        array(LOW, heads, L, TILE),
+        array(LOW, heads, L, TILE),
+        array(WIDE, heads, 1, L),
+        array(LOW, len(chosen), L, D - OUT),
+    ]
+    if last:
+        outs += [array(WIDE, L, D), array(WIDE, L, 1), array(LOW, L, D)]
+    else:
+        outs += [array(WIDE, L, D)]
+    return call(
+        partial(attend_kernel, blocks, chosen, last),
         "attend",
         where,
-        [inputs, weight, bias, vectors, segments],
-        [
-            array(LOW, HEADS, L, 2 * HD),
-            array(LOW, HEADS, L, 2 * HD),
-            array(LOW, HEADS, L, HD),
-            array(LOW, blocks, L, D // blocks),
-            array(WIDE, L, D),
-            array(WIDE, L, 1),
-            array(LOW, L, D),
-        ],
-        [pltpu.VMEM((L, D), WIDE)],
+        [inputs, weight, bias, vectors, segments] + ([] if held is None else [held]),
+        outs,
+        [pltpu.VMEM((L, D), WIDE)] if last else [],
         wait_for=wait_for,
     )
 
@@ -404,52 +474,70 @@
     )
 
 
-def narrow_kernel(rows, where, active_ref, w_ref, vec_ref, starts_ref, *refs):
-    units, (out, unit_out, inverse_out, cls_out, y_ref) = refs[:rows], refs[rows:]
-    for row in range(rows):
-        at = slice(row * L, (row + 1) * L)
-        y_ref[at] = units[row][...] * vec_ref[:, G1 : G1 + D] + (
-            vec_ref[:, C1 : C1 + D] + vec_ref[:, B2 : B2 + D]
-        )
-
-        def block(m, carry):
-            y_ref[at] += dot(active_ref[m, at], w_ref[m], (1, 1))
-            return carry
-
-        lax.fori_loop(0, w_ref.shape[0], block, 0)
-        unit, inverse = normalize(y_ref[at])
-        unit_out[at] = unit
-        inverse_out[at] = inverse
-        output = unit * vec_ref[:, G2 : G2 + D] + vec_ref[:, C2 : C2 + D]
-        out[at] = output.astype(LOW)
-        y_ref[at] = output
-    for p in range(cls_out.shape[0]):
-        cls_out[p : p + 1, :] = y_ref[pl.ds(starts_ref[p], 1), :]
-
-
-def narrow(where, active, weight, vectors, starts, units):
-    tokens = active.shape[1]
+def early_kernel(rows, blocks, where, active_ref, w_ref, vec_ref, starts_ref, *refs):
+    units, (cls_out, active_wide, rows_ref, sum_ref) = refs[:rows], refs[rows:]
+    few = cls_out.shape[0]
+    each = few // rows
+    for p in range(few):
+        at = pl.ds(starts_ref[p] - p // each * L, 1)
+        sum_ref[p : p + 1] = units[p // each][at, :]
+    sum_ref[...] = sum_ref[...] * vec_ref[:, G1 : G1 + D] + (
+        vec_ref[:, C1 : C1 + D] + vec_ref[:, B2 : B2 + D]
+    )
+    for m in range(blocks):
+        for p in range(few):
+            base = pl.multiple_of(starts_ref[p] // 16 * 16, 16)
+            active_wide[...] = active_ref[m, pl.ds(base, 16), :].astype(WIDE)
+            rows_ref[p : p + 1] = active_wide[pl.ds(starts_ref[p] - base, 1), :]
+        sum_ref[...] += dot(rows_ref[...].astype(LOW), w_ref[m], (1, 1))
+    unit, _ = normalize(sum_ref[...])
+    output = unit * vec_ref[:, G2 : G2 + D] + vec_ref[:, C2 : C2 + D]
+    cls_out[...] = output.astype(LOW).astype(WIDE)
+
+
+def early(where, active, weight, vectors, starts, units):
     few = starts.shape[0]
     return call(
-        partial(narrow_kernel, len(units)),
+        partial(early_kernel, len(units), active.shape[0]),
+        "early",
+        where,
+        [active, weight, vectors, starts, *units],
+        [array(WIDE, few, D)],
+        [pltpu.VMEM((16, D), WIDE), pltpu.VMEM((few, D), WIDE), pltpu.VMEM((few, D), WIDE)],
+        limit=8,
+    )
+
+
+def narrow_kernel(row, where, active_ref, w_ref, vec_ref, unit_ref, out, unit_out, inverse_out):
+    at = slice(row * L, (row + 1) * L)
+    value = unit_ref[...] * vec_ref[:, G1 : G1 + D] + (
+        vec_ref[:, C1 : C1 + D] + vec_ref[:, B2 : B2 + D]
+    )
+    for m in range(w_ref.shape[0]):
+        value += dot(active_ref[m, at], w_ref[m], (1, 1))
+    unit, inverse = normalize(value)
+    unit_out[...] = unit
+    inverse_out[...] = inverse
+    out[...] = (unit * vec_ref[:, G2 : G2 + D] + vec_ref[:, C2 : C2 + D]).astype(LOW)
+
+
+def narrow(where, row, active, weight, vectors, unit, wait_for=()):
+    return call(
+        partial(narrow_kernel, row),
         "narrow",
         where,
-        [active, weight, vectors, starts, *units],
-        [
-            array(LOW, tokens, D),
-            array(WIDE, tokens, D),
-            array(WIDE, tokens, 1),
-            array(WIDE, few, D),
-        ],
-        [pltpu.VMEM((tokens, D), WIDE)],
+        [active, weight, vectors, unit],
+        [array(LOW, L, D), array(WIDE, L, D), array(WIDE, L, 1)],
+        wait_for=wait_for,
     )
 
 
 def contrast_kernel(
-    where, cot_ref, unit_ref, inverse_ref, vec_ref, starts_ref,
-    own_ref, all_ref, ids_ref, ids_own_ref, partners_own_ref,
-    grad_out, low_out, bias_out, gain_out, shift_out, y_ref,
+    rows, where, cot_ref, vec_ref, starts_ref, own_ref, all_ref, ids_ref, ids_own_ref,
+    partners_own_ref, *refs
 ):
+    units, inverses, refs = refs[:rows], refs[rows : 2 * rows], refs[2 * rows :]
+    (grad_out, low_out, bias_out, gain_out, shift_out, y_ref) = refs
     scale = 2.0 / math.sqrt(D)
     everyone = all_ref[...]
     own = own_ref[...].astype(LOW)
@@ -477,25 +565,26 @@
         ref[...] = jnp.zeros_like(ref)
     for part in range(y_ref.shape[0] // PART):
         at = slice(part * PART, (part + 1) * PART)
+        row, inner = part * PART // L, slice(part * PART % L, part * PART % L + PART)
         grad = y_ref[at]
-        unit = unit_ref[at]
+        unit = units[row][inner]
         gain_out[...] += column_sum(grad * unit)
         shift_out[...] += column_sum(grad)
-        back = norm_back(grad, unit, inverse_ref[at], vec_ref[:, G2 : G2 + D])
+        back = norm_back(grad, unit, inverses[row][inner], vec_ref[:, G2 : G2 + D])
         grad_out[at] = back
         low = back.astype(LOW)
         low_out[at] = low
         bias_out[...] += column_sum(low.astype(WIDE))
 
 
-def contrast(where, cotangent, unit, inverse, vectors, starts, own, everyone, ids, ids_own, partners_own):
+def contrast(where, cotangent, units, inverses, vectors, starts, own, everyone, ids, ids_own, partners_own):
     tokens = cotangent.shape[0]
     return call(
-        contrast_kernel,
+        partial(contrast_kernel, len(units)),
         "contrast",
         where,
         [
-            cotangent, unit, inverse, vectors, starts, own, everyone, ids, ids_own, partners_own,
+            cotangent, vectors, starts, own, everyone, ids, ids_own, partners_own, *units, *inverses,
         ],
         [
             array(WIDE, tokens, D),
@@ -562,7 +651,6 @@
 def middle_kernel(blocks, rows, where, hidden_ref, up_ref, sum_ref, vec_ref, w_ref, *refs):
     units, inverses, refs = refs[:rows], refs[rows : 2 * rows], refs[2 * rows :]
     grad_out, low_out, bias_out, gain_out, shift_out, context_out = refs
-    width = D // blocks
     for ref in (bias_out, gain_out, shift_out):
         ref[...] = jnp.zeros_like(ref)
     for row in range(rows):
@@ -587,7 +675,9 @@
             low_out[outer] = low
             bias_out[...] += column_sum(low.astype(WIDE))
         for m in range(blocks):
-            context_out[row * blocks + m] = dot(low_out[at], w_ref[m, :, :width]).astype(LOW)
+            context_out[row * blocks + m] = dot(
+                low_out[at], w_ref[block_of(m, where), :, OUT:]
+            ).astype(LOW)
 
 
 def middle(where, hidden_grad, up, sum_grad, units, inverses, vectors, weight, wait_for=()):
@@ -604,99 +694,101 @@
             array(WIDE, 1, D),
             array(WIDE, 1, D),
             array(WIDE, 1, D),
-            array(LOW, rows * blocks, L, D // blocks),
+            array(LOW, rows * blocks, L, D - OUT),
         ],
         wait_for=wait_for,
     )
 
 
-def attend_back_kernel(blocks, row, where, q_ref, k_ref, v_ref, grad_ref, out):
-    heads = HEADS // blocks
-    width = HD * heads
-
-    def block(m, carry):
-        out[m, :, :width] = jnp.zeros((L, width), LOW)
-        for h in range(heads):
-            queries, keys, value = q_ref[m * heads + h], k_ref[m * heads + h], v_ref[m * heads + h]
-            grad = grad_ref[row * blocks + m, :, h * HD : (h + 1) * HD]
-            weights = jnp.exp(dot(keys, queries, (1, 1)))
-            weight_grad = dot(value, grad, (1, 1))
+def attend_back_kernel(blocks, row, chosen, where, q_ref, k_ref, v_ref, log_ref, grad_ref, out):
+    lanes = lax.broadcasted_iota(jnp.int32, (L, TILE), 1)
+    low_half = lanes < HD
+
+    def block(i, carry):
+        key_grads = []
+        for h in range(HEADS_BLOCK):
+            n = i * HEADS_BLOCK + h
+            queries, keys = q_ref[n], k_ref[n]
+            at = (h + 1) // 2 * TILE
+            grad = grad_ref[row * blocks + chosen[0] + i, :, at : at + TILE]
+            weights = jnp.exp(dot(keys, queries, (1, 1)) - log_ref[n])
+            weight_grad = dot(v_ref[n], grad, (1, 1))
             middle_sum = jnp.sum(weight_grad * weights, axis=0, keepdims=True)
             score_grad = (weights * (weight_grad - middle_sum)).astype(LOW)
-            at = width + h * HD
-            query_grad = (dot(keys.T, score_grad)[:HD] * HD ** (-0.5)).T
-            out[m, :, at : at + HD] = query_grad.astype(LOW)
-            out[m, :, at + width : at + width + HD] = dot(score_grad, queries)[:, :HD].astype(LOW)
-            out[m, :, at + 2 * width : at + 2 * width + HD] = dot(
-                weights.astype(LOW), grad
-            ).astype(LOW)
+            query_grad = (dot(keys.T, score_grad) * HD ** (-0.5)).T
+            value_grad = dot(weights.astype(LOW), grad)
+            key_grads.append(dot(score_grad, queries))
+            pair = (value_grad, query_grad) if SIDES[h] else (query_grad, value_grad)
+            out[i, :, h * TILE : (h + 1) * TILE] = jnp.where(low_half, *pair).astype(LOW)
+        pair = jnp.where(low_half, key_grads[0], key_grads[1])
+        out[i, :, KEYS : KEYS + TILE] = pair.astype(LOW)
+        out[i, :, OUT : OUT + TILE] = jnp.where(low_half, key_grads[2], 0.0).astype(LOW)
+        out[i, :, OUT + TILE :] = jnp.zeros((L, D - OUT - TILE), LOW)
         return carry
 
-    lax.fori_loop(0, blocks, block, 0)
-
-
-def attend_back(where, row, blocks, queries, keys, values, context_grad, wait_for=()):
-    return call(
-        partial(attend_back_kernel, blocks, row),
+    lax.fori_loop(0, len(chosen), block, 0)
+
+
+def attend_back(where, row, blocks, chosen, queries, keys, values, logs, context_grad, wait_for=()):
+    return call(
+        partial(attend_back_kernel, blocks, row, chosen),
         "attend_back",
         where,
-        [queries, keys, values, context_grad],
-        [array(LOW, blocks, L, D)],
+        [queries, keys, values, logs, context_grad],
+        [array(LOW, len(chosen), L, D)],
         wait_for=wait_for,
     )
 
 
-def attention_grad_kernel(summand, rows, where, x_ref, low_ref, *refs):
+def attention_grad_kernel(summand, rows, chosen, where, x_ref, low_ref, *refs):
     grads, contexts, refs = refs[:rows], refs[rows : 2 * rows], refs[2 * rows :]
     bias_out, outs, (x_turned, low_turned) = refs[0], refs[1:-2], refs[-2:]
     x_turned[...] = x_ref[...].T
     low_turned[...] = low_ref[...].T
-    width = contexts[0].shape[2]
-    for g in range(summand.blocks):
-        m = block_of(g, where)
+    for i, g in enumerate(chosen):
         bias = jnp.zeros((1, D), WIDE)
         value = jnp.zeros((D, D), WIDE)
-        own = jnp.zeros((D, width), WIDE)
+        own = jnp.zeros((D, D - OUT), WIDE)
         for row in range(rows):
             at = slice(row * L, (row + 1) * L)
-            grad = grads[row][m]
+            grad = grads[row][i]
             bias += column_sum(grad.astype(WIDE))
             value += dot(x_turned[:, at], grad)
-            own += dot(low_turned[:, at], contexts[row][m])
-        bias_out[m] = bias
-        value = jnp.concatenate([own, value[:, width:]], axis=1).astype(LOW)
+            own += dot(low_turned[:, at], contexts[row][i])
+        bias_out[i] = bias
+        value = jnp.concatenate([value[:, :OUT], value[:, OUT:] + own], axis=1).astype(LOW)
         summand.write(outs, value, g, where)
 
 
-def grad_of_attention(where, inputs, grad_low, grads, contexts, summand, wait_for=()):
+def grad_of_attention(where, chosen, inputs, grad_low, grads, contexts, summand, wait_for=()):
     tokens = inputs.shape[0]
     return call(
-        partial(attention_grad_kernel, summand, len(grads)),
+        partial(attention_grad_kernel, summand, len(grads), chosen),
         "grad_of_attention",
         where,
         [inputs, grad_low, *grads, *contexts],
-        [array(WIDE, summand.blocks, 1, D)] + summand.shapes,
+        [array(WIDE, len(chosen), 1, D)] + summand.shapes[:1],
         [pltpu.VMEM((D, tokens), LOW)] * 2,
         wait_for=wait_for,
     )
 
 
 def input_grad_kernel(rows, where, w_ref, first_ref, *refs):
-    grads, out = refs[:rows], refs[rows]
+    grads, out = refs[:-1], refs[-1]
+    cuts = len(grads) // rows
     for row in range(rows):
         at = slice(row * L, (row + 1) * L)
-        out[at] = first_ref[at]
-
-        def block(m, carry):
-            out[at] += dot(grads[row][m], w_ref[m], (1, 1))
-            return carry
-
-        lax.fori_loop(0, w_ref.shape[0], block, 0)
-
-
-def grad_of_input(where, grads, weight, first_grad, wait_for=()):
-    return call(
-        partial(input_grad_kernel, len(grads)),
+        value = first_ref[at]
+        for c in range(cuts):
+            ref = grads[row * cuts + c]
+            for i in range(ref.shape[0]):
+                value += dot(ref[i], w_ref[block_of(c * ref.shape[0] + i, where)], (1, 1))
+        out[at] = value
+
+
+def grad_of_input(where, rows, grads, weight, first_grad, wait_for=()):
+    return call(
+        partial(input_grad_kernel, rows),
         "grad_of_input",
         where,
         [weight, first_grad, *grads],
@@ -705,23 +797,33 @@
     )
 
 
-def pack_kernel(where, bias_ref, up_ref, *refs):
-    out = refs[-1]
-    blocks = bias_ref.shape[0]
-    width = D // blocks
-    rows = [bias_ref[m] for m in range(blocks)]
-    out[:, :D] = jnp.concatenate([row[:, width : 2 * width] for row in rows], axis=1)
-    out[:, D : 2 * D] = jnp.concatenate([row[:, 3 * width :] for row in rows], axis=1)
+def pack_kernel(cuts, where, *refs):
+    biases, up_ref, others, out = refs[:cuts], refs[cuts], refs[cuts + 1 : -2], refs[-2]
+    rows_ref = refs[-1]
+    each = biases[0].shape[0]
+    blocks = cuts * each
+    for g in range(blocks):
+        rows_ref[block_of(g, where)] = biases[g // each][g % each]
+    rows = [rows_ref[m] for m in range(blocks)]
+    out[:, :D] = jnp.concatenate([query_columns(row) for row in rows], axis=1)
+    out[:, D : 2 * D] = jnp.concatenate([value_columns(row) for row in rows], axis=1)
     units = FF // blocks
     for m in range(blocks):
         out[:, 2 * D + m * units : 2 * D + (m + 1) * units] = up_ref[m]
-    for i, ref in enumerate(refs[:-1]):
+    for i, ref in enumerate(others):
         out[:, TAIL + i * D : TAIL + (i + 1) * D] = ref[...]
 
 
-def pack(where, bias_grad, up_bias_grad, *others):
-    return call(
-        pack_kernel, "pack", where, [bias_grad, up_bias_grad, *others], [array(WIDE, 1, VEC)], limit=8
+def pack(where, biases, up_bias_grad, *others):
+    blocks = up_bias_grad.shape[0]
+    return call(
+        partial(pack_kernel, len(biases)),
+        "pack",
+        where,
+        [*biases, up_bias_grad, *others],
+        [array(WIDE, 1, VEC)],
+        [pltpu.VMEM((blocks, 1, D), WIDE)],
+        limit=8,
     )[0]
 
 
@@ -849,11 +951,10 @@
     own_rows = rows * PASS
     width = D // mp_size
     where = place()
-    weight_shard = jnp.concatenate(
-        [out_weight.T, qkv_weight[0], qkv_weight[1], qkv_weight[2]], axis=1
-    ).astype(LOW)
+    down_turned = down_weight.T
+    weight_shard = arrange(where, qkv_weight, out_weight)
     up_shard = up_weight.astype(LOW)
-    down_shard = down_weight.T.astype(LOW)
+    down_shard = down_turned.astype(LOW)
     local_lengths = lax.dynamic_slice_in_dim(lengths, mp_index * rows, rows, 0)
     inputs = lax.dynamic_slice_in_dim(block_input, mp_index * tokens, tokens, 0)
     segments = passage_ids(local_lengths).reshape(tokens, 1)
@@ -863,19 +964,18 @@
     ids_own = (dp_index * mp_size + mp_index) * own_rows + jnp.arange(own_rows, dtype=jnp.int32)
     ids_all = shared_ids(own_rows)
     vec = vectors.reshape(1, VEC)
-    none = jnp.zeros((mp_size, width), WIDE)
-    bias = jnp.concatenate(
-        [none, vectors[:D].reshape(mp_size, width), none, vectors[D : 2 * D].reshape(mp_size, width)],
-        axis=1,
-    ).reshape(mp_size, 1, D)
+    bias = arrange_bias(where, vec, mp_size)
     bias_up = vectors[2 * D : TAIL].reshape(mp_size, 1, D)
 
     summand = Summand(mp_size, dp_size)
 
-    def attend_row(row, weight, *wait_for):
+    def attend_part(row, chosen, held, weight, *wait_for):
         at = slice(row * L, (row + 1) * L)
-        return attend(where, inputs[at], weight, bias, vec, segments[at], wait_for=wait_for)
-
+        return attend(
+            where, chosen, held, inputs[at], weight, bias, vec, segments[at], wait_for=wait_for
+        )
+
+    halves = [range(mp_size // 2), range(mp_size // 2, mp_size)]
     if on_grid():
         weight_z = gather_z(weight_shard)
         weight_near = gather_near(weight_z)
@@ -884,33 +984,50 @@
         weight_parts = weight_near + weight_far
         weight = settle(where, weight_parts + gather_core(weight_parts))
         up_z = after(up_z, *weight_far)
-        kept = [attend_row(0, weight, *up_z)]
-        up_near = gather_near(up_z, kept[0][-1])
-        down_z = gather_z(after(down_shard, *up_z), kept[0][-1])
-        kept.append(attend_row(1, weight, *up_near, *down_z))
-        up_far = gather_far(up_near, kept[1][-1])
-        up_parts = up_near + up_far
-        up = settle(where, up_parts + gather_core(up_parts))
-        down_near = gather_near(down_z, kept[1][-1])
+        kept = [[None, None] for _ in range(rows)]
+        kept[0][0] = attend_part(0, halves[0], None, weight, *up_z)
+        up_near = gather_near(up_z, kept[0][0][-1])
+        down_z = gather_z(after(down_shard, *up_z), kept[0][0][-1])
+        kept[0][1] = attend_part(0, halves[1], kept[0][0][5], weight, *up_near)
+        kept[1][0] = attend_part(1, halves[0], None, weight, kept[0][1][-1], *down_z)
+        up_far = gather_far(up_near, kept[1][0][-1])
+        up_cores = gather_core(up_near, kept[1][0][-1])
+        down_near = gather_near(after(down_z, *up_near), kept[1][0][-1])
+        kept[1][1] = attend_part(1, halves[1], kept[1][0][5], weight, *up_far)
+        up_cores += gather_core(up_far, kept[1][1][-1])
+        up = settle(where, up_near + up_far + up_cores)
     else:
         weight = gather_plain(weight_shard)
         up = gather_plain(up_shard)
         down_near = []
-        kept = [attend_row(row, weight) for row in range(rows)]
-    queries, keys, values, contexts, units_first, inverses_first, lows, _ = zip(*kept)
+        kept = []
+        for row in range(rows):
+            first = attend_part(row, halves[0], None, weight)
+            kept.append([first, attend_part(row, halves[1], first[5], weight)])
+    units_first, inverses_first, lows = zip(*[kept[row][1][5:8] for row in range(rows)])
     active, slope, widened = widen(where, lows, up, bias_up, wait_for=down_near)
     if on_grid():
         down_far = gather_far(after(down_near, *up_far), widened)
-        down_parts = down_near + down_far
-        down = settle(where, down_parts + gather_core(down_near, widened) + gather_core(down_far))
+        down_cores = gather_core(down_near, widened) + gather_core(down_far)
+        down = settle(where, down_near + down_far + down_cores)
     else:
         down = gather_plain(down_shard)
-    block_output, unit_second, inverse_second, cls_own, _ = narrow(
-        where, active, down, vec, starts, units_first
-    )
-    cls_all = share(cls_own.astype(LOW))
+    cls_own, ended = early(where, active, down, vec, starts, units_first)
+    narrowed = []
+    if on_grid():
+        rounds = share_core(cls_own.astype(LOW))
+        narrowed.append(narrow(where, 0, active, down, vec, units_first[0], (ended, rounds)))
+        rounds = share_plane(rounds, narrowed[0][-1])
+        narrowed.append(narrow(where, 1, active, down, vec, units_first[1], (rounds,)))
+        cls_all = share_line(rounds, narrowed[1][-1])
+    else:
+        for row in range(rows):
+            narrowed.append(narrow(where, row, active, down, vec, units_first[row]))
+        cls_all = share_plain(cls_own.astype(LOW))
+    outputs, units_second, inverses_second, _ = zip(*narrowed)
+    block_output = jnp.concatenate(outputs, axis=0)
     sum_grad, branch_low, down_bias_grad, gain_second_grad, shift_second_grad, _ = contrast(
-        where, cotangent, unit_second, inverse_second, vec, starts, cls_own, cls_all,
+        where, cotangent, units_second, inverses_second, vec, starts, cls_own, cls_all,
         ids_all[None, :], ids_own[:, None], partner_own[:, None],
     )
     *down_part, ended = grad_of_down(where, branch_low, active, summand)
@@ -926,32 +1043,54 @@
         wait_for=(added,) if on_grid() else (),
     )
 
-    def back_row(row, *wait_for):
+    def back_part(row, half, *wait_for):
         return attend_back(
-            where, row, mp_size, queries[row], keys[row], values[row], context_grad, wait_for=wait_for
+            where, row, mp_size, halves[half], *kept[row][half][:4], context_grad, wait_for=wait_for
         )
 
+    def grad_part(half, *wait_for):
+        return grad_of_attention(
+            where, halves[half], inputs, attended_low, [back[row][half] for row in range(rows)],
+            [kept[row][half][4] for row in range(rows)], summand, wait_for=wait_for,
+        )
+
+    back = [[None, None] for _ in range(rows)]
     if on_grid():
         *down_sum, down_added = scatter_far(where, down_sum)
         *up_sum, up_added = scatter_core(where, up_part)
-        first_row, ended = back_row(0, down_added, up_added)
+        back[0][1], ended = back_part(0, 1, down_added, up_added)
+        back[1][1], ended = back_part(1, 1, ended)
+        bias_other, other_part, ended = grad_part(1)
         *down_sum, down_added = scatter_near(where, down_sum, ended)
-        second_row, ended = back_row(1, down_added)
+        back[0][0], ended = back_part(0, 0, ended, down_added)
         *up_sum, up_added = scatter_far(where, up_sum, ended)
-        grads = [first_row, second_row]
-        ties = (up_added,)
+        other_part = send(other_part, CORE)
+        back[1][0], ended = back_part(1, 0, up_added, other_part)
+        down_parts = scatter_z(down_sum, ended)
+        bias_own, own_part, ended = grad_part(0)
+        *attention_sum, added = scatter_core(where, [own_part], arrived=other_part)
+        *up_sum, up_added = scatter_near(where, up_sum, ended, wait_for=(added,))
     else:
-        grads = [back_row(row)[0] for row in range(rows)]
-        ties = ()
-    bias_grad, *attention_part, ended = grad_of_attention(
-        where, inputs, attended_low, grads, contexts, summand, wait_for=ties
-    )
+        for row in range(rows):
+            for half in (0, 1):
+                back[row][half] = back_part(row, half)[0]
+        bias_other, other_part, _ = grad_part(1)
+        bias_own, own_part, _ = grad_part(0)
+    vector_local = pack(
+        where,
+        [bias_own, bias_other],
+        up_bias_grad,
+        out_bias_grad,
+        down_bias_grad,
+        gain_first_grad,
+        shift_first_grad,
+        gain_second_grad,
+        shift_second_grad,
+    )
+    grads = [back[row][half] for row in range(rows) for half in (0, 1)]
     if on_grid():
-        down_parts = scatter_z(down_sum, ended)
-        *up_sum, up_added = scatter_near(where, up_sum, ended)
-        *attention_sum, added = scatter_core(where, attention_part)
         input_grad, ended = grad_of_input(
-            where, grads, weight, first_grad, wait_for=(added, up_added)
+            where, rows, grads, weight, first_grad, wait_for=(added, up_added)
         )
         up_parts = scatter_z(up_sum, ended)
         *attention_sum, _ = scatter_far(where, attention_sum, ended)
@@ -960,22 +1099,12 @@
     else:
         down_parts = [scatter_plain(down_part)]
         up_parts = [scatter_plain(up_part)]
-        attention_parts = [scatter_plain(attention_part)]
-        input_grad, _ = grad_of_input(where, grads, weight, first_grad)
-    vector_local = pack(
-        where,
-        bias_grad,
-        up_bias_grad,
-        out_bias_grad,
-        down_bias_grad,
-        gain_first_grad,
-        shift_first_grad,
-        gain_second_grad,
-        shift_second_grad,
-    )
+        both = jnp.concatenate([own_part[: mp_size // 2], other_part[mp_size // 2 :]])
+        attention_parts = [scatter_plain([both])]
+        input_grad, _ = grad_of_input(where, rows, grads, weight, first_grad)
     down_grad, down_second_new, down_update, down_squares = adapt(
-        "adapt_down", where, down_parts, [lambda g: [(None, g.T)]],
-        [down_first], [down_second], [down_weight],
+        "adapt_down", where, down_parts, [lambda g: [(None, g)]],
+        [down_first.T], [down_second.T], [down_turned],
     )
     up_grad, up_second_new, up_update, up_squares = adapt(
         "adapt_up", where, up_parts, [lambda g: [(None, g)]], [up_first], [up_second], [up_weight]
@@ -988,8 +1117,12 @@
         where,
         attention_parts,
         [
-            lambda g: [(i, g[:, (i + 1) * width : (i + 2) * width]) for i in range(3)],
-            lambda g: [(None, g[:, :width].T)],
+            lambda g: [
+                (0, query_columns(g)),
+                (1, g[:, KEYS : KEYS + width]),
+                (2, value_columns(g)),
+            ],
+            lambda g: [(None, g[:, KEYS + width :].T)],
         ],
         [qkv_first, out_first],
         [qkv_second, out_second],
@@ -1008,7 +1141,7 @@
         )
     )
     vector_grad, sums = summed[:, :VEC], summed[:, VEC:]
-    weights = [qkv_weight, out_weight, up_weight, down_weight]
+    weights = [qkv_weight, out_weight, up_weight, down_turned]
     updates = [qkv_update, out_update, up_update, down_update]
     (
         qkv_new, qkv_copy, out_new, out_copy, up_new, up_copy, down_new, down_copy,
@@ -1023,19 +1156,19 @@
         qkv_grad,
         out_grad,
         up_grad,
-        down_grad,
+        down_grad.T,
         qkv_second_new,
         out_second_new,
         up_second_new,
-        down_second_new,
+        down_second_new.T,
         qkv_new,
         out_new,
         up_new,
-        down_new,
+        down_new.T,
         qkv_copy,
         out_copy,
         up_copy,
-        down_copy,
+        down_copy.T,
         vector_grad.reshape(VEC),
         vector_second_new.reshape(VEC),
         vector_new.reshape(VEC),

time: 336 us -> 298 us (0.89)
  waiting for transfers between devices: 74 us -> 52.8 us
  local copies, waits for them, and re-layouts: 36.1 us -> 17.4 us
    ppermute x71, waiting for transfers between devices: 74 us -> 52.8 us  [send(): return after(lax.ppermute(value, AXES, pairs), *beside)]
    unnamed x159 -> x188, local copies, waits for them, and re-layouts: 29.2 us -> 13.2 us
    pallas_call x29 -> x38, Pallas kernels: 146 us -> 147 us  [call(): pl.pallas_call(body, in_specs=[pl.BlockSpec(memory_space=pltpu.SMEM)] + [...]
  transfers between devices with their start and end apart: 71 -> 71, of which waited for: 26 -> 21; matrix products, arithmetic and copies ran while one was open for 3% -> 2% of each run, Pallas kernels for 35% -> 43%
where the time goes in v3:
time: 298 us; the launch traced here: 295 us
  Pallas kernels  147 us (49%)
  starting transfers between devices  73 us (24%)
  waiting for transfers between devices  52.8 us (18%)
  local copies, waits for them, and re-layouts  17.4 us (6%)
    pallas_call x38, Pallas kernels, call(): pl.pallas_call(body, in_specs=[pl.BlockSpec(memory_space=pltpu.SMEM)] + [...  147 us
    ppermute x71, starting transfers between devices, send(): return after(lax.ppermute(value, AXES, pairs), *beside)  73 us
    ppermute x71, waiting for transfers between devices, send(): return after(lax.ppermute(value, AXES, pairs), *beside)  52.8 us
    unnamed x188, local copies, waits for them, and re-layouts  13.2 us
  transfers between devices with their start and end apart: 71, of which 21 were waited for; matrix products, arithmetic and copies ran while one was open for 2% of the time, Pallas kernels for 43%

profile of v3, /device:TPU:0, one launch (start us, length us, event | category | flops | bytes accessed | tf_op | source)
XLA Modules:
  0.0 294.9 jit_solution(10441959556928887559)
XLA Ops:
  15.4 6.8 %collective-permute-done.2 = bf16[96,768]{1,0:T(8,128)(2,1)S(1)} collective-permute-done((bf16[96,768]{1,0:T(8,128)(2,1)S(1)}, bf16[96,768]{1,0:T(8,128)(2,1)S(1)}, u32[]{:S(2)}, u32[]{:S(2)}) %collective-permute-start.2) | collective-permute-done | bytes 147488 | tf_op jit(solution)/shard_map/ppermute | solution.py:70
  24.6 7.6 %collective-permute-done.4 = bf16[2,96,768]{2,1,0:T(8,128)(2,1)S(1)} collective-permute-done((bf16[2,96,768]{2,1,0:T(8,128)(2,1)S(1)}, bf16[2,96,768]{2,1,0:T(8,128)(2,1)S(1)}, u32[]{:S(2)}, u32[]{:S(2)}) %collective-permute-start.4) | collective-permute-done | bytes 294944 | tf_op jit(solution)/shard_map/ppermute | solution.py:70
  37.4 4.5 %collective-permute-done.11.refs_6_ = bf16[96,768]{1,0:T(8,128)(2,1)S(1)} collective-permute-done((bf16[96,768]{1,0:T(8,128)(2,1)S(1)}, bf16[96,768]{1,0:T(8,128)(2,1)S(1)}, u32[]{:S(2)}, u32[]{:S(2)}) %collective-permute-start.11) | collective-permute-done | bytes 147488 | tf_op jit(solution)/shard_map/ppermute | solution.py:70
  48.1 4.1 %collective-permute-done.13.refs_8_ = bf16[96,768]{1,0:T(8,128)(2,1)S(1)} collective-permute-done((bf16[96,768]{1,0:T(8,128)(2,1)S(1)}, bf16[96,768]{1,0:T(8,128)(2,1)S(1)}, u32[]{:S(2)}, u32[]{:S(2)}) %collective-permute-start.13) | collective-permute-done | bytes 147488 | tf_op jit(solution)/shard_map/ppermute | solution.py:70
  61.3 6.2 %attend.4 = (bf16[6,512,128]{2,1,0:T(8,128)(2,1)S(1)}, bf16[6,512,128]{2,1,0:T(8,128)(2,1)S(1)}, bf16[6,512,128]{2,1,0:T(8,128)(2,1)S(1)}, f32[6,1,512]{2,1,0:T(...) custom-call(s32[5]{0:T(128)S(1)} %stack.77.where, ...), custom_call_target="tpu_custom_call" | custom-call | flops 30000001024 | bytes 1048576 | tf_op jit(solution)/shard_map/attend/pallas_call | solution.py:223
  69.6 6.4 %attend.5 = (bf16[6,512,128]{2,1,0:T(8,128)(2,1)S(1)}, bf16[6,512,128]{2,1,0:T(8,128)(2,1)S(1)}, bf16[6,512,128]{2,1,0:T(8,128)(2,1)S(1)}, f32[6,1,512]{2,1,0:T(...) custom-call(s32[5]{0:T(128)S(1)} %stack.77.where, ...), custom_call_target="tpu_custom_call" | custom-call | flops 30000001024 | bytes 1048576 | tf_op jit(solution)/shard_map/attend/pallas_call | solution.py:223
  79.4 5.9 %attend.6 = (bf16[6,512,128]{2,1,0:T(8,128)(2,1)S(1)}, bf16[6,512,128]{2,1,0:T(8,128)(2,1)S(1)}, bf16[6,512,128]{2,1,0:T(8,128)(2,1)S(1)}, f32[6,1,512]{2,1,0:T(...) custom-call(s32[5]{0:T(128)S(1)} %stack.77.where, ...), custom_call_target="tpu_custom_call" | custom-call | flops 30000001024 | bytes 1048576 | tf_op jit(solution)/shard_map/attend/pallas_call | solution.py:223
  90.2 6.7 %attend.7 = (bf16[6,512,128]{2,1,0:T(8,128)(2,1)S(1)}, bf16[6,512,128]{2,1,0:T(8,128)(2,1)S(1)}, bf16[6,512,128]{2,1,0:T(8,128)(2,1)S(1)}, f32[6,1,512]{2,1,0:T(...) custom-call(s32[5]{0:T(128)S(1)} %stack.77.where, ...), custom_call_target="tpu_custom_call" | custom-call | flops 30000001024 | bytes 1048576 | tf_op jit(solution)/shard_map/attend/pallas_call | solution.py:223
  100.7 10.3 %widen.1 = (bf16[4,1024,768]{2,1,0:T(8,128)(2,1)S(1)}, bf16[4,1024,768]{2,1,0:T(8,128)(2,1)S(1)}, f32[8,128]{1,0:T(8,128)}) custom-call(s32[5]{0:T(128)S(1)} %stack.77.where, bf16[512,768]{1,0:T(8,128)(2,1)S(1)} %get-tuple-element.236.refs_0_.refs_3_, bf16[512,768]{1,0:T(8,128)(2,1)S(1)} %get-tuple-element.246.refs_1_.refs_4_, ...), custom_call_target="tpu_custom_call" | custom-call | flops 30000001024 | bytes 1048576 | tf_op jit(solution)/shard_map/widen/pallas_call | solution.py:223
  129.6 4.2 %narrow.2 = (bf16[512,768]{1,0:T(8,128)(2,1)S(1)}, f32[512,768]{1,0:T(8,128)S(1)}, f32[512,1]{1,0:T(8,128)S(1)}, f32[8,128]{1,0:T(8,128)}) custom-call(s32[5]{0:T(128)S(1)} %stack.77.where, bf16[4,1024,768]{2,1,0:T(8,128)(2,1)S(1)} %bitcast.103, bf16[4,768,768]{2,1,0:T(8,128)(2,1)S(1)} %bitcast.99, f32[1,9216]{1,0:T(1,128)S(1)} %bitcast.72, ...), custom_call_target="tpu_custom_call" | custom-call | flops 30000001024 | bytes 1048576 | tf_op jit(solution)/shard_map/narrow/pallas_call | solution.py:223
  139.0 4.2 %narrow.3 = (bf16[512,768]{1,0:T(8,128)(2,1)S(1)}, f32[512,768]{1,0:T(8,128)S(1)}, f32[512,1]{1,0:T(8,128)S(1)}, f32[8,128]{1,0:T(8,128)}) custom-call(s32[5]{0:T(128)S(1)} %stack.77.where, bf16[4,1024,768]{2,1,0:T(8,128)(2,1)S(1)} %bitcast.103, bf16[4,768,768]{2,1,0:T(8,128)(2,1)S(1)} %bitcast.100, f32[1,9216]{1,0:T(1,128)S(1)} %bitcast.73, ...), custom_call_target="tpu_custom_call" | custom-call | flops 30000001024 | bytes 1048576 | tf_op jit(solution)/shard_map/narrow/pallas_call | solution.py:223
  149.1 5.7 %grad_of_down.1 = (bf16[2,2,2,2,96,768]{5,4,3,2,1,0:T(8,128)(2,1)S(1)}, bf16[2,2,2,2,96,768]{5,4,3,2,1,0:T(8,128)(2,1)S(1)}, f32[8,128]{1,0:T(8,128)S(1)}) custom-call(s32[5]{0:T(128)S(1)} %stack.77.where, bf16[1024,768]{1,0:T(8,128)(2,1)S(1)} %get-tuple-element.286.refs_0_, bf16[4,1024,768]{2,1,0:T(8,128)(2,1)S(1)} %bitcast.103), custom_call_target="tpu_custom_call" | custom-call | flops 30000001024 | bytes 1048576 | tf_op jit(solution)/shard_map/grad_of_down/pallas_call | solution.py:223
  154.9 11.6 %grad_of_up.1 = (bf16[4,1024,768]{2,1,0:T(8,128)(2,1)S(1)}, f32[4,1,768]{2,1,0:T(1,128)S(1)}, bf16[2,2,2,2,96,768]{5,4,3,2,1,0:T(8,128)(2,1)S(1)}, bf16[2,2,2,2,96,768]{5,4,3,2,1,0:T(8,128)(2,1)S(1)}, f32[8,128]{1,0:T(8,128)}) custom-call(s32[5]{0:T(128)S(1)} %stack.77.where, bf16[1024,768]{1,0:T(8,128)(2,1)S(1)} %get-tuple-element.286.refs_0_, ...), custom_call_target="tpu_custom_call" | custom-call | flops 30000001024 | bytes 1048576 | tf_op jit(solution)/shard_map/grad_of_up/pallas_call | solution.py:223
  175.2 11.0 %middle.1 = (f32[1024,768]{1,0:T(8,128)S(1)}, bf16[1024,768]{1,0:T(8,128)(2,1)S(1)}, f32[1,768]{1,0:T(1,128)S(1)}, f32[1,768]{1,0:T(1,128)S(1)}, f32[1,768]{1,0:...) custom-call(s32[5]{0:T(128)S(1)} %stack.77.where, ...), custom_call_target="tpu_custom_call" | custom-call | flops 30000001024 | bytes 1048576 | tf_op jit(solution)/shard_map/middle/pallas_call | solution.py:223
  189.2 6.2 %attend_back.4 = (bf16[2,512,768]{2,1,0:T(8,128)(2,1)S(1)}, f32[8,128]{1,0:T(8,128)S(1)}) custom-call(s32[5]{0:T(128)S(1)} %stack.77.where, bf16[6,512,128]{2,1,0:T(8,128)(2,1)S(1)} %copy-done.43, bf16[6,512,128]{2,1,0:T(8,128)(2,1)S(1)} %copy-done.45, bf16[6,512,128]{2,1,0:T(8,128)(2,1)S(1)} %copy-done.47, f32[6,1,512]{2,1,0:T(1,128)S(1)} %get-tuple-element.306.refs_3_, ...), custom_call_target="tpu_custom_call" | custom-call | flops 30000001024 | bytes 1048576 | tf_op jit(solution)/shard_map/attend_back/pallas_call | solution.py:223
  195.4 6.4 %attend_back.5 = (bf16[2,512,768]{2,1,0:T(8,128)(2,1)S(1)}, f32[8,128]{1,0:T(8,128)}) custom-call(s32[5]{0:T(128)S(1)} %stack.77.where, bf16[6,512,128]{2,1,0:T(8,128)(2,1)S(1)} %copy-done.49, bf16[6,512,128]{2,1,0:T(8,128)(2,1)S(1)} %copy-done.51, bf16[6,512,128]{2,1,0:T(8,128)(2,1)S(1)} %copy-done.53, f32[6,1,512]{2,1,0:T(1,128)S(1)} %get-tuple-element.319.refs_3_, ...), custom_call_target="tpu_custom_call" | custom-call | flops 30000001024 | bytes 1048576 | tf_op jit(solution)/shard_map/attend_back/pallas_call | solution.py:223
  201.9 4.1 %grad_of_attention.2 = (f32[2,1,768]{2,1,0:T(1,128)S(1)}, bf16[2,2,2,2,96,768]{5,4,3,2,1,0:T(8,128)(2,1)S(1)}, f32[8,128]{1,0:T(8,128)S(1)}) custom-call(s32[5]{0:T(128)S(1)} %stack.77.where, bf16[1024,768]{1,0:T(8,128)(2,1)S(1)} %constant_dynamic-slice_fusion.3.refs_0_, bf16[1024,768]{1,0:T(8,128)(2,1)S(1)} %get-tuple-element.302.refs_1_, ...), custom_call_target="tpu_custom_call" | custom-call | flops 30000001024 | bytes 1048576 | tf_op jit(solution)/shard_map/grad_of_attention/pallas_call | solution.py:223
  207.8 6.2 %attend_back.6 = (bf16[2,512,768]{2,1,0:T(8,128)(2,1)S(1)}, f32[8,128]{1,0:T(8,128)}) custom-call(s32[5]{0:T(128)S(1)} %stack.77.where, bf16[6,512,128]{2,1,0:T(8,128)(2,1)S(1)} %copy-done.61, bf16[6,512,128]{2,1,0:T(8,128)(2,1)S(1)} %copy-done.63, bf16[6,512,128]{2,1,0:T(8,128)(2,1)S(1)} %copy-done.65, f32[6,1,512]{2,1,0:T(1,128)S(1)} %get-tuple-element.300.refs_3_, ...), custom_call_target="tpu_custom_call" | custom-call | flops 30000001024 | bytes 1048576 | tf_op jit(solution)/shard_map/attend_back/pallas_call | solution.py:223
  222.3 6.5 %attend_back.7 = (bf16[2,512,768]{2,1,0:T(8,128)(2,1)S(1)}, f32[8,128]{1,0:T(8,128)}) custom-call(s32[5]{0:T(128)S(1)} %stack.77.where, bf16[6,512,128]{2,1,0:T(8,128)(2,1)S(1)} %copy-done.55, bf16[6,512,128]{2,1,0:T(8,128)(2,1)S(1)} %copy-done.57, bf16[6,512,128]{2,1,0:T(8,128)(2,1)S(1)} %copy-done.59, f32[6,1,512]{2,1,0:T(1,128)S(1)} %get-tuple-element.336.refs_3_, ...), custom_call_target="tpu_custom_call" | custom-call | flops 30000001024 | bytes 1048576 | tf_op jit(solution)/shard_map/attend_back/pallas_call | solution.py:223
  228.9 4.6 %grad_of_attention.3 = (f32[2,1,768]{2,1,0:T(1,128)S(1)}, bf16[2,2,2,2,96,768]{5,4,3,2,1,0:T(8,128)(2,1)S(1)}, f32[8,128]{1,0:T(8,128)}) custom-call(s32[5]{0:T(128)S(1)} %stack.77.where, bf16[1024,768]{1,0:T(8,128)(2,1)S(1)} %constant_dynamic-slice_fusion.3.refs_0_, bf16[1024,768]{1,0:T(8,128)(2,1)S(1)} %get-tuple-element.302.refs_1_, ...), custom_call_target="tpu_custom_call" | custom-call | flops 30000001024 | bytes 1048576 | tf_op jit(solution)/shard_map/grad_of_attention/pallas_call | solution.py:223
  241.8 7.4 %grad_of_input.1 = (f32[1024,768]{1,0:T(8,128)}, f32[8,128]{1,0:T(8,128)}) custom-call(s32[5]{0:T(128)S(1)} %stack.77.where, bf16[4,768,768]{2,1,0:T(8,128)(2,1)S(1)} %bitcast.93, f32[1024,768]{1,0:T(8,128)S(1)} %get-tuple-element.296.refs_1_, bf16[2,512,768]{2,1,0:T(8,128)(2,1)S(1)} %get-tuple-element.332.refs_2_, bf16[2,512,768]{2,1,0:T(8,128)(2,1)S(1)} %copy-done.35, ...), custom_call_target="tpu_custom_call" | custom-call | flops 30000001024 | bytes 1048576 | tf_op jit(solution)/shard_map/grad_of_input/pallas_call | solution.py:223
  255.4 3.5 %collective-permute-done.53.refs_2_ = bf16[2,96,768]{2,1,0:T(8,128)(2,1)S(1)} collective-permute-done((bf16[2,96,768]{2,1,0:T(8,128)(2,1)S(1)}, bf16[2,96,768]{2,1,0:T(8,128)(2,1)S(1)}, u32[]{:S(2)}, u32[]{:S(2)}) %collective-permute-start.53) | collective-permute-done | bytes 294944 | tf_op jit(solution)/shard_map/ppermute | solution.py:70
  269.1 3.5 %collective-permute-done.56.refs_2_ = bf16[96,768]{1,0:T(8,128)(2,1)S(1)} collective-permute-done((bf16[96,768]{1,0:T(8,128)(2,1)S(1)}, bf16[96,768]{1,0:T(8,128)(2,1)S(1)}, u32[]{:S(2)}, u32[]{:S(2)}) %collective-permute-start.56) | collective-permute-done | bytes 147488 | tf_op jit(solution)/shard_map/ppermute | solution.py:70
  288.0 3.9 %collective-permute-done.68 = f32[1,9344]{1,0:T(1,128)S(1)} collective-permute-done((f32[1,9344]{1,0:T(1,128)S(1)}, f32[1,9344]{1,0:T(1,128)S(1)}, u32[]{:S(2)}, u32[]{:S(2)}) %collective-permute-start.68) | collective-permute-done | bytes 37408 | tf_op jit(solution)/shard_map/ppermute | solution.py:70
  (395 shorter events, 144.9 us)
Async XLA Ops:
  24.0 19.9 %collective-permute-start.5 = (bf16[4,96,768]{2,1,0:T(8,128)(2,1)S(1)}, bf16[4,96,768]{2,1,0:T(8,128)(2,1)S(1)}, u32[]{:S(2)}, u32[]{:S(2)}) collective-permute-start(bf16[4,96,768]{2,1,0:T(8,128)(2,1)S(1)} %pad_maximum_fusion.1.refs_0_), channel_id=1, source_target_pairs={{0,2},{1,3},{2,0},{3,1},{4,6},{5,7},{6,4},{7,5},{8,10},{9,11},{10,... | collective-permute-start | bytes 1769480 | tf_op jit(solution)/shard_map/ppermute | solution.py:70
  52.2 23.8 %collective-permute-start.16 = (bf16[96,768]{1,0:T(8,128)(2,1)S(1)}, bf16[96,768]{1,0:T(8,128)(2,1)S(1)}, u32[]{:S(2)}, u32[]{:S(2)}) collective-permute-start(bf16[96,768]{1,0:T(8,128)(2,1)S(1)} %bitcast_convert_fusion.refs_6_), channel_id=1, source_target_pairs={{0,8},{1,9},{2,10},{3,11},{4,12},{5,13},{6,14},{7,15},{8,16},{9,17... | collective-permute-start | bytes 442376 | tf_op jit(solution)/shard_map/ppermute | solution.py:70
  52.3 23.8 %collective-permute-start.17 = (bf16[96,768]{1,0:T(8,128)(2,1)S(1)}, bf16[96,768]{1,0:T(8,128)(2,1)S(1)}, u32[]{:S(2)}, u32[]{:S(2)}) collective-permute-start(bf16[96,768]{1,0:T(8,128)(2,1)S(1)} %bitcast_convert_fusion.refs_6_), channel_id=1, source_target_pairs={{0,16},{1,17},{2,18},{3,19},{4,20},{5,21},{6,22},{7,23},{8,24},{9,... | collective-permute-start | bytes 442376 | tf_op jit(solution)/shard_map/ppermute | solution.py:70
  55.0 21.2 %collective-permute-start.18 = (bf16[96,768]{1,0:T(8,128)(2,1)S(1)}, bf16[96,768]{1,0:T(8,128)(2,1)S(1)}, u32[]{:S(2)}, u32[]{:S(2)}) collective-permute-start(bf16[96,768]{1,0:T(8,128)(2,1)S(1)} %bitcast_convert_fusion.refs_6_), channel_id=1, source_target_pairs={{0,24},{1,25},{2,26},{3,27},{4,28},{5,29},{6,30},{7,31},{8,0},{9,1... | collective-permute-start | bytes 442376 | tf_op jit(solution)/shard_map/ppermute | solution.py:70
  68.4 21.2 %collective-permute-start.19 = (bf16[4,96,768]{2,1,0:T(8,128)(2,1)S(1)}, bf16[4,96,768]{2,1,0:T(8,128)(2,1)S(1)}, u32[]{:S(2)}, u32[]{:S(2)}) collective-permute-start(bf16[4,96,768]{2,1,0:T(8,128)(2,1)S(1)} %get-tuple-element.508.refs_6_.refs_0_), channel_id=1, source_target_pairs={{0,2},{1,3},{2,0},{3,1},{4,6},{5,7},{6,4},{7,5},{8,10},{9,11},{10,... | collective-permute-start | bytes 1769480 | tf_op jit(solution)/shard_map/ppermute | solution.py:70
  69.0 20.6 %collective-permute-start.20 = (bf16[4,96,768]{2,1,0:T(8,128)(2,1)S(1)}, bf16[4,96,768]{2,1,0:T(8,128)(2,1)S(1)}, u32[]{:S(2)}, u32[]{:S(2)}) collective-permute-start(bf16[4,96,768]{2,1,0:T(8,128)(2,1)S(1)} %get-tuple-element.509.refs_7_.refs_1_), channel_id=1, source_target_pairs={{0,4},{1,5},{2,6},{3,7},{4,0},{5,1},{6,2},{7,3},{8,12},{9,13},{10,... | collective-permute-start | bytes 1769480 | tf_op jit(solution)/shard_map/ppermute | solution.py:70
  76.1 20.9 %collective-permute-start.21 = (bf16[4,96,768]{2,1,0:T(8,128)(2,1)S(1)}, bf16[4,96,768]{2,1,0:T(8,128)(2,1)S(1)}, u32[]{:S(2)}, u32[]{:S(2)}) collective-permute-start(bf16[4,96,768]{2,1,0:T(8,128)(2,1)S(1)} %get-tuple-element.508.refs_6_.refs_0_), channel_id=1, source_target_pairs={{0,1},{1,0},{2,3},{3,2},{4,5},{5,4},{6,7},{7,6},{8,9},{9,8},{10,11... | collective-permute-start | bytes 1769480 | tf_op jit(solution)/shard_map/ppermute | solution.py:70
  89.0 30.1 %collective-permute-start.29 = (bf16[4,96,768]{2,1,0:T(8,128)(2,1)S(1)}, bf16[4,96,768]{2,1,0:T(8,128)(2,1)S(1)}, u32[]{:S(2)}, u32[]{:S(2)}) collective-permute-start(bf16[4,96,768]{2,1,0:T(8,128)(2,1)S(1)} %pad_maximum_fusion.5.refs_4_.refs_0_), channel_id=1, source_target_pairs={{0,1},{1,0},{2,3},{3,2},{4,5},{5,4},{6,7},{7,6},{8,9},{9,8},{10,11... | collective-permute-start | bytes 1769480 | tf_op jit(solution)/shard_map/ppermute | solution.py:70
  97.0 22.1 %collective-permute-start.30 = (bf16[4,96,768]{2,1,0:T(8,128)(2,1)S(1)}, bf16[4,96,768]{2,1,0:T(8,128)(2,1)}, u32[]{:S(2)}, u32[]{:S(2)}) collective-permute-start(bf16[4,96,768]{2,1,0:T(8,128)(2,1)S(1)} %pad_maximum_fusion.6.refs_5_.refs_1_), channel_id=1, source_target_pairs={{0,1},{1,0},{2,3},{3,2},{4,5},{5,4},{6,7},{7,6},{8,9},{9,8},{10,11... | collective-permute-start | bytes 1769480 | tf_op jit(solution)/shard_map/ppermute | solution.py:70
  97.2 19.3 %collective-permute-start.27 = (bf16[4,96,768]{2,1,0:T(8,128)(2,1)S(1)}, bf16[4,96,768]{2,1,0:T(8,128)(2,1)}, u32[]{:S(2)}, u32[]{:S(2)}) collective-permute-start(bf16[4,96,768]{2,1,0:T(8,128)(2,1)S(1)} %pad_maximum_fusion.5.refs_4_.refs_0_), channel_id=1, source_target_pairs={{0,2},{1,3},{2,0},{3,1},{4,6},{5,7},{6,4},{7,5},{8,10},{9,11},{10,... | collective-permute-start | bytes 1769480 | tf_op jit(solution)/shard_map/ppermute | solution.py:70
  98.7 17.7 %collective-permute-start.28 = (bf16[4,96,768]{2,1,0:T(8,128)(2,1)S(1)}, bf16[4,96,768]{2,1,0:T(8,128)(2,1)}, u32[]{:S(2)}, u32[]{:S(2)}) collective-permute-start(bf16[4,96,768]{2,1,0:T(8,128)(2,1)S(1)} %pad_maximum_fusion.6.refs_5_.refs_1_), channel_id=1, source_target_pairs={{0,4},{1,5},{2,6},{3,7},{4,0},{5,1},{6,2},{7,3},{8,12},{9,13},{10,... | collective-permute-start | bytes 1769480 | tf_op jit(solution)/shard_map/ppermute | solution.py:70
  168.1 18.1 %collective-permute-start.41 = (bf16[2,2,96,768]{3,2,1,0:T(8,128)(2,1)S(1)}, bf16[2,2,96,768]{3,2,1,0:T(8,128)(2,1)S(1)}, u32[]{:S(2)}, u32[]{:S(2)}) collective-permute-start(bf16[2,2,96,768]{3,2,1,0:T(8,128)(2,1)S(1)} %get-tuple-element.309), channel_id=1, source_target_pairs={{0,2},{1,3},{2,0},{3,1},{4,6},{5,7},{6,4},{7,5},{8,10},{9,11},{10,... | collective-permute-start | bytes 1769480 | tf_op jit(solution)/shard_map/ppermute | solution.py:70
  168.7 17.5 %collective-permute-start.42 = (bf16[2,2,96,768]{3,2,1,0:T(8,128)(2,1)S(1)}, bf16[2,2,96,768]{3,2,1,0:T(8,128)(2,1)S(1)}, u32[]{:S(2)}, u32[]{:S(2)}) collective-permute-start(bf16[2,2,96,768]{3,2,1,0:T(8,128)(2,1)S(1)} %get-tuple-element.310), channel_id=1, source_target_pairs={{0,4},{1,5},{2,6},{3,7},{4,0},{5,1},{6,2},{7,3},{8,12},{9,13},{10,... | collective-permute-start | bytes 1769480 | tf_op jit(solution)/shard_map/ppermute | solution.py:70
  173.0 41.0 %collective-permute-start.46 = (bf16[2,2,96,768]{3,2,1,0:T(8,128)(2,1)}, bf16[2,2,96,768]{3,2,1,0:T(8,128)(2,1)}, u32[]{:S(2)}, u32[]{:S(2)}) collective-permute-start(bf16[2,2,96,768]{3,2,1,0:T(8,128)(2,1)} %get-tuple-element.339), channel_id=1, source_target_pairs={{0,2},{1,3},{2,0},{3,1},{4,6},{5,7},{6,4},{7,5},{8,10},{9,11},{10,... | collective-permute-start | bytes 1769480 | tf_op jit(solution)/shard_map/ppermute | solution.py:70
  173.6 40.4 %collective-permute-start.47 = (bf16[2,2,96,768]{3,2,1,0:T(8,128)(2,1)}, bf16[2,2,96,768]{3,2,1,0:T(8,128)(2,1)}, u32[]{:S(2)}, u32[]{:S(2)}) collective-permute-start(bf16[2,2,96,768]{3,2,1,0:T(8,128)(2,1)} %get-tuple-element.342), channel_id=1, source_target_pairs={{0,4},{1,5},{2,6},{3,7},{4,0},{5,1},{6,2},{7,3},{8,12},{9,13},{10,... | collective-permute-start | bytes 1769480 | tf_op jit(solution)/shard_map/ppermute | solution.py:70
  187.1 19.1 %collective-permute-start.44 = (bf16[2,96,768]{2,1,0:T(8,128)(2,1)S(1)}, bf16[2,96,768]{2,1,0:T(8,128)(2,1)S(1)}, u32[]{:S(2)}, u32[]{:S(2)}) collective-permute-start(bf16[2,96,768]{2,1,0:T(8,128)(2,1)S(1)} %get-tuple-element.327), channel_id=1, source_target_pairs={{0,4},{1,5},{2,6},{3,7},{4,0},{5,1},{6,2},{7,3},{8,12},{9,13},{10,... | collective-permute-start | bytes 884744 | tf_op jit(solution)/shard_map/ppermute | solution.py:70
  187.9 18.3 %collective-permute-start.45 = (bf16[2,96,768]{2,1,0:T(8,128)(2,1)S(1)}, bf16[2,96,768]{2,1,0:T(8,128)(2,1)S(1)}, u32[]{:S(2)}, u32[]{:S(2)}) collective-permute-start(bf16[2,96,768]{2,1,0:T(8,128)(2,1)S(1)} %get-tuple-element.329), channel_id=1, source_target_pairs={{0,2},{1,3},{2,0},{3,1},{4,6},{5,7},{6,4},{7,5},{8,10},{9,11},{10,... | collective-permute-start | bytes 884744 | tf_op jit(solution)/shard_map/ppermute | solution.py:70
  215.8 17.7 %collective-permute-start.49 = (bf16[2,96,768]{2,1,0:T(8,128)(2,1)S(1)}, bf16[2,96,768]{2,1,0:T(8,128)(2,1)S(1)}, u32[]{:S(2)}, u32[]{:S(2)}) collective-permute-start(bf16[2,96,768]{2,1,0:T(8,128)(2,1)S(1)} %get-tuple-element.353), channel_id=1, source_target_pairs={{0,4},{1,5},{2,6},{3,7},{4,0},{5,1},{6,2},{7,3},{8,12},{9,13},{10,... | collective-permute-start | bytes 884744 | tf_op jit(solution)/shard_map/ppermute | solution.py:70
  217.9 19.2 %collective-permute-start.61 = (bf16[96,768]{1,0:T(8,128)(2,1)S(1)}, bf16[96,768]{1,0:T(8,128)(2,1)S(1)}, u32[]{:S(2)}, u32[]{:S(2)}) collective-permute-start(bf16[96,768]{1,0:T(8,128)(2,1)S(1)} %get-tuple-element.386), channel_id=1, source_target_pairs={{0,8},{1,9},{2,10},{3,11},{4,12},{5,13},{6,14},{7,15},{8,16},{9,17... | collective-permute-start | bytes 442376 | tf_op jit(solution)/shard_map/ppermute | solution.py:70
  219.9 18.4 %collective-permute-start.62 = (bf16[96,768]{1,0:T(8,128)(2,1)S(1)}, bf16[96,768]{1,0:T(8,128)(2,1)S(1)}, u32[]{:S(2)}, u32[]{:S(2)}) collective-permute-start(bf16[96,768]{1,0:T(8,128)(2,1)S(1)} %get-tuple-element.389), channel_id=1, source_target_pairs={{0,16},{1,17},{2,18},{3,19},{4,20},{5,21},{6,22},{7,23},{8,24},{9,... | collective-permute-start | bytes 442376 | tf_op jit(solution)/shard_map/ppermute | solution.py:70
  221.2 18.6 %collective-permute-start.63 = (bf16[96,768]{1,0:T(8,128)(2,1)S(1)}, bf16[96,768]{1,0:T(8,128)(2,1)S(1)}, u32[]{:S(2)}, u32[]{:S(2)}) collective-permute-start(bf16[96,768]{1,0:T(8,128)(2,1)S(1)} %get-tuple-element.391), channel_id=1, source_target_pairs={{0,24},{1,25},{2,26},{3,27},{4,28},{5,29},{6,30},{7,31},{8,0},{9,1... | collective-permute-start | bytes 442376 | tf_op jit(solution)/shard_map/ppermute | solution.py:70
  234.5 16.5 %collective-permute-start.51 = (bf16[2,2,96,768]{3,2,1,0:T(8,128)(2,1)S(1)}, bf16[2,2,96,768]{3,2,1,0:T(8,128)(2,1)S(1)}, u32[]{:S(2)}, u32[]{:S(2)}) collective-permute-start(bf16[2,2,96,768]{3,2,1,0:T(8,128)(2,1)S(1)} %get-tuple-element.362), channel_id=1, source_target_pairs={{0,2},{1,3},{2,0},{3,1},{4,6},{5,7},{6,4},{7,5},{8,10},{9,11},{10,... | collective-permute-start | bytes 1769480 | tf_op jit(solution)/shard_map/ppermute | solution.py:70
  237.2 18.2 %collective-permute-start.58 = (bf16[96,768]{1,0:T(8,128)(2,1)S(1)}, bf16[96,768]{1,0:T(8,128)(2,1)S(1)}, u32[]{:S(2)}, u32[]{:S(2)}) collective-permute-start(bf16[96,768]{1,0:T(8,128)(2,1)S(1)} %get-tuple-element.378), channel_id=1, source_target_pairs={{0,8},{1,9},{2,10},{3,11},{4,12},{5,13},{6,14},{7,15},{8,16},{9,17... | collective-permute-start | bytes 442376 | tf_op jit(solution)/shard_map/ppermute | solution.py:70
  238.3 17.1 %collective-permute-start.59 = (bf16[96,768]{1,0:T(8,128)(2,1)S(1)}, bf16[96,768]{1,0:T(8,128)(2,1)S(1)}, u32[]{:S(2)}, u32[]{:S(2)}) collective-permute-start(bf16[96,768]{1,0:T(8,128)(2,1)S(1)} %get-tuple-element.380), channel_id=1, source_target_pairs={{0,16},{1,17},{2,18},{3,19},{4,20},{5,21},{6,22},{7,23},{8,24},{9,... | collective-permute-start | bytes 442376 | tf_op jit(solution)/shard_map/ppermute | solution.py:70
  (137 other events, 1170.1 us)

commit v4 on v3

--- a/solution.py
+++ b/solution.py
@@ -117,6 +117,14 @@
     if not on_grid():
         return g
     return ((where[2] + g % 2) % 2) * 2 + (where[3] + g // 2) % 2
+
+
+def scatter_z_both(left, right, *beside):
+    parts = [(left[0], right[0])]
+    for s in (1, 2, 3):
+        pair = send(jnp.stack([left[s], right[s]]), UP_Z[s], *beside)
+        parts.append((pair[0], pair[1]))
+    return zip(*parts)
 
 
 def scatter_plain(parts):
@@ -390,29 +398,32 @@
         m = block_of(chosen[0] + i, where)
         projected = (dot(x, w_ref[m]) + bias_ref[m]).astype(LOW)
         parts = [jnp.zeros((HD, L), LOW)]
+        scores, values = [], []
         for h in range(HEADS_BLOCK):
             q_scale, q_tail, k_scale, k_tail, v_scale = sides[h]
             tile = projected[:, h * TILE : (h + 1) * TILE]
             query = tile * q_scale + q_tail
             at = KEYS + h // 2 * TILE
             keys = projected[:, at : at + TILE] * k_scale + k_tail
-            value = tile.T[: HD] if SIDES[h] else tile.T[HD:]
-            scores = dot(keys, query, (1, 1))
-            highest = jnp.max(scores, axis=0, keepdims=True)
-            weights = jnp.exp(scores - highest)
-            totals = jnp.sum(weights, axis=0, keepdims=True)
-            mixed = dot(value, weights.astype(LOW)) * (1.0 / totals)
-            parts.append(mixed.astype(LOW))
+            values.append(tile.T[:HD] if SIDES[h] else tile.T[HD:])
+            scores.append(dot(keys, query, (1, 1)))
             q_out[i * HEADS_BLOCK + h] = query
             k_out[i * HEADS_BLOCK + h] = keys
             v_out[i * HEADS_BLOCK + h] = tile * v_scale
+        for h in range(HEADS_BLOCK):
+            highest = jnp.max(scores[h], axis=0, keepdims=True)
+            weights = jnp.exp(scores[h] - highest)
+            totals = jnp.sum(weights, axis=0, keepdims=True)
+            mixed = dot(values[h], weights.astype(LOW)) * (1.0 / totals)
+            parts.append(mixed.astype(LOW))
             log_out[i * HEADS_BLOCK + h] = highest + jnp.log(totals)
         context = jnp.concatenate(parts, axis=0).T
         context_out[i] = context
         sum_ref[...] += dot(context, w_ref[m, :, OUT:], (1, 1))
         return carry
 
-    lax.fori_loop(0, len(chosen), block, 0)
+    for i in range(len(chosen)):
+        block(i, 0)
     if last:
         unit, inverse = normalize(sum_ref[...])
         unit_out[...] = unit
@@ -450,15 +461,17 @@
     lows, (w_ref, bias_ref, active_out, slope_out) = refs[:rows], refs[rows:]
 
     def block(m, carry):
+        hiddens = [dot(lows[row][...], w_ref[m]) + bias_ref[m] for row in range(rows)]
         for row in range(rows):
-            hidden = dot(lows[row][...], w_ref[m]) + bias_ref[m]
+            hidden = hiddens[row]
             half = 0.5 * (1.0 + lax.erf(hidden * math.sqrt(0.5)))
             active_out[m, row * L : (row + 1) * L] = (hidden * half).astype(LOW)
             density = jnp.exp(-0.5 * hidden * hidden) * (1.0 / math.sqrt(2.0 * math.pi))
             slope_out[m, row * L : (row + 1) * L] = (half + hidden * density).astype(LOW)
         return carry
 
-    lax.fori_loop(0, w_ref.shape[0], block, 0)
+    for i in range(w_ref.shape[0]):
+        block(i, 0)
 
 
 def widen(where, lows, weight, bias, wait_for=()):
@@ -655,13 +668,10 @@
         ref[...] = jnp.zeros_like(ref)
     for row in range(rows):
         at = slice(row * L, (row + 1) * L)
-        grad_out[at] = sum_ref[at]
-
-        def block(m, carry):
-            grad_out[at] += dot(hidden_ref[m, at], up_ref[m], (1, 1))
-            return carry
-
-        lax.fori_loop(0, blocks, block, 0)
+        value = sum_ref[at]
+        for m in range(blocks):
+            value += dot(hidden_ref[m, at], up_ref[m], (1, 1))
+        grad_out[at] = value
         for part in range(L // PART):
             inner = slice(part * PART, (part + 1) * PART)
             outer = slice(row * L + part * PART, row * L + (part + 1) * PART)
@@ -705,19 +715,21 @@
     low_half = lanes < HD
 
     def block(i, carry):
-        key_grads = []
+        key_grads, scores, weight_grads, grads = [], [], [], []
         for h in range(HEADS_BLOCK):
             n = i * HEADS_BLOCK + h
-            queries, keys = q_ref[n], k_ref[n]
             at = (h + 1) // 2 * TILE
-            grad = grad_ref[row * blocks + chosen[0] + i, :, at : at + TILE]
-            weights = jnp.exp(dot(keys, queries, (1, 1)) - log_ref[n])
-            weight_grad = dot(v_ref[n], grad, (1, 1))
-            middle_sum = jnp.sum(weight_grad * weights, axis=0, keepdims=True)
-            score_grad = (weights * (weight_grad - middle_sum)).astype(LOW)
-            query_grad = (dot(keys.T, score_grad) * HD ** (-0.5)).T
-            value_grad = dot(weights.astype(LOW), grad)
-            key_grads.append(dot(score_grad, queries))
+            grads.append(grad_ref[row * blocks + chosen[0] + i, :, at : at + TILE])
+            scores.append(dot(k_ref[n], q_ref[n], (1, 1)))
+            weight_grads.append(dot(v_ref[n], grads[h], (1, 1)))
+        for h in range(HEADS_BLOCK):
+            n = i * HEADS_BLOCK + h
+            weights = jnp.exp(scores[h] - log_ref[n])
+            middle_sum = jnp.sum(weight_grads[h] * weights, axis=0, keepdims=True)
+            score_grad = (weights * (weight_grads[h] - middle_sum)).astype(LOW)
+            query_grad = (dot(k_ref[n].T, score_grad) * HD ** (-0.5)).T
+            value_grad = dot(weights.astype(LOW), grads[h])
+            key_grads.append(dot(score_grad, q_ref[n]))
             pair = (value_grad, query_grad) if SIDES[h] else (query_grad, value_grad)
             out[i, :, h * TILE : (h + 1) * TILE] = jnp.where(low_half, *pair).astype(LOW)
         pair = jnp.where(low_half, key_grads[0], key_grads[1])
@@ -726,7 +738,8 @@
         out[i, :, OUT + TILE :] = jnp.zeros((L, D - OUT - TILE), LOW)
         return carry
 
-    lax.fori_loop(0, len(chosen), block, 0)
+    for i in range(len(chosen)):
+        block(i, 0)
 
 
 def attend_back(where, row, blocks, chosen, queries, keys, values, logs, context_grad, wait_for=()):
@@ -987,7 +1000,7 @@
         kept = [[None, None] for _ in range(rows)]
         kept[0][0] = attend_part(0, halves[0], None, weight, *up_z)
         up_near = gather_near(up_z, kept[0][0][-1])
-        down_z = gather_z(after(down_shard, *up_z), kept[0][0][-1])
+        down_z = gather_z(after(down_shard, kept[0][0][-1]), kept[0][0][-1])
         kept[0][1] = attend_part(0, halves[1], kept[0][0][5], weight, *up_near)
         kept[1][0] = attend_part(1, halves[0], None, weight, kept[0][1][-1], *down_z)
         up_far = gather_far(up_near, kept[1][0][-1])
@@ -1066,7 +1079,6 @@
         *up_sum, up_added = scatter_far(where, up_sum, ended)
         other_part = send(other_part, CORE)
         back[1][0], ended = back_part(1, 0, up_added, other_part)
-        down_parts = scatter_z(down_sum, ended)
         bias_own, own_part, ended = grad_part(0)
         *attention_sum, added = scatter_core(where, [own_part], arrived=other_part)
         *up_sum, up_added = scatter_near(where, up_sum, ended, wait_for=(added,))
@@ -1092,9 +1104,9 @@
         input_grad, ended = grad_of_input(
             where, rows, grads, weight, first_grad, wait_for=(added, up_added)
         )
-        up_parts = scatter_z(up_sum, ended)
         *attention_sum, _ = scatter_far(where, attention_sum, ended)
-        *attention_sum, _ = scatter_near(where, attention_sum)
+        *attention_sum, ended = scatter_near(where, attention_sum)
+        down_parts, up_parts = [list(p) for p in scatter_z_both(down_sum, up_sum, ended)]
         attention_parts = scatter_z(attention_sum)
     else:
         down_parts = [scatter_plain(down_part)]

time: 298 us -> 294 us (0.987)
  Pallas kernels: 147 us -> 137 us
  waiting for transfers between devices: 52.8 us -> 61.1 us
  starting transfers between devices: 73 us -> 66.8 us
    pallas_call x38, Pallas kernels: 147 us -> 137 us  [call(): pl.pallas_call(body, in_specs=[pl.BlockSpec(memory_space=pltpu.SMEM)] + [...]
    ppermute x71 -> x68, waiting for transfers between devices: 52.8 us -> 61.1 us  [send(): return after(lax.ppermute(value, AXES, pairs), *beside)]
    ppermute x71 -> x68, starting transfers between devices: 73 us -> 66.8 us  [send(): return after(lax.ppermute(value, AXES, pairs), *beside)]
    unnamed x188 -> x192, local copies, waits for them, and re-layouts: 13.2 us -> 13.3 us
  transfers between devices with their start and end apart: 71 -> 68, of which waited for: 21 -> 23; matrix products, arithmetic and copies ran while one was open for 2% -> 2% of each run, Pallas kernels for 43% -> 41%
where the time goes in v4:
time: 294 us; the launch traced here: 289 us
  Pallas kernels  137 us (47%)
  starting transfers between devices  66.8 us (23%)
  waiting for transfers between devices  61.1 us (21%)
  local copies, waits for them, and re-layouts  17.6 us (6%)
  other arithmetic  2.95 us (1%)
    pallas_call x38, Pallas kernels, call(): pl.pallas_call(body, in_specs=[pl.BlockSpec(memory_space=pltpu.SMEM)] + [...  137 us
    ppermute x68, starting transfers between devices, send(): return after(lax.ppermute(value, AXES, pairs), *beside)  66.8 us
    ppermute x68, waiting for transfers between devices, send(): return after(lax.ppermute(value, AXES, pairs), *beside)  61.1 us
    unnamed x192, local copies, waits for them, and re-layouts  13.3 us
  transfers between devices with their start and end apart: 68, of which 23 were waited for; matrix products, arithmetic and copies ran while one was open for 2% of the time, Pallas kernels for 41%

profile of v4, /device:TPU:0, one launch (start us, length us, event | category | flops | bytes accessed | tf_op | source)
XLA Modules:
  0.0 288.5 jit_solution(17725843198108413723)
XLA Ops:
  15.4 6.8 %collective-permute-done.2 = bf16[96,768]{1,0:T(8,128)(2,1)S(1)} collective-permute-done((bf16[96,768]{1,0:T(8,128)(2,1)S(1)}, bf16[96,768]{1,0:T(8,128)(2,1)S(1)}, u32[]{:S(2)}, u32[]{:S(2)}) %collective-permute-start.2) | collective-permute-done | bytes 147488 | tf_op jit(solution)/shard_map/ppermute | solution.py:70
  24.6 7.6 %collective-permute-done.4 = bf16[2,96,768]{2,1,0:T(8,128)(2,1)S(1)} collective-permute-done((bf16[2,96,768]{2,1,0:T(8,128)(2,1)S(1)}, bf16[2,96,768]{2,1,0:T(8,128)(2,1)S(1)}, u32[]{:S(2)}, u32[]{:S(2)}) %collective-permute-start.4) | collective-permute-done | bytes 294944 | tf_op jit(solution)/shard_map/ppermute | solution.py:70
  37.4 4.5 %collective-permute-done.11.refs_6_ = bf16[96,768]{1,0:T(8,128)(2,1)S(1)} collective-permute-done((bf16[96,768]{1,0:T(8,128)(2,1)S(1)}, bf16[96,768]{1,0:T(8,128)(2,1)S(1)}, u32[]{:S(2)}, u32[]{:S(2)}) %collective-permute-start.11) | collective-permute-done | bytes 147488 | tf_op jit(solution)/shard_map/ppermute | solution.py:70
  48.1 4.1 %collective-permute-done.13.refs_8_ = bf16[96,768]{1,0:T(8,128)(2,1)S(1)} collective-permute-done((bf16[96,768]{1,0:T(8,128)(2,1)S(1)}, bf16[96,768]{1,0:T(8,128)(2,1)S(1)}, u32[]{:S(2)}, u32[]{:S(2)}) %collective-permute-start.13) | collective-permute-done | bytes 147488 | tf_op jit(solution)/shard_map/ppermute | solution.py:70
  57.5 4.9 %attend.4 = (bf16[6,512,128]{2,1,0:T(8,128)(2,1)S(1)}, bf16[6,512,128]{2,1,0:T(8,128)(2,1)S(1)}, bf16[6,512,128]{2,1,0:T(8,128)(2,1)S(1)}, f32[6,1,512]{2,1,0:T(...) custom-call(s32[5]{0:T(128)S(1)} %stack.104.where, ...), custom_call_target="tpu_custom_call" | custom-call | flops 30000001024 | bytes 1048576 | tf_op jit(solution)/shard_map/attend/pallas_call | solution.py:231
  68.7 5.4 %attend.5 = (bf16[6,512,128]{2,1,0:T(8,128)(2,1)S(1)}, bf16[6,512,128]{2,1,0:T(8,128)(2,1)S(1)}, bf16[6,512,128]{2,1,0:T(8,128)(2,1)S(1)}, f32[6,1,512]{2,1,0:T(...) custom-call(s32[5]{0:T(128)S(1)} %stack.104.where, ...), custom_call_target="tpu_custom_call" | custom-call | flops 30000001024 | bytes 1048576 | tf_op jit(solution)/shard_map/attend/pallas_call | solution.py:231
  77.8 4.9 %attend.6 = (bf16[6,512,128]{2,1,0:T(8,128)(2,1)S(1)}, bf16[6,512,128]{2,1,0:T(8,128)(2,1)S(1)}, bf16[6,512,128]{2,1,0:T(8,128)(2,1)S(1)}, f32[6,1,512]{2,1,0:T(...) custom-call(s32[5]{0:T(128)S(1)} %stack.104.where, ...), custom_call_target="tpu_custom_call" | custom-call | flops 30000001024 | bytes 1048576 | tf_op jit(solution)/shard_map/attend/pallas_call | solution.py:231
  83.5 4.5 %collective-permute-done.25 = bf16[2,96,768]{2,1,0:T(8,128)(2,1)S(1)} collective-permute-done((bf16[2,96,768]{2,1,0:T(8,128)(2,1)S(1)}, bf16[2,96,768]{2,1,0:T(8,128)(2,1)S(1)}, u32[]{:S(2)}, u32[]{:S(2)}) %collective-permute-start.25) | collective-permute-done | bytes 294944 | tf_op jit(solution)/shard_map/ppermute | solution.py:70
  89.3 5.8 %attend.7 = (bf16[6,512,128]{2,1,0:T(8,128)(2,1)S(1)}, bf16[6,512,128]{2,1,0:T(8,128)(2,1)S(1)}, bf16[6,512,128]{2,1,0:T(8,128)(2,1)S(1)}, f32[6,1,512]{2,1,0:T(...) custom-call(s32[5]{0:T(128)S(1)} %stack.104.where, ...), custom_call_target="tpu_custom_call" | custom-call | flops 30000001024 | bytes 1048576 | tf_op jit(solution)/shard_map/attend/pallas_call | solution.py:231
  99.0 8.8 %widen.1 = (bf16[4,1024,768]{2,1,0:T(8,128)(2,1)S(1)}, bf16[4,1024,768]{2,1,0:T(8,128)(2,1)S(1)}, f32[8,128]{1,0:T(8,128)}) custom-call(s32[5]{0:T(128)S(1)} %stack.104.where, bf16[512,768]{1,0:T(8,128)(2,1)S(1)} %get-tuple-element.233.refs_0_.refs_3_, bf16[512,768]{1,0:T(8,128)(2,1)S(1)} %get-tuple-element.243.refs_1_.refs_4_, ...), custom_call_target="tpu_custom_call" | custom-call | flops 30000001024 | bytes 1048576 | tf_op jit(solution)/shard_map/widen/pallas_call | solution.py:231
  126.1 4.4 %narrow.2 = (bf16[512,768]{1,0:T(8,128)(2,1)S(1)}, f32[512,768]{1,0:T(8,128)S(1)}, f32[512,1]{1,0:T(8,128)S(1)}, f32[8,128]{1,0:T(8,128)}) custom-call(s32[5]{0:T(128)S(1)} %stack.104.where, bf16[4,1024,768]{2,1,0:T(8,128)(2,1)S(1)} %bitcast.127, bf16[4,768,768]{2,1,0:T(8,128)(2,1)S(1)} %bitcast.123, f32[1,9216]{1,0:T(1,128)S(1)} %bitcast.96, ...), custom_call_target="tpu_custom_call" | custom-call | flops 30000001024 | bytes 1048576 | tf_op jit(solution)/shard_map/narrow/pallas_call | solution.py:231
  135.3 4.2 %narrow.3 = (bf16[512,768]{1,0:T(8,128)(2,1)S(1)}, f32[512,768]{1,0:T(8,128)S(1)}, f32[512,1]{1,0:T(8,128)S(1)}, f32[8,128]{1,0:T(8,128)}) custom-call(s32[5]{0:T(128)S(1)} %stack.104.where, bf16[4,1024,768]{2,1,0:T(8,128)(2,1)S(1)} %bitcast.127, bf16[4,768,768]{2,1,0:T(8,128)(2,1)S(1)} %bitcast.124, f32[1,9216]{1,0:T(1,128)S(1)} %bitcast.97, ...), custom_call_target="tpu_custom_call" | custom-call | flops 30000001024 | bytes 1048576 | tf_op jit(solution)/shard_map/narrow/pallas_call | solution.py:231
  145.9 5.7 %grad_of_down.1 = (bf16[2,2,2,2,96,768]{5,4,3,2,1,0:T(8,128)(2,1)S(1)}, bf16[2,2,2,2,96,768]{5,4,3,2,1,0:T(8,128)(2,1)S(1)}, f32[8,128]{1,0:T(8,128)S(1)}) custom-call(s32[5]{0:T(128)S(1)} %stack.104.where, bf16[1024,768]{1,0:T(8,128)(2,1)S(1)} %get-tuple-element.283.refs_0_, bf16[4,1024,768]{2,1,0:T(8,128)(2,1)S(1)} %bitcast.127), custom_call_target="tpu_custom_call" | custom-call | flops 30000001024 | bytes 1048576 | tf_op jit(solution)/shard_map/grad_of_down/pallas_call | solution.py:231
  151.7 11.9 %grad_of_up.1 = (bf16[4,1024,768]{2,1,0:T(8,128)(2,1)S(1)}, f32[4,1,768]{2,1,0:T(1,128)S(1)}, bf16[2,2,2,2,96,768]{5,4,3,2,1,0:T(8,128)(2,1)S(1)}, bf16[2,2,2,2,96,768]{5,4,3,2,1,0:T(8,128)(2,1)S(1)}, f32[8,128]{1,0:T(8,128)}) custom-call(s32[5]{0:T(128)S(1)} %stack.104.where, bf16[1024,768]{1,0:T(8,128)(2,1)S(1)} %get-tuple-element.283.refs_0_, ...), custom_call_target="tpu_custom_call" | custom-call | flops 30000001024 | bytes 1048576 | tf_op jit(solution)/shard_map/grad_of_up/pallas_call | solution.py:231
  172.2 10.4 %middle.1 = (f32[1024,768]{1,0:T(8,128)S(1)}, bf16[1024,768]{1,0:T(8,128)(2,1)S(1)}, f32[1,768]{1,0:T(1,128)S(1)}, f32[1,768]{1,0:T(1,128)S(1)}, f32[1,768]{1,0:...) custom-call(s32[5]{0:T(128)S(1)} %stack.104.where, ...), custom_call_target="tpu_custom_call" | custom-call | flops 30000001024 | bytes 1048576 | tf_op jit(solution)/shard_map/middle/pallas_call | solution.py:231
  185.9 5.1 %attend_back.4 = (bf16[2,512,768]{2,1,0:T(8,128)(2,1)S(1)}, f32[8,128]{1,0:T(8,128)S(1)}) custom-call(s32[5]{0:T(128)S(1)} %stack.104.where, bf16[6,512,128]{2,1,0:T(8,128)(2,1)S(1)} %copy-done.43, bf16[6,512,128]{2,1,0:T(8,128)(2,1)S(1)} %copy-done.45, bf16[6,512,128]{2,1,0:T(8,128)(2,1)S(1)} %copy-done.47, f32[6,1,512]{2,1,0:T(1,128)S(1)} %get-tuple-element.303.refs_3_, ...), custom_call_target="tpu_custom_call" | custom-call | flops 30000001024 | bytes 1048576 | tf_op jit(solution)/shard_map/attend_back/pallas_call | solution.py:231
  191.1 5.7 %attend_back.5 = (bf16[2,512,768]{2,1,0:T(8,128)(2,1)S(1)}, f32[8,128]{1,0:T(8,128)}) custom-call(s32[5]{0:T(128)S(1)} %stack.104.where, bf16[6,512,128]{2,1,0:T(8,128)(2,1)S(1)} %copy-done.49, bf16[6,512,128]{2,1,0:T(8,128)(2,1)S(1)} %copy-done.51, bf16[6,512,128]{2,1,0:T(8,128)(2,1)S(1)} %copy-done.53, f32[6,1,512]{2,1,0:T(1,128)S(1)} %get-tuple-element.316.refs_3_, ...), custom_call_target="tpu_custom_call" | custom-call | flops 30000001024 | bytes 1048576 | tf_op jit(solution)/shard_map/attend_back/pallas_call | solution.py:231
  196.8 4.4 %grad_of_attention.2 = (f32[2,1,768]{2,1,0:T(1,128)S(1)}, bf16[2,2,2,2,96,768]{5,4,3,2,1,0:T(8,128)(2,1)S(1)}, f32[8,128]{1,0:T(8,128)S(1)}) custom-call(s32[5]{0:T(128)S(1)} %stack.104.where, bf16[1024,768]{1,0:T(8,128)(2,1)S(1)} %constant_dynamic-slice_fusion.3.refs_0_, bf16[1024,768]{1,0:T(8,128)(2,1)S(1)} %get-tuple-element.299.refs_1_, ...), custom_call_target="tpu_custom_call" | custom-call | flops 30000001024 | bytes 1048576 | tf_op jit(solution)/shard_map/grad_of_attention/pallas_call | solution.py:231
  202.9 5.6 %attend_back.6 = (bf16[2,512,768]{2,1,0:T(8,128)(2,1)S(1)}, f32[8,128]{1,0:T(8,128)}) custom-call(s32[5]{0:T(128)S(1)} %stack.104.where, bf16[6,512,128]{2,1,0:T(8,128)(2,1)S(1)} %copy-done.61, bf16[6,512,128]{2,1,0:T(8,128)(2,1)S(1)} %copy-done.63, bf16[6,512,128]{2,1,0:T(8,128)(2,1)S(1)} %copy-done.65, f32[6,1,512]{2,1,0:T(1,128)S(1)} %copy-done.79, ...), custom_call_target="tpu_custom_call" | custom-call | flops 30000001024 | bytes 1048576 | tf_op jit(solution)/shard_map/attend_back/pallas_call | solution.py:231
  212.0 5.6 %attend_back.7 = (bf16[2,512,768]{2,1,0:T(8,128)(2,1)S(1)}, f32[8,128]{1,0:T(8,128)}) custom-call(s32[5]{0:T(128)S(1)} %stack.104.where, bf16[6,512,128]{2,1,0:T(8,128)(2,1)S(1)} %copy-done.55, bf16[6,512,128]{2,1,0:T(8,128)(2,1)S(1)} %copy-done.57, bf16[6,512,128]{2,1,0:T(8,128)(2,1)S(1)} %copy-done.59, f32[6,1,512]{2,1,0:T(1,128)S(1)} %get-tuple-element.333.refs_3_, ...), custom_call_target="tpu_custom_call" | custom-call | flops 30000001024 | bytes 1048576 | tf_op jit(solution)/shard_map/attend_back/pallas_call | solution.py:231
  217.7 4.8 %grad_of_attention.3 = (f32[2,1,768]{2,1,0:T(1,128)S(1)}, bf16[2,2,2,2,96,768]{5,4,3,2,1,0:T(8,128)(2,1)S(1)}, f32[8,128]{1,0:T(8,128)}) custom-call(s32[5]{0:T(128)S(1)} %stack.104.where, bf16[1024,768]{1,0:T(8,128)(2,1)S(1)} %constant_dynamic-slice_fusion.3.refs_0_, bf16[1024,768]{1,0:T(8,128)(2,1)S(1)} %get-tuple-element.299.refs_1_, ...), custom_call_target="tpu_custom_call" | custom-call | flops 30000001024 | bytes 1048576 | tf_op jit(solution)/shard_map/grad_of_attention/pallas_call | solution.py:231
  231.5 7.4 %grad_of_input.1 = (f32[1024,768]{1,0:T(8,128)}, f32[8,128]{1,0:T(8,128)}) custom-call(s32[5]{0:T(128)S(1)} %stack.104.where, bf16[4,768,768]{2,1,0:T(8,128)(2,1)S(1)} %bitcast.117, f32[1024,768]{1,0:T(8,128)S(1)} %get-tuple-element.293.refs_1_, bf16[2,512,768]{2,1,0:T(8,128)(2,1)S(1)} %get-tuple-element.329.refs_2_, bf16[2,512,768]{2,1,0:T(8,128)(2,1)S(1)} %copy-done.35, ...), custom_call_target="tpu_custom_call" | custom-call | flops 30000001024 | bytes 1048576 | tf_op jit(solution)/shard_map/grad_of_input/pallas_call | solution.py:231
  243.7 5.2 %collective-permute-done.53.refs_2_ = bf16[2,96,768]{2,1,0:T(8,128)(2,1)S(1)} collective-permute-done((bf16[2,96,768]{2,1,0:T(8,128)(2,1)S(1)}, bf16[2,96,768]{2,1,0:T(8,128)(2,1)S(1)}, u32[]{:S(2)}, u32[]{:S(2)}) %collective-permute-start.53) | collective-permute-done | bytes 294944 | tf_op jit(solution)/shard_map/ppermute | solution.py:70
  259.0 6.5 %collective-permute-done.56.refs_2_ = bf16[96,768]{1,0:T(8,128)(2,1)S(1)} collective-permute-done((bf16[96,768]{1,0:T(8,128)(2,1)S(1)}, bf16[96,768]{1,0:T(8,128)(2,1)S(1)}, u32[]{:S(2)}, u32[]{:S(2)}) %collective-permute-start.56) | collective-permute-done | bytes 147488 | tf_op jit(solution)/shard_map/ppermute | solution.py:70
  (399 shorter events, 141.8 us)
Async XLA Ops:
  24.0 19.9 %collective-permute-start.5 = (bf16[4,96,768]{2,1,0:T(8,128)(2,1)S(1)}, bf16[4,96,768]{2,1,0:T(8,128)(2,1)S(1)}, u32[]{:S(2)}, u32[]{:S(2)}) collective-permute-start(bf16[4,96,768]{2,1,0:T(8,128)(2,1)S(1)} %pad_maximum_fusion.1.refs_0_), channel_id=1, source_target_pairs={{0,2},{1,3},{2,0},{3,1},{4,6},{5,7},{6,4},{7,5},{8,10},{9,11},{10,... | collective-permute-start | bytes 1769480 | tf_op jit(solution)/shard_map/ppermute | solution.py:70
  32.2 13.6 %collective-permute-start.6 = (bf16[4,96,768]{2,1,0:T(8,128)(2,1)S(1)}, bf16[4,96,768]{2,1,0:T(8,128)(2,1)}, u32[]{:S(2)}, u32[]{:S(2)}) collective-permute-start(bf16[4,96,768]{2,1,0:T(8,128)(2,1)S(1)} %pad_maximum_fusion.2.refs_1_), channel_id=1, source_target_pairs={{0,4},{1,5},{2,6},{3,7},{4,0},{5,1},{6,2},{7,3},{8,12},{9,13},{10,... | collective-permute-start | bytes 1769480 | tf_op jit(solution)/shard_map/ppermute | solution.py:70
  37.4 16.5 %collective-permute-start.7 = (bf16[4,96,768]{2,1,0:T(8,128)(2,1)S(1)}, bf16[4,96,768]{2,1,0:T(8,128)(2,1)S(1)}, u32[]{:S(2)}, u32[]{:S(2)}) collective-permute-start(bf16[4,96,768]{2,1,0:T(8,128)(2,1)S(1)} %pad_maximum_fusion.1.refs_0_), channel_id=1, source_target_pairs={{0,1},{1,0},{2,3},{3,2},{4,5},{5,4},{6,7},{7,6},{8,9},{9,8},{10,11... | collective-permute-start | bytes 1769480 | tf_op jit(solution)/shard_map/ppermute | solution.py:70
  41.9 13.5 %collective-permute-start.8 = (bf16[4,96,768]{2,1,0:T(8,128)(2,1)S(1)}, bf16[4,96,768]{2,1,0:T(8,128)(2,1)S(1)}, u32[]{:S(2)}, u32[]{:S(2)}) collective-permute-start(bf16[4,96,768]{2,1,0:T(8,128)(2,1)S(1)} %pad_maximum_fusion.2.refs_1_), channel_id=1, source_target_pairs={{0,1},{1,0},{2,3},{3,2},{4,5},{5,4},{6,7},{7,6},{8,9},{9,8},{10,11... | collective-permute-start | bytes 1769480 | tf_op jit(solution)/shard_map/ppermute | solution.py:70
  52.3 15.1 %collective-permute-start.14 = (bf16[2,96,768]{2,1,0:T(8,128)(2,1)S(1)}, bf16[2,96,768]{2,1,0:T(8,128)(2,1)S(1)}, u32[]{:S(2)}, u32[]{:S(2)}) collective-permute-start(bf16[2,96,768]{2,1,0:T(8,128)(2,1)S(1)} %pad_maximum_fusion.9), channel_id=1, source_target_pairs={{0,4},{1,5},{2,6},{3,7},{4,0},{5,1},{6,2},{7,3},{8,12},{9,13},{10,... | collective-permute-start | bytes 884744 | tf_op jit(solution)/shard_map/ppermute | solution.py:70
  53.9 13.6 %collective-permute-start.15 = (bf16[2,96,768]{2,1,0:T(8,128)(2,1)S(1)}, bf16[2,96,768]{2,1,0:T(8,128)(2,1)S(1)}, u32[]{:S(2)}, u32[]{:S(2)}) collective-permute-start(bf16[2,96,768]{2,1,0:T(8,128)(2,1)S(1)} %pad_maximum_fusion.10), channel_id=1, source_target_pairs={{0,2},{1,3},{2,0},{3,1},{4,6},{5,7},{6,4},{7,5},{8,10},{9,11},{10,... | collective-permute-start | bytes 884744 | tf_op jit(solution)/shard_map/ppermute | solution.py:70
  67.6 21.2 %collective-permute-start.19 = (bf16[4,96,768]{2,1,0:T(8,128)(2,1)S(1)}, bf16[4,96,768]{2,1,0:T(8,128)(2,1)S(1)}, u32[]{:S(2)}, u32[]{:S(2)}) collective-permute-start(bf16[4,96,768]{2,1,0:T(8,128)(2,1)S(1)} %get-tuple-element.508.refs_6_.refs_0_), channel_id=1, source_target_pairs={{0,2},{1,3},{2,0},{3,1},{4,6},{5,7},{6,4},{7,5},{8,10},{9,11},{10,... | collective-permute-start | bytes 1769480 | tf_op jit(solution)/shard_map/ppermute | solution.py:70
  68.2 20.6 %collective-permute-start.20 = (bf16[4,96,768]{2,1,0:T(8,128)(2,1)S(1)}, bf16[4,96,768]{2,1,0:T(8,128)(2,1)S(1)}, u32[]{:S(2)}, u32[]{:S(2)}) collective-permute-start(bf16[4,96,768]{2,1,0:T(8,128)(2,1)S(1)} %get-tuple-element.509.refs_7_.refs_1_), channel_id=1, source_target_pairs={{0,4},{1,5},{2,6},{3,7},{4,0},{5,1},{6,2},{7,3},{8,12},{9,13},{10,... | collective-permute-start | bytes 1769480 | tf_op jit(solution)/shard_map/ppermute | solution.py:70
  74.2 21.1 %collective-permute-start.21 = (bf16[4,96,768]{2,1,0:T(8,128)(2,1)S(1)}, bf16[4,96,768]{2,1,0:T(8,128)(2,1)S(1)}, u32[]{:S(2)}, u32[]{:S(2)}) collective-permute-start(bf16[4,96,768]{2,1,0:T(8,128)(2,1)S(1)} %get-tuple-element.508.refs_6_.refs_0_), channel_id=1, source_target_pairs={{0,1},{1,0},{2,3},{3,2},{4,5},{5,4},{6,7},{7,6},{8,9},{9,8},{10,11... | collective-permute-start | bytes 1769480 | tf_op jit(solution)/shard_map/ppermute | solution.py:70
  88.1 27.7 %collective-permute-start.29 = (bf16[4,96,768]{2,1,0:T(8,128)(2,1)S(1)}, bf16[4,96,768]{2,1,0:T(8,128)(2,1)S(1)}, u32[]{:S(2)}, u32[]{:S(2)}) collective-permute-start(bf16[4,96,768]{2,1,0:T(8,128)(2,1)S(1)} %pad_maximum_fusion.5.refs_4_.refs_0_), channel_id=1, source_target_pairs={{0,1},{1,0},{2,3},{3,2},{4,5},{5,4},{6,7},{7,6},{8,9},{9,8},{10,11... | collective-permute-start | bytes 1769480 | tf_op jit(solution)/shard_map/ppermute | solution.py:70
  95.3 20.5 %collective-permute-start.30 = (bf16[4,96,768]{2,1,0:T(8,128)(2,1)S(1)}, bf16[4,96,768]{2,1,0:T(8,128)(2,1)S(1)}, u32[]{:S(2)}, u32[]{:S(2)}) collective-permute-start(bf16[4,96,768]{2,1,0:T(8,128)(2,1)S(1)} %pad_maximum_fusion.6.refs_5_.refs_1_), channel_id=1, source_target_pairs={{0,1},{1,0},{2,3},{3,2},{4,5},{5,4},{6,7},{7,6},{8,9},{9,8},{10,11... | collective-permute-start | bytes 1769480 | tf_op jit(solution)/shard_map/ppermute | solution.py:70
  95.4 17.7 %collective-permute-start.27 = (bf16[4,96,768]{2,1,0:T(8,128)(2,1)S(1)}, bf16[4,96,768]{2,1,0:T(8,128)(2,1)}, u32[]{:S(2)}, u32[]{:S(2)}) collective-permute-start(bf16[4,96,768]{2,1,0:T(8,128)(2,1)S(1)} %pad_maximum_fusion.5.refs_4_.refs_0_), channel_id=1, source_target_pairs={{0,2},{1,3},{2,0},{3,1},{4,6},{5,7},{6,4},{7,5},{8,10},{9,11},{10,... | collective-permute-start | bytes 1769480 | tf_op jit(solution)/shard_map/ppermute | solution.py:70
  96.9 16.2 %collective-permute-start.28 = (bf16[4,96,768]{2,1,0:T(8,128)(2,1)S(1)}, bf16[4,96,768]{2,1,0:T(8,128)(2,1)}, u32[]{:S(2)}, u32[]{:S(2)}) collective-permute-start(bf16[4,96,768]{2,1,0:T(8,128)(2,1)S(1)} %pad_maximum_fusion.6.refs_5_.refs_1_), channel_id=1, source_target_pairs={{0,4},{1,5},{2,6},{3,7},{4,0},{5,1},{6,2},{7,3},{8,12},{9,13},{10,... | collective-permute-start | bytes 1769480 | tf_op jit(solution)/shard_map/ppermute | solution.py:70
  165.1 17.5 %collective-permute-start.41 = (bf16[2,2,96,768]{3,2,1,0:T(8,128)(2,1)S(1)}, bf16[2,2,96,768]{3,2,1,0:T(8,128)(2,1)S(1)}, u32[]{:S(2)}, u32[]{:S(2)}) collective-permute-start(bf16[2,2,96,768]{3,2,1,0:T(8,128)(2,1)S(1)} %get-tuple-element.306), channel_id=1, source_target_pairs={{0,2},{1,3},{2,0},{3,1},{4,6},{5,7},{6,4},{7,5},{8,10},{9,11},{10,... | collective-permute-start | bytes 1769480 | tf_op jit(solution)/shard_map/ppermute | solution.py:70
  165.7 16.9 %collective-permute-start.42 = (bf16[2,2,96,768]{3,2,1,0:T(8,128)(2,1)S(1)}, bf16[2,2,96,768]{3,2,1,0:T(8,128)(2,1)S(1)}, u32[]{:S(2)}, u32[]{:S(2)}) collective-permute-start(bf16[2,2,96,768]{3,2,1,0:T(8,128)(2,1)S(1)} %get-tuple-element.307), channel_id=1, source_target_pairs={{0,4},{1,5},{2,6},{3,7},{4,0},{5,1},{6,2},{7,3},{8,12},{9,13},{10,... | collective-permute-start | bytes 1769480 | tf_op jit(solution)/shard_map/ppermute | solution.py:70
  170.0 38.5 %collective-permute-start.46 = (bf16[2,2,96,768]{3,2,1,0:T(8,128)(2,1)}, bf16[2,2,96,768]{3,2,1,0:T(8,128)(2,1)}, u32[]{:S(2)}, u32[]{:S(2)}) collective-permute-start(bf16[2,2,96,768]{3,2,1,0:T(8,128)(2,1)} %get-tuple-element.336), channel_id=1, source_target_pairs={{0,2},{1,3},{2,0},{3,1},{4,6},{5,7},{6,4},{7,5},{8,10},{9,11},{10,... | collective-permute-start | bytes 1769480 | tf_op jit(solution)/shard_map/ppermute | solution.py:70
  170.6 37.9 %collective-permute-start.47 = (bf16[2,2,96,768]{3,2,1,0:T(8,128)(2,1)}, bf16[2,2,96,768]{3,2,1,0:T(8,128)(2,1)}, u32[]{:S(2)}, u32[]{:S(2)}) collective-permute-start(bf16[2,2,96,768]{3,2,1,0:T(8,128)(2,1)} %get-tuple-element.339), channel_id=1, source_target_pairs={{0,4},{1,5},{2,6},{3,7},{4,0},{5,1},{6,2},{7,3},{8,12},{9,13},{10,... | collective-permute-start | bytes 1769480 | tf_op jit(solution)/shard_map/ppermute | solution.py:70
  183.4 17.8 %collective-permute-start.44 = (bf16[2,96,768]{2,1,0:T(8,128)(2,1)S(1)}, bf16[2,96,768]{2,1,0:T(8,128)(2,1)S(1)}, u32[]{:S(2)}, u32[]{:S(2)}) collective-permute-start(bf16[2,96,768]{2,1,0:T(8,128)(2,1)S(1)} %get-tuple-element.324), channel_id=1, source_target_pairs={{0,4},{1,5},{2,6},{3,7},{4,0},{5,1},{6,2},{7,3},{8,12},{9,13},{10,... | collective-permute-start | bytes 884744 | tf_op jit(solution)/shard_map/ppermute | solution.py:70
  184.3 16.9 %collective-permute-start.45 = (bf16[2,96,768]{2,1,0:T(8,128)(2,1)S(1)}, bf16[2,96,768]{2,1,0:T(8,128)(2,1)S(1)}, u32[]{:S(2)}, u32[]{:S(2)}) collective-permute-start(bf16[2,96,768]{2,1,0:T(8,128)(2,1)S(1)} %get-tuple-element.326), channel_id=1, source_target_pairs={{0,2},{1,3},{2,0},{3,1},{4,6},{5,7},{6,4},{7,5},{8,10},{9,11},{10,... | collective-permute-start | bytes 884744 | tf_op jit(solution)/shard_map/ppermute | solution.py:70
  223.6 15.3 %collective-permute-start.51 = (bf16[2,2,96,768]{3,2,1,0:T(8,128)(2,1)S(1)}, bf16[2,2,96,768]{3,2,1,0:T(8,128)(2,1)S(1)}, u32[]{:S(2)}, u32[]{:S(2)}) collective-permute-start(bf16[2,2,96,768]{3,2,1,0:T(8,128)(2,1)S(1)} %get-tuple-element.359), channel_id=1, source_target_pairs={{0,2},{1,3},{2,0},{3,1},{4,6},{5,7},{6,4},{7,5},{8,10},{9,11},{10,... | collective-permute-start | bytes 1769480 | tf_op jit(solution)/shard_map/ppermute | solution.py:70
  225.2 14.9 %collective-permute-start.52 = (bf16[2,2,96,768]{3,2,1,0:T(8,128)(2,1)S(1)}, bf16[2,2,96,768]{3,2,1,0:T(8,128)(2,1)S(1)}, u32[]{:S(2)}, u32[]{:S(2)}) collective-permute-start(bf16[2,2,96,768]{3,2,1,0:T(8,128)(2,1)S(1)} %get-tuple-element.362), channel_id=1, source_target_pairs={{0,4},{1,5},{2,6},{3,7},{4,0},{5,1},{6,2},{7,3},{8,12},{9,13},{10,... | collective-permute-start | bytes 1769480 | tf_op jit(solution)/shard_map/ppermute | solution.py:70
  226.8 27.1 %collective-permute-start.58 = (bf16[2,96,768]{2,1,0:T(8,128)(2,1)S(1)}, bf16[2,96,768]{2,1,0:T(8,128)(2,1)S(1)}, u32[]{:S(2)}, u32[]{:S(2)}) collective-permute-start(bf16[2,96,768]{2,1,0:T(8,128)(2,1)S(1)} %pad_maximum_fusion.13), channel_id=1, source_target_pairs={{0,8},{1,9},{2,10},{3,11},{4,12},{5,13},{6,14},{7,15},{8,16},{9,17... | collective-permute-start | bytes 884744 | tf_op jit(solution)/shard_map/ppermute | solution.py:70
  228.9 26.1 %collective-permute-start.59 = (bf16[2,96,768]{2,1,0:T(8,128)(2,1)S(1)}, bf16[2,96,768]{2,1,0:T(8,128)(2,1)S(1)}, u32[]{:S(2)}, u32[]{:S(2)}) collective-permute-start(bf16[2,96,768]{2,1,0:T(8,128)(2,1)S(1)} %pad_maximum_fusion.14), channel_id=1, source_target_pairs={{0,16},{1,17},{2,18},{3,19},{4,20},{5,21},{6,22},{7,23},{8,24},{9,... | collective-permute-start | bytes 884744 | tf_op jit(solution)/shard_map/ppermute | solution.py:70
  230.2 24.8 %collective-permute-start.60 = (bf16[2,96,768]{2,1,0:T(8,128)(2,1)S(1)}, bf16[2,96,768]{2,1,0:T(8,128)(2,1)S(1)}, u32[]{:S(2)}, u32[]{:S(2)}) collective-permute-start(bf16[2,96,768]{2,1,0:T(8,128)(2,1)S(1)} %pad_maximum_fusion.15), channel_id=1, source_target_pairs={{0,24},{1,25},{2,26},{3,27},{4,28},{5,29},{6,30},{7,31},{8,0},{9,1... | collective-permute-start | bytes 884744 | tf_op jit(solution)/shard_map/ppermute | solution.py:70
  (136 other events, 1089.3 us)

commit v5 on v4

--- a/solution.py
+++ b/solution.py
@@ -855,14 +855,14 @@
     return jnp.sum(jnp.sum(value * value, axis=0, keepdims=True), axis=1, keepdims=True)
 
 
-def adapt_kernel(cut, parts, where, *refs):
+def adapt_kernel(cut, parts, joined, where, *refs):
     total_sum = refs[0][...].astype(WIDE)
     for ref in refs[1:parts]:
         total_sum += ref[...].astype(WIDE)
     refs = refs[parts:]
     count = len(cut)
     firsts, seconds, weights = refs[:count], refs[count : 2 * count], refs[2 * count : 3 * count]
-    outs = refs[3 * count :]
+    extra, outs = refs[3 * count : 3 * count + joined], refs[3 * count + joined :]
     lines = []
     for i, pick in enumerate(cut):
         for part, grad in pick(total_sum):
@@ -881,14 +881,24 @@
     for i, (weight_square, update_square) in enumerate(lines):
         held = jnp.where(lanes == 2 * i, weight_square, held)
         held = jnp.where(lanes == 2 * i + 1, update_square, held)
-    outs[-1][...] = held
-
-
-def adapt(name, where, parts, cut, firsts, seconds, weights):
-    outs = [array(WIDE, *w.shape) for w in weights for _ in range(3)] + [array(WIDE, 1, 128)]
-    operands = [*parts, *firsts, *seconds, *weights]
-    return call(
-        partial(adapt_kernel, cut, len(parts)),
+    if joined:
+        vector_ref, *others = extra
+        for i, ref in enumerate(others):
+            for side in range(2):
+                value = ref[:, side : side + 1]
+                held = jnp.where(lanes == 2 * (len(lines) + i) + side, value, held)
+        outs[-1][:, :VEC] = vector_ref[...]
+        outs[-1][:, VEC:] = held
+    else:
+        outs[-1][...] = held
+
+
+def adapt(name, where, parts, cut, firsts, seconds, weights, joined=()):
+    outs = [array(WIDE, *w.shape) for w in weights for _ in range(3)]
+    outs += [array(WIDE, 1, VEC + 128 if joined else 128)]
+    operands = [*parts, *firsts, *seconds, *weights, *joined]
+    return call(
+        partial(adapt_kernel, cut, len(parts), len(joined)),
         name,
         where,
         operands,
@@ -1123,7 +1133,7 @@
     )
     (
         qkv_grad, qkv_second_new, qkv_update,
-        out_grad, out_second_new, out_update, attention_squares,
+        out_grad, out_second_new, out_update, joined,
     ) = adapt(
         "adapt_attention",
         where,
@@ -1139,19 +1149,9 @@
         [qkv_first, out_first],
         [qkv_second, out_second],
         [qkv_weight, out_weight],
-    )
-    summed = total(
-        jnp.concatenate(
-            [
-                vector_local,
-                attention_squares[:, :8],
-                up_squares[:, :2],
-                down_squares[:, :2],
-                jnp.zeros((1, 116), WIDE),
-            ],
-            axis=1,
-        )
-    )
+        [vector_local, up_squares, down_squares],
+    )
+    summed = total(joined)
     vector_grad, sums = summed[:, :VEC], summed[:, VEC:]
     weights = [qkv_weight, out_weight, up_weight, down_turned]
     updates = [qkv_update, out_update, up_update, down_update]

time: 294 us -> 294 us (level)
    unnamed x192 -> x182, local copies, waits for them, and re-layouts: 13.3 us -> 12.5 us
  transfers between devices with their start and end apart: 68 -> 68, of which waited for: 23 -> 23; matrix products, arithmetic and copies ran while one was open for 2% -> 3% of each run, Pallas kernels for 41% -> 41%
where the time goes in v5:
time: 294 us; the launch traced here: 289 us
  Pallas kernels  138 us (47%)
  starting transfers between devices  67 us (23%)
  waiting for transfers between devices  61.2 us (21%)
  local copies, waits for them, and re-layouts  16.7 us (6%)
  other arithmetic  3.88 us (1%)
    pallas_call x38, Pallas kernels, call(): pl.pallas_call(body, in_specs=[pl.BlockSpec(memory_space=pltpu.SMEM)] + [...  138 us
    ppermute x68, starting transfers between devices, send(): return after(lax.ppermute(value, AXES, pairs), *beside)  67 us
    ppermute x68, waiting for transfers between devices, send(): return after(lax.ppermute(value, AXES, pairs), *beside)  61.2 us
    unnamed x182, local copies, waits for them, and re-layouts  12.5 us
  transfers between devices with their start and end apart: 68, of which 23 were waited for; matrix products, arithmetic and copies ran while one was open for 3% of the time, Pallas kernels for 41%

profile of v5, /device:TPU:0, one launch (start us, length us, event | category | flops | bytes accessed | tf_op | source)
XLA Modules:
  0.0 289.0 jit_solution(17649673738264911930)
XLA Ops:
  15.4 6.8 %collective-permute-done.2 = bf16[96,768]{1,0:T(8,128)(2,1)S(1)} collective-permute-done((bf16[96,768]{1,0:T(8,128)(2,1)S(1)}, bf16[96,768]{1,0:T(8,128)(2,1)S(1)}, u32[]{:S(2)}, u32[]{:S(2)}) %collective-permute-start.2) | collective-permute-done | bytes 147488 | tf_op jit(solution)/shard_map/ppermute | solution.py:70
  24.6 7.7 %collective-permute-done.4 = bf16[2,96,768]{2,1,0:T(8,128)(2,1)} collective-permute-done((bf16[2,96,768]{2,1,0:T(8,128)(2,1)S(1)}, bf16[2,96,768]{2,1,0:T(8,128)(2,1)}, u32[]{:S(2)}, u32[]{:S(2)}) %collective-permute-start.4) | collective-permute-done | bytes 294944 | tf_op jit(solution)/shard_map/ppermute | solution.py:70
  38.4 4.5 %collective-permute-done.11.refs_6_ = bf16[96,768]{1,0:T(8,128)(2,1)S(1)} collective-permute-done((bf16[96,768]{1,0:T(8,128)(2,1)S(1)}, bf16[96,768]{1,0:T(8,128)(2,1)S(1)}, u32[]{:S(2)}, u32[]{:S(2)}) %collective-permute-start.11) | collective-permute-done | bytes 147488 | tf_op jit(solution)/shard_map/ppermute | solution.py:70
  49.2 4.1 %collective-permute-done.13.refs_8_ = bf16[96,768]{1,0:T(8,128)(2,1)S(1)} collective-permute-done((bf16[96,768]{1,0:T(8,128)(2,1)S(1)}, bf16[96,768]{1,0:T(8,128)(2,1)S(1)}, u32[]{:S(2)}, u32[]{:S(2)}) %collective-permute-start.13) | collective-permute-done | bytes 147488 | tf_op jit(solution)/shard_map/ppermute | solution.py:70
  58.5 4.9 %attend.4 = (bf16[6,512,128]{2,1,0:T(8,128)(2,1)S(1)}, bf16[6,512,128]{2,1,0:T(8,128)(2,1)S(1)}, bf16[6,512,128]{2,1,0:T(8,128)(2,1)S(1)}, f32[6,1,512]{2,1,0:T(...) custom-call(s32[5]{0:T(128)S(1)} %stack.104.where, ...), custom_call_target="tpu_custom_call" | custom-call | flops 30000001024 | bytes 1048576 | tf_op jit(solution)/shard_map/attend/pallas_call | solution.py:231
  69.6 5.4 %attend.5 = (bf16[6,512,128]{2,1,0:T(8,128)(2,1)S(1)}, bf16[6,512,128]{2,1,0:T(8,128)(2,1)S(1)}, bf16[6,512,128]{2,1,0:T(8,128)(2,1)S(1)}, f32[6,1,512]{2,1,0:T(...) custom-call(s32[5]{0:T(128)S(1)} %stack.104.where, ...), custom_call_target="tpu_custom_call" | custom-call | flops 30000001024 | bytes 1048576 | tf_op jit(solution)/shard_map/attend/pallas_call | solution.py:231
  78.7 4.9 %attend.6 = (bf16[6,512,128]{2,1,0:T(8,128)(2,1)S(1)}, bf16[6,512,128]{2,1,0:T(8,128)(2,1)S(1)}, bf16[6,512,128]{2,1,0:T(8,128)(2,1)S(1)}, f32[6,1,512]{2,1,0:T(...) custom-call(s32[5]{0:T(128)S(1)} %stack.104.where, ...), custom_call_target="tpu_custom_call" | custom-call | flops 30000001024 | bytes 1048576 | tf_op jit(solution)/shard_map/attend/pallas_call | solution.py:231
  84.5 4.5 %collective-permute-done.25 = bf16[2,96,768]{2,1,0:T(8,128)(2,1)S(1)} collective-permute-done((bf16[2,96,768]{2,1,0:T(8,128)(2,1)S(1)}, bf16[2,96,768]{2,1,0:T(8,128)(2,1)S(1)}, u32[]{:S(2)}, u32[]{:S(2)}) %collective-permute-start.25) | collective-permute-done | bytes 294944 | tf_op jit(solution)/shard_map/ppermute | solution.py:70
  90.3 5.9 %attend.7 = (bf16[6,512,128]{2,1,0:T(8,128)(2,1)S(1)}, bf16[6,512,128]{2,1,0:T(8,128)(2,1)S(1)}, bf16[6,512,128]{2,1,0:T(8,128)(2,1)S(1)}, f32[6,1,512]{2,1,0:T(...) custom-call(s32[5]{0:T(128)S(1)} %stack.104.where, ...), custom_call_target="tpu_custom_call" | custom-call | flops 30000001024 | bytes 1048576 | tf_op jit(solution)/shard_map/attend/pallas_call | solution.py:231
  100.0 8.8 %widen.1 = (bf16[4,1024,768]{2,1,0:T(8,128)(2,1)S(1)}, bf16[4,1024,768]{2,1,0:T(8,128)(2,1)S(1)}, f32[8,128]{1,0:T(8,128)}) custom-call(s32[5]{0:T(128)S(1)} %stack.104.where, bf16[512,768]{1,0:T(8,128)(2,1)S(1)} %get-tuple-element.233.refs_0_.refs_3_, bf16[512,768]{1,0:T(8,128)(2,1)S(1)} %get-tuple-element.243.refs_1_.refs_4_, ...), custom_call_target="tpu_custom_call" | custom-call | flops 30000001024 | bytes 1048576 | tf_op jit(solution)/shard_map/widen/pallas_call | solution.py:231
  127.4 4.4 %narrow.2 = (bf16[512,768]{1,0:T(8,128)(2,1)S(1)}, f32[512,768]{1,0:T(8,128)S(1)}, f32[512,1]{1,0:T(8,128)S(1)}, f32[8,128]{1,0:T(8,128)}) custom-call(s32[5]{0:T(128)S(1)} %stack.104.where, bf16[4,1024,768]{2,1,0:T(8,128)(2,1)S(1)} %bitcast.121, bf16[4,768,768]{2,1,0:T(8,128)(2,1)S(1)} %bitcast.117, f32[1,9216]{1,0:T(1,128)S(1)} %bitcast.93, ...), custom_call_target="tpu_custom_call" | custom-call | flops 30000001024 | bytes 1048576 | tf_op jit(solution)/shard_map/narrow/pallas_call | solution.py:231
  136.6 4.2 %narrow.3 = (bf16[512,768]{1,0:T(8,128)(2,1)S(1)}, f32[512,768]{1,0:T(8,128)S(1)}, f32[512,1]{1,0:T(8,128)S(1)}, f32[8,128]{1,0:T(8,128)}) custom-call(s32[5]{0:T(128)S(1)} %stack.104.where, bf16[4,1024,768]{2,1,0:T(8,128)(2,1)S(1)} %bitcast.121, bf16[4,768,768]{2,1,0:T(8,128)(2,1)S(1)} %bitcast.118, f32[1,9216]{1,0:T(1,128)S(1)} %bitcast.94, ...), custom_call_target="tpu_custom_call" | custom-call | flops 30000001024 | bytes 1048576 | tf_op jit(solution)/shard_map/narrow/pallas_call | solution.py:231
  147.2 5.6 %grad_of_down.1 = (bf16[2,2,2,2,96,768]{5,4,3,2,1,0:T(8,128)(2,1)S(1)}, bf16[2,2,2,2,96,768]{5,4,3,2,1,0:T(8,128)(2,1)S(1)}, f32[8,128]{1,0:T(8,128)S(1)}) custom-call(s32[5]{0:T(128)S(1)} %stack.104.where, bf16[1024,768]{1,0:T(8,128)(2,1)S(1)} %get-tuple-element.283.refs_0_, bf16[4,1024,768]{2,1,0:T(8,128)(2,1)S(1)} %bitcast.121), custom_call_target="tpu_custom_call" | custom-call | flops 30000001024 | bytes 1048576 | tf_op jit(solution)/shard_map/grad_of_down/pallas_call | solution.py:231
  153.0 11.7 %grad_of_up.1 = (bf16[4,1024,768]{2,1,0:T(8,128)(2,1)S(1)}, f32[4,1,768]{2,1,0:T(1,128)S(1)}, bf16[2,2,2,2,96,768]{5,4,3,2,1,0:T(8,128)(2,1)S(1)}, bf16[2,2,2,2,96,768]{5,4,3,2,1,0:T(8,128)(2,1)S(1)}, f32[8,128]{1,0:T(8,128)}) custom-call(s32[5]{0:T(128)S(1)} %stack.104.where, bf16[1024,768]{1,0:T(8,128)(2,1)S(1)} %get-tuple-element.283.refs_0_, ...), custom_call_target="tpu_custom_call" | custom-call | flops 30000001024 | bytes 1048576 | tf_op jit(solution)/shard_map/grad_of_up/pallas_call | solution.py:231
  173.4 10.3 %middle.1 = (f32[1024,768]{1,0:T(8,128)S(1)}, bf16[1024,768]{1,0:T(8,128)(2,1)S(1)}, f32[1,768]{1,0:T(1,128)S(1)}, f32[1,768]{1,0:T(1,128)S(1)}, f32[1,768]{1,0:...) custom-call(s32[5]{0:T(128)S(1)} %stack.104.where, ...), custom_call_target="tpu_custom_call" | custom-call | flops 30000001024 | bytes 1048576 | tf_op jit(solution)/shard_map/middle/pallas_call | solution.py:231
  187.1 5.2 %attend_back.4 = (bf16[2,512,768]{2,1,0:T(8,128)(2,1)S(1)}, f32[8,128]{1,0:T(8,128)S(1)}) custom-call(s32[5]{0:T(128)S(1)} %stack.104.where, bf16[6,512,128]{2,1,0:T(8,128)(2,1)S(1)} %copy-done.42, bf16[6,512,128]{2,1,0:T(8,128)(2,1)S(1)} %copy-done.44, bf16[6,512,128]{2,1,0:T(8,128)(2,1)S(1)} %copy-done.46, f32[6,1,512]{2,1,0:T(1,128)S(1)} %get-tuple-element.303.refs_3_, ...), custom_call_target="tpu_custom_call" | custom-call | flops 30000001024 | bytes 1048576 | tf_op jit(solution)/shard_map/attend_back/pallas_call | solution.py:231
  192.3 5.7 %attend_back.5 = (bf16[2,512,768]{2,1,0:T(8,128)(2,1)S(1)}, f32[8,128]{1,0:T(8,128)}) custom-call(s32[5]{0:T(128)S(1)} %stack.104.where, bf16[6,512,128]{2,1,0:T(8,128)(2,1)S(1)} %copy-done.48, bf16[6,512,128]{2,1,0:T(8,128)(2,1)S(1)} %copy-done.50, bf16[6,512,128]{2,1,0:T(8,128)(2,1)S(1)} %copy-done.52, f32[6,1,512]{2,1,0:T(1,128)S(1)} %get-tuple-element.316.refs_3_, ...), custom_call_target="tpu_custom_call" | custom-call | flops 30000001024 | bytes 1048576 | tf_op jit(solution)/shard_map/attend_back/pallas_call | solution.py:231
  198.0 4.4 %grad_of_attention.2 = (f32[2,1,768]{2,1,0:T(1,128)S(1)}, bf16[2,2,2,2,96,768]{5,4,3,2,1,0:T(8,128)(2,1)S(1)}, f32[8,128]{1,0:T(8,128)S(1)}) custom-call(s32[5]{0:T(128)S(1)} %stack.104.where, bf16[1024,768]{1,0:T(8,128)(2,1)S(1)} %constant_dynamic-slice_fusion.3.refs_0_, bf16[1024,768]{1,0:T(8,128)(2,1)S(1)} %get-tuple-element.299.refs_1_, ...), custom_call_target="tpu_custom_call" | custom-call | flops 30000001024 | bytes 1048576 | tf_op jit(solution)/shard_map/grad_of_attention/pallas_call | solution.py:231
  204.1 5.7 %attend_back.6 = (bf16[2,512,768]{2,1,0:T(8,128)(2,1)S(1)}, f32[8,128]{1,0:T(8,128)}) custom-call(s32[5]{0:T(128)S(1)} %stack.104.where, bf16[6,512,128]{2,1,0:T(8,128)(2,1)S(1)} %copy-done.60, bf16[6,512,128]{2,1,0:T(8,128)(2,1)S(1)} %copy-done.62, bf16[6,512,128]{2,1,0:T(8,128)(2,1)S(1)} %copy-done.64, f32[6,1,512]{2,1,0:T(1,128)S(1)} %get-tuple-element.297.refs_3_, ...), custom_call_target="tpu_custom_call" | custom-call | flops 30000001024 | bytes 1048576 | tf_op jit(solution)/shard_map/attend_back/pallas_call | solution.py:231
  213.2 5.7 %attend_back.7 = (bf16[2,512,768]{2,1,0:T(8,128)(2,1)S(1)}, f32[8,128]{1,0:T(8,128)}) custom-call(s32[5]{0:T(128)S(1)} %stack.104.where, bf16[6,512,128]{2,1,0:T(8,128)(2,1)S(1)} %copy-done.54, bf16[6,512,128]{2,1,0:T(8,128)(2,1)S(1)} %copy-done.56, bf16[6,512,128]{2,1,0:T(8,128)(2,1)S(1)} %copy-done.58, f32[6,1,512]{2,1,0:T(1,128)S(1)} %get-tuple-element.333.refs_3_, ...), custom_call_target="tpu_custom_call" | custom-call | flops 30000001024 | bytes 1048576 | tf_op jit(solution)/shard_map/attend_back/pallas_call | solution.py:231
  218.9 4.6 %grad_of_attention.3 = (f32[2,1,768]{2,1,0:T(1,128)S(1)}, bf16[2,2,2,2,96,768]{5,4,3,2,1,0:T(8,128)(2,1)S(1)}, f32[8,128]{1,0:T(8,128)}) custom-call(s32[5]{0:T(128)S(1)} %stack.104.where, bf16[1024,768]{1,0:T(8,128)(2,1)S(1)} %constant_dynamic-slice_fusion.3.refs_0_, bf16[1024,768]{1,0:T(8,128)(2,1)S(1)} %get-tuple-element.299.refs_1_, ...), custom_call_target="tpu_custom_call" | custom-call | flops 30000001024 | bytes 1048576 | tf_op jit(solution)/shard_map/grad_of_attention/pallas_call | solution.py:231
  232.5 7.4 %grad_of_input.1 = (f32[1024,768]{1,0:T(8,128)}, f32[8,128]{1,0:T(8,128)}) custom-call(s32[5]{0:T(128)S(1)} %stack.104.where, bf16[4,768,768]{2,1,0:T(8,128)(2,1)S(1)} %bitcast.111, f32[1024,768]{1,0:T(8,128)S(1)} %get-tuple-element.293.refs_1_, bf16[2,512,768]{2,1,0:T(8,128)(2,1)S(1)} %get-tuple-element.329.refs_2_, bf16[2,512,768]{2,1,0:T(8,128)(2,1)S(1)} %copy-done.34, ...), custom_call_target="tpu_custom_call" | custom-call | flops 30000001024 | bytes 1048576 | tf_op jit(solution)/shard_map/grad_of_input/pallas_call | solution.py:231
  245.0 4.9 %collective-permute-done.53.refs_2_ = bf16[2,96,768]{2,1,0:T(8,128)(2,1)S(1)} collective-permute-done((bf16[2,96,768]{2,1,0:T(8,128)(2,1)S(1)}, bf16[2,96,768]{2,1,0:T(8,128)(2,1)S(1)}, u32[]{:S(2)}, u32[]{:S(2)}) %collective-permute-start.53) | collective-permute-done | bytes 294944 | tf_op jit(solution)/shard_map/ppermute | solution.py:70
  260.0 6.5 %collective-permute-done.56.refs_2_ = bf16[96,768]{1,0:T(8,128)(2,1)S(1)} collective-permute-done((bf16[96,768]{1,0:T(8,128)(2,1)S(1)}, bf16[96,768]{1,0:T(8,128)(2,1)S(1)}, u32[]{:S(2)}, u32[]{:S(2)}) %collective-permute-start.56) | collective-permute-done | bytes 147488 | tf_op jit(solution)/shard_map/ppermute | solution.py:70
  (387 shorter events, 142.7 us)
Async XLA Ops:
  24.0 19.9 %collective-permute-start.5 = (bf16[4,96,768]{2,1,0:T(8,128)(2,1)S(1)}, bf16[4,96,768]{2,1,0:T(8,128)(2,1)S(1)}, u32[]{:S(2)}, u32[]{:S(2)}) collective-permute-start(bf16[4,96,768]{2,1,0:T(8,128)(2,1)S(1)} %pad_maximum_fusion.1.refs_0_), channel_id=1, source_target_pairs={{0,2},{1,3},{2,0},{3,1},{4,6},{5,7},{6,4},{7,5},{8,10},{9,11},{10,... | collective-permute-start | bytes 1769480 | tf_op jit(solution)/shard_map/ppermute | solution.py:70
  33.3 13.6 %collective-permute-start.6 = (bf16[4,96,768]{2,1,0:T(8,128)(2,1)S(1)}, bf16[4,96,768]{2,1,0:T(8,128)(2,1)}, u32[]{:S(2)}, u32[]{:S(2)}) collective-permute-start(bf16[4,96,768]{2,1,0:T(8,128)(2,1)S(1)} %pad_maximum_fusion.2.refs_1_), channel_id=1, source_target_pairs={{0,4},{1,5},{2,6},{3,7},{4,0},{5,1},{6,2},{7,3},{8,12},{9,13},{10,... | collective-permute-start | bytes 1769480 | tf_op jit(solution)/shard_map/ppermute | solution.py:70
  38.4 16.5 %collective-permute-start.7 = (bf16[4,96,768]{2,1,0:T(8,128)(2,1)S(1)}, bf16[4,96,768]{2,1,0:T(8,128)(2,1)S(1)}, u32[]{:S(2)}, u32[]{:S(2)}) collective-permute-start(bf16[4,96,768]{2,1,0:T(8,128)(2,1)S(1)} %pad_maximum_fusion.1.refs_0_), channel_id=1, source_target_pairs={{0,1},{1,0},{2,3},{3,2},{4,5},{5,4},{6,7},{7,6},{8,9},{9,8},{10,11... | collective-permute-start | bytes 1769480 | tf_op jit(solution)/shard_map/ppermute | solution.py:70
  43.0 13.5 %collective-permute-start.8 = (bf16[4,96,768]{2,1,0:T(8,128)(2,1)S(1)}, bf16[4,96,768]{2,1,0:T(8,128)(2,1)S(1)}, u32[]{:S(2)}, u32[]{:S(2)}) collective-permute-start(bf16[4,96,768]{2,1,0:T(8,128)(2,1)S(1)} %pad_maximum_fusion.2.refs_1_), channel_id=1, source_target_pairs={{0,1},{1,0},{2,3},{3,2},{4,5},{5,4},{6,7},{7,6},{8,9},{9,8},{10,11... | collective-permute-start | bytes 1769480 | tf_op jit(solution)/shard_map/ppermute | solution.py:70
  53.3 15.0 %collective-permute-start.14 = (bf16[2,96,768]{2,1,0:T(8,128)(2,1)S(1)}, bf16[2,96,768]{2,1,0:T(8,128)(2,1)S(1)}, u32[]{:S(2)}, u32[]{:S(2)}) collective-permute-start(bf16[2,96,768]{2,1,0:T(8,128)(2,1)S(1)} %pad_maximum_fusion.9), channel_id=1, source_target_pairs={{0,4},{1,5},{2,6},{3,7},{4,0},{5,1},{6,2},{7,3},{8,12},{9,13},{10,... | collective-permute-start | bytes 884744 | tf_op jit(solution)/shard_map/ppermute | solution.py:70
  54.9 13.5 %collective-permute-start.15 = (bf16[2,96,768]{2,1,0:T(8,128)(2,1)S(1)}, bf16[2,96,768]{2,1,0:T(8,128)(2,1)S(1)}, u32[]{:S(2)}, u32[]{:S(2)}) collective-permute-start(bf16[2,96,768]{2,1,0:T(8,128)(2,1)S(1)} %pad_maximum_fusion.10), channel_id=1, source_target_pairs={{0,2},{1,3},{2,0},{3,1},{4,6},{5,7},{6,4},{7,5},{8,10},{9,11},{10,... | collective-permute-start | bytes 884744 | tf_op jit(solution)/shard_map/ppermute | solution.py:70
  68.5 21.2 %collective-permute-start.19 = (bf16[4,96,768]{2,1,0:T(8,128)(2,1)S(1)}, bf16[4,96,768]{2,1,0:T(8,128)(2,1)S(1)}, u32[]{:S(2)}, u32[]{:S(2)}) collective-permute-start(bf16[4,96,768]{2,1,0:T(8,128)(2,1)S(1)} %get-tuple-element.508.refs_6_.refs_0_), channel_id=1, source_target_pairs={{0,2},{1,3},{2,0},{3,1},{4,6},{5,7},{6,4},{7,5},{8,10},{9,11},{10,... | collective-permute-start | bytes 1769480 | tf_op jit(solution)/shard_map/ppermute | solution.py:70
  69.1 20.6 %collective-permute-start.20 = (bf16[4,96,768]{2,1,0:T(8,128)(2,1)S(1)}, bf16[4,96,768]{2,1,0:T(8,128)(2,1)S(1)}, u32[]{:S(2)}, u32[]{:S(2)}) collective-permute-start(bf16[4,96,768]{2,1,0:T(8,128)(2,1)S(1)} %get-tuple-element.509.refs_7_.refs_1_), channel_id=1, source_target_pairs={{0,4},{1,5},{2,6},{3,7},{4,0},{5,1},{6,2},{7,3},{8,12},{9,13},{10,... | collective-permute-start | bytes 1769480 | tf_op jit(solution)/shard_map/ppermute | solution.py:70
  75.1 21.1 %collective-permute-start.21 = (bf16[4,96,768]{2,1,0:T(8,128)(2,1)S(1)}, bf16[4,96,768]{2,1,0:T(8,128)(2,1)S(1)}, u32[]{:S(2)}, u32[]{:S(2)}) collective-permute-start(bf16[4,96,768]{2,1,0:T(8,128)(2,1)S(1)} %get-tuple-element.508.refs_6_.refs_0_), channel_id=1, source_target_pairs={{0,1},{1,0},{2,3},{3,2},{4,5},{5,4},{6,7},{7,6},{8,9},{9,8},{10,11... | collective-permute-start | bytes 1769480 | tf_op jit(solution)/shard_map/ppermute | solution.py:70
  89.0 27.8 %collective-permute-start.29 = (bf16[4,96,768]{2,1,0:T(8,128)(2,1)S(1)}, bf16[4,96,768]{2,1,0:T(8,128)(2,1)S(1)}, u32[]{:S(2)}, u32[]{:S(2)}) collective-permute-start(bf16[4,96,768]{2,1,0:T(8,128)(2,1)S(1)} %pad_maximum_fusion.5.refs_4_.refs_0_), channel_id=1, source_target_pairs={{0,1},{1,0},{2,3},{3,2},{4,5},{5,4},{6,7},{7,6},{8,9},{9,8},{10,11... | collective-permute-start | bytes 1769480 | tf_op jit(solution)/shard_map/ppermute | solution.py:70
  96.3 20.6 %collective-permute-start.30 = (bf16[4,96,768]{2,1,0:T(8,128)(2,1)S(1)}, bf16[4,96,768]{2,1,0:T(8,128)(2,1)}, u32[]{:S(2)}, u32[]{:S(2)}) collective-permute-start(bf16[4,96,768]{2,1,0:T(8,128)(2,1)S(1)} %pad_maximum_fusion.6.refs_5_.refs_1_), channel_id=1, source_target_pairs={{0,1},{1,0},{2,3},{3,2},{4,5},{5,4},{6,7},{7,6},{8,9},{9,8},{10,11... | collective-permute-start | bytes 1769480 | tf_op jit(solution)/shard_map/ppermute | solution.py:70
  96.4 17.8 %collective-permute-start.27 = (bf16[4,96,768]{2,1,0:T(8,128)(2,1)S(1)}, bf16[4,96,768]{2,1,0:T(8,128)(2,1)}, u32[]{:S(2)}, u32[]{:S(2)}) collective-permute-start(bf16[4,96,768]{2,1,0:T(8,128)(2,1)S(1)} %pad_maximum_fusion.5.refs_4_.refs_0_), channel_id=1, source_target_pairs={{0,2},{1,3},{2,0},{3,1},{4,6},{5,7},{6,4},{7,5},{8,10},{9,11},{10,... | collective-permute-start | bytes 1769480 | tf_op jit(solution)/shard_map/ppermute | solution.py:70
  97.9 16.3 %collective-permute-start.28 = (bf16[4,96,768]{2,1,0:T(8,128)(2,1)S(1)}, bf16[4,96,768]{2,1,0:T(8,128)(2,1)}, u32[]{:S(2)}, u32[]{:S(2)}) collective-permute-start(bf16[4,96,768]{2,1,0:T(8,128)(2,1)S(1)} %pad_maximum_fusion.6.refs_5_.refs_1_), channel_id=1, source_target_pairs={{0,4},{1,5},{2,6},{3,7},{4,0},{5,1},{6,2},{7,3},{8,12},{9,13},{10,... | collective-permute-start | bytes 1769480 | tf_op jit(solution)/shard_map/ppermute | solution.py:70
  166.3 17.4 %collective-permute-start.41 = (bf16[2,2,96,768]{3,2,1,0:T(8,128)(2,1)S(1)}, bf16[2,2,96,768]{3,2,1,0:T(8,128)(2,1)S(1)}, u32[]{:S(2)}, u32[]{:S(2)}) collective-permute-start(bf16[2,2,96,768]{3,2,1,0:T(8,128)(2,1)S(1)} %get-tuple-element.306), channel_id=1, source_target_pairs={{0,2},{1,3},{2,0},{3,1},{4,6},{5,7},{6,4},{7,5},{8,10},{9,11},{10,... | collective-permute-start | bytes 1769480 | tf_op jit(solution)/shard_map/ppermute | solution.py:70
  166.9 16.9 %collective-permute-start.42 = (bf16[2,2,96,768]{3,2,1,0:T(8,128)(2,1)S(1)}, bf16[2,2,96,768]{3,2,1,0:T(8,128)(2,1)S(1)}, u32[]{:S(2)}, u32[]{:S(2)}) collective-permute-start(bf16[2,2,96,768]{3,2,1,0:T(8,128)(2,1)S(1)} %get-tuple-element.307), channel_id=1, source_target_pairs={{0,4},{1,5},{2,6},{3,7},{4,0},{5,1},{6,2},{7,3},{8,12},{9,13},{10,... | collective-permute-start | bytes 1769480 | tf_op jit(solution)/shard_map/ppermute | solution.py:70
  171.2 38.5 %collective-permute-start.46 = (bf16[2,2,96,768]{3,2,1,0:T(8,128)(2,1)}, bf16[2,2,96,768]{3,2,1,0:T(8,128)(2,1)}, u32[]{:S(2)}, u32[]{:S(2)}) collective-permute-start(bf16[2,2,96,768]{3,2,1,0:T(8,128)(2,1)} %get-tuple-element.336), channel_id=1, source_target_pairs={{0,2},{1,3},{2,0},{3,1},{4,6},{5,7},{6,4},{7,5},{8,10},{9,11},{10,... | collective-permute-start | bytes 1769480 | tf_op jit(solution)/shard_map/ppermute | solution.py:70
  171.8 37.9 %collective-permute-start.47 = (bf16[2,2,96,768]{3,2,1,0:T(8,128)(2,1)}, bf16[2,2,96,768]{3,2,1,0:T(8,128)(2,1)}, u32[]{:S(2)}, u32[]{:S(2)}) collective-permute-start(bf16[2,2,96,768]{3,2,1,0:T(8,128)(2,1)} %get-tuple-element.339), channel_id=1, source_target_pairs={{0,4},{1,5},{2,6},{3,7},{4,0},{5,1},{6,2},{7,3},{8,12},{9,13},{10,... | collective-permute-start | bytes 1769480 | tf_op jit(solution)/shard_map/ppermute | solution.py:70
  184.6 17.8 %collective-permute-start.44 = (bf16[2,96,768]{2,1,0:T(8,128)(2,1)S(1)}, bf16[2,96,768]{2,1,0:T(8,128)(2,1)S(1)}, u32[]{:S(2)}, u32[]{:S(2)}) collective-permute-start(bf16[2,96,768]{2,1,0:T(8,128)(2,1)S(1)} %get-tuple-element.324), channel_id=1, source_target_pairs={{0,4},{1,5},{2,6},{3,7},{4,0},{5,1},{6,2},{7,3},{8,12},{9,13},{10,... | collective-permute-start | bytes 884744 | tf_op jit(solution)/shard_map/ppermute | solution.py:70
  185.8 16.7 %collective-permute-start.45 = (bf16[2,96,768]{2,1,0:T(8,128)(2,1)S(1)}, bf16[2,96,768]{2,1,0:T(8,128)(2,1)S(1)}, u32[]{:S(2)}, u32[]{:S(2)}) collective-permute-start(bf16[2,96,768]{2,1,0:T(8,128)(2,1)S(1)} %get-tuple-element.326), channel_id=1, source_target_pairs={{0,2},{1,3},{2,0},{3,1},{4,6},{5,7},{6,4},{7,5},{8,10},{9,11},{10,... | collective-permute-start | bytes 884744 | tf_op jit(solution)/shard_map/ppermute | solution.py:70
  224.6 15.3 %collective-permute-start.51 = (bf16[2,2,96,768]{3,2,1,0:T(8,128)(2,1)S(1)}, bf16[2,2,96,768]{3,2,1,0:T(8,128)(2,1)S(1)}, u32[]{:S(2)}, u32[]{:S(2)}) collective-permute-start(bf16[2,2,96,768]{3,2,1,0:T(8,128)(2,1)S(1)} %get-tuple-element.359), channel_id=1, source_target_pairs={{0,2},{1,3},{2,0},{3,1},{4,6},{5,7},{6,4},{7,5},{8,10},{9,11},{10,... | collective-permute-start | bytes 1769480 | tf_op jit(solution)/shard_map/ppermute | solution.py:70
  226.2 14.9 %collective-permute-start.52 = (bf16[2,2,96,768]{3,2,1,0:T(8,128)(2,1)S(1)}, bf16[2,2,96,768]{3,2,1,0:T(8,128)(2,1)S(1)}, u32[]{:S(2)}, u32[]{:S(2)}) collective-permute-start(bf16[2,2,96,768]{3,2,1,0:T(8,128)(2,1)S(1)} %get-tuple-element.362), channel_id=1, source_target_pairs={{0,4},{1,5},{2,6},{3,7},{4,0},{5,1},{6,2},{7,3},{8,12},{9,13},{10,... | collective-permute-start | bytes 1769480 | tf_op jit(solution)/shard_map/ppermute | solution.py:70
  227.8 27.1 %collective-permute-start.58 = (bf16[2,96,768]{2,1,0:T(8,128)(2,1)S(1)}, bf16[2,96,768]{2,1,0:T(8,128)(2,1)S(1)}, u32[]{:S(2)}, u32[]{:S(2)}) collective-permute-start(bf16[2,96,768]{2,1,0:T(8,128)(2,1)S(1)} %pad_maximum_fusion.13), channel_id=1, source_target_pairs={{0,8},{1,9},{2,10},{3,11},{4,12},{5,13},{6,14},{7,15},{8,16},{9,17... | collective-permute-start | bytes 884744 | tf_op jit(solution)/shard_map/ppermute | solution.py:70
  230.0 26.1 %collective-permute-start.59 = (bf16[2,96,768]{2,1,0:T(8,128)(2,1)S(1)}, bf16[2,96,768]{2,1,0:T(8,128)(2,1)S(1)}, u32[]{:S(2)}, u32[]{:S(2)}) collective-permute-start(bf16[2,96,768]{2,1,0:T(8,128)(2,1)S(1)} %pad_maximum_fusion.14), channel_id=1, source_target_pairs={{0,16},{1,17},{2,18},{3,19},{4,20},{5,21},{6,22},{7,23},{8,24},{9,... | collective-permute-start | bytes 884744 | tf_op jit(solution)/shard_map/ppermute | solution.py:70
  231.3 24.8 %collective-permute-start.60 = (bf16[2,96,768]{2,1,0:T(8,128)(2,1)S(1)}, bf16[2,96,768]{2,1,0:T(8,128)(2,1)S(1)}, u32[]{:S(2)}, u32[]{:S(2)}) collective-permute-start(bf16[2,96,768]{2,1,0:T(8,128)(2,1)S(1)} %pad_maximum_fusion.15), channel_id=1, source_target_pairs={{0,24},{1,25},{2,26},{3,27},{4,28},{5,29},{6,30},{7,31},{8,0},{9,1... | collective-permute-start | bytes 884744 | tf_op jit(solution)/shard_map/ppermute | solution.py:70
  (131 other events, 1068.7 us)
